TPU v7x, 256 devices: a whole 4x4x8 slice. The times are simulated.
256 devices in a mesh: dp: 8 (over x, core), expert: 32 (over y, z).
Axes of the slice: x: 4, y: 4, z: 8, core: 2. Of those that a mesh axis runs over, the one named last changes fastest.
Arguments:
- out_grad: bfloat16 [49152, 4096], P(('dp', 'expert')), may hold values from -24 to 24
- route_gates: float32 [49152, 8], P(('dp', 'expert')), may hold values from 0.02 to 0.4
- expert_ids: int32 [49152, 8], P(('dp', 'expert')), may hold values from 0 to 127, all different within a row; in each aligned block of 192 rows (0 to 191, 192 to 383, ...) at most 18 rows name the same one
- partner_offset: int32 [32], P('expert'), may hold values from 1 to 7
- saved_pre: bfloat16 [8, 32, 576, 1536], P('dp', 'expert'), may hold values from -6 to 6
- down_weight: bfloat16 [32, 768, 4096], P('expert', None, 'dp'), may hold values from -0.21875 to 0.21875
- gate_up_weight: bfloat16 [32, 4096, 1536], P('expert', 'dp'), may hold values from -0.09375 to 0.09375
Outputs:
- token_grad: bfloat16 [49152, 4096], P(('dp', 'expert'))
- hidden_grad: bfloat16 [8, 32, 576, 1536], P('dp', 'expert')
Inputs may be any that keep to these rules, and one draw needn't show every extreme that they name: `expert_ids`: each row names 8 different experts; among the rows of one device no expert is named by more than 18 rows.
All inputs are finite; a program needn't handle non-finite values.
Results may differ from a plain program's by a relative error of at most 0.0064.
Values may be sent and summed in bfloat16 or wider, within the bound.
No kernel may reach another device: no remote copies, remote signals or barrier semaphores. Data moves between devices by JAX's collectives and lax.ppermute only.
A program may use at most 128 MiB of HBM per device.

v0:
```python
import jax
import jax.numpy as jnp
from jax import lax
from jax.sharding import PartitionSpec as P

ALL_EXP = 128
CAP = 15
OC = 3


def passed_along(shard, axis, by):
    count = lax.axis_size(axis)
    return lax.ppermute(shard, axis, [(i, (i + by) % count) for i in range(count)])


def route_ranks(route_ids):
    onehot = (route_ids[:, None] == jnp.arange(ALL_EXP, dtype=jnp.int32)[None, :]).astype(jnp.int32)
    before = jnp.cumsum(onehot, axis=0) - onehot
    return jnp.sum(before * onehot, axis=1)


def body(out_grad, route_gates, expert_ids, partner_offset, saved_pre, down_weight, gate_up_weight):
    experts = lax.axis_size("expert")
    replicas = lax.axis_size("dp")
    slot_width = CAP + OC
    tok_rows = out_grad.shape[0]
    model_width = out_grad.shape[1]
    choose_count = expert_ids.shape[1]
    hidden = down_weight.shape[1]
    route_ids = expert_ids.reshape(-1)
    route_total = route_ids.shape[0]
    slot_rank = route_ranks(route_ids)
    in_window = route_ids < experts
    owner_row = jnp.where(in_window, route_ids * slot_width + slot_rank, experts * slot_width)
    slot_table = jnp.full((experts * slot_width,), -1, jnp.int32)
    slot_table = slot_table.at[owner_row].set(jnp.arange(route_total, dtype=jnp.int32), mode="drop")
    filled = slot_table >= 0
    safe_route = jnp.where(filled, slot_table, 0)
    token_of = safe_route // choose_count
    gate_of = jnp.where(filled, route_gates.reshape(-1)[safe_route], 0.0)
    outgoing = (gate_of[:, None] * out_grad[token_of].astype(jnp.float32)).astype(jnp.bfloat16)
    outgoing = outgoing.reshape(experts, slot_width, model_width)
    arrived = lax.all_to_all(outgoing, "expert", split_axis=0, concat_axis=0, tiled=True)
    home_rows = arrived[:, :CAP]
    spill_rows = arrived[:, CAP:]
    offset_value = partner_offset[0]
    digits = replicas.bit_length() - 1
    forwarded = spill_rows
    for bit_index in range(digits):
        shifted = passed_along(forwarded, "dp", 1 << bit_index)
        forwarded = jnp.where(offset_value >> bit_index & 1 == 1, shifted, forwarded)
    slot_rows = jnp.concatenate(
        [home_rows.reshape(-1, model_width), forwarded.reshape(-1, model_width)], 0
    )
    hidden_cot = jnp.einsum(
        "rn,hn->rh",
        slot_rows,
        lax.all_gather(down_weight, "dp", axis=2, tiled=True)[0],
        preferred_element_type=jnp.float32,
    )
    pre_acts = saved_pre[0, 0].astype(jnp.float32)
    gate_pre = pre_acts[:, :hidden]
    up_pre = pre_acts[:, hidden:]
    sigma_gate = jax.nn.sigmoid(gate_pre)
    hidden_grad = jnp.concatenate(
        [
            hidden_cot * up_pre * sigma_gate * (1.0 + gate_pre * (1.0 - sigma_gate)),
            hidden_cot * gate_pre * sigma_gate,
        ],
        axis=1,
    ).astype(jnp.bfloat16)
    back_rows = jnp.einsum(
        "rc,nc->rn",
        hidden_grad,
        lax.all_gather(gate_up_weight, "dp", axis=1, tiled=True)[0],
        preferred_element_type=jnp.float32,
    ).astype(jnp.bfloat16)
    home_back = back_rows[: experts * CAP].reshape(experts, CAP, model_width)
    spill_back = back_rows[experts * CAP :].reshape(experts, OC, model_width)
    for bit_index in range(digits):
        shifted_back = passed_along(spill_back, "dp", -(1 << bit_index))
        spill_back = jnp.where(offset_value >> bit_index & 1 == 1, shifted_back, spill_back)
    returned = lax.all_to_all(
        jnp.concatenate([home_back, spill_back], 1),
        "expert",
        split_axis=0,
        concat_axis=0,
        tiled=True,
    )
    flat_back = returned.reshape(-1, model_width)
    live_rows = jnp.where(filled[:, None], flat_back.astype(jnp.float32), 0.0)
    token_grad = jnp.zeros((tok_rows, model_width), jnp.float32).at[token_of].add(live_rows)
    return (token_grad.astype(jnp.bfloat16), hidden_grad.reshape(saved_pre.shape))


def solution(mesh):
    placed = (
        P(("dp", "expert"), None),
        P(("dp", "expert"), None),
        P(("dp", "expert"), None),
        P("expert"),
        P("dp", "expert", None, None),
        P("expert", None, "dp"),
        P("expert", "dp", None),
    )
    return jax.shard_map(
        body,
        mesh=mesh,
        in_specs=placed,
        out_specs=(P(("dp", "expert"), None), P("dp", "expert", None, None)),
        check_vma=False,
    )
```

profile of v0, /device:TPU:35, one launch (start us, length us, event | category | flops | bytes accessed | tf_op | source)
XLA Modules:
  0.0 544.6 jit_solution(1429470805349879329)
XLA Ops:
  7.2 0.7 all-gather.3.cloned.1.call-update
  8.0 0.7 all-gather.5.cloned.1.call-update
  8.7 0.8 copy.18
  11.6 6.2 %scatter_custom_fusion = s32[576]{0:T(1024)S(1)} fusion(s32[1536]{0:T(1024)S(1)} %fusion.26, s32[1536]{0:T(1024)S(1)} %iota.11, s32[]{:T(128)} %constant.40.clone.1), kind=kCustom, calls=%fused_computation.63 | custom fusion | bytes 2308 | tf_op jit(solution)/shard_map/scatter | solution.py:36
  17.9 5.1 gather_fusion.1
  23.0 8.7 %reshape.151 = f32[32,18,4096]{2,1,0:T(8,128)} reshape(bf16[576,4096]{1,0:T(8,128)(2,1)} %gather_fusion.1) | data formatting | bytes 14155776 | tf_op jit(solution)/shard_map/convert_element_type | solution.py:41
  32.0 3.6 gather_fusion
  35.7 9.5 %multiply_convert_fusion = bf16[32,18,4096]{2,1,0:T(8,128)(2,1)} fusion(f32[32,18,4096]{2,1,0:T(8,128)} %reshape.151, f32[32,18]{1,0:T(8,128)S(1)} %mul.52), kind=kLoop, calls=%fused_computation.6 | loop fusion | flops 4718592 | bytes 14158080 | tf_op jit(solution)/shard_map/convert_element_type | solution.py:41
  45.2 150.6 %all_to_all.10 = bf16[32,18,4096]{2,1,0:T(8,128)(2,1)S(1)} all-to-all(bf16[32,18,4096]{2,1,0:T(8,128)(2,1)} %multiply_convert_fusion), channel_id=1, replica_groups=mesh['dp'=8,'expert'=32] {'expert'}, dimensions={0} | all-to-all | bytes 9437184 | tf_op jit(solution)/shard_map/all_to_all | solution.py:43
  195.7 0.8 slice.39
  196.5 0.6 copy.23
  197.1 3.5 collective-permute-start
  201.3 8.3 %collective-permute-done = bf16[32,3,4096]{2,0,1:T(8,128)(2,1)S(1)} collective-permute-done((bf16[32,3,4096]{2,0,1:T(8,128)(2,1)S(1)}, bf16[32,3,4096]{2,0,1:T(8,128)(2,1)S(1)}, u32[]{:S(2)}, u32[]{:S(2)}) %collective-permute-start) | collective-permute-done | bytes 786464 | tf_op jit(solution)/shard_map/ppermute | solution.py:13
  209.6 1.4 copy_select_fusion.5
  211.0 0.6 copy.25
  211.6 1.3 collective-permute-start.1
  212.8 16.7 %collective-permute-done.1 = bf16[32,3,4096]{2,0,1:T(8,128)(2,1)S(1)} collective-permute-done((bf16[32,3,4096]{2,0,1:T(8,128)(2,1)S(1)}, bf16[32,3,4096]{2,0,1:T(8,128)(2,1)S(1)}, u32[]{:S(2)}, u32[]{:S(2)}) %collective-permute-start.1) | collective-permute-done | bytes 786464 | tf_op jit(solution)/shard_map/ppermute | solution.py:13
  229.5 0.9 copy_select_fusion.4
  230.4 0.6 copy.27
  231.0 2.3 bitcast_convert_fusion
  233.3 2.2 slice.38
  235.5 5.1 reshape.147
  240.7 8.5 %collective-permute-done.2 = bf16[32,3,4096]{2,0,1:T(8,128)(2,1)S(1)} collective-permute-done((bf16[32,3,4096]{2,0,1:T(8,128)(2,1)S(1)}, bf16[32,3,4096]{2,0,1:T(8,128)(2,1)S(1)}, u32[]{:S(2)}, u32[]{:S(2)}) %collective-permute-start.2) | collective-permute-done | bytes 786464 | tf_op jit(solution)/shard_map/ppermute | solution.py:13
  249.2 0.9 copy_select_fusion.3
  250.1 1.4 reshape.148
  251.5 9.5 %fusion.16 = (bf16[576,768]{1,0:T(8,128)(2,1)S(1)}, bf16[576,768]{1,0:T(8,128)(2,1)S(1)}) fusion(f32[576,1536]{1,0:T(8,128)} %bitcast_convert_fusion, bf16[1,768,4096]{2,1,0:T(8,128)(2,1)} %all-gather.3.cloned.1.call-done, bf16[96,4096]{1,0:T(8,128)(2,1)} %reshape.148, bf16[480,4096]{1,0:T(8,128)(2,1)} %reshape.147), kind=kOutput, calls=%fused_computation.21 | convolution fusion | flops 3639066624 | bytes 16318464 | tf_op jit(solution)/shard_map/rn,hn->rh/dot_general | solution.py:55
  261.0 10.8 %fusion.6 = bf16[576,4096]{1,0:T(8,128)(2,1)S(1)} fusion(bf16[1,4096,1536]{2,1,0:T(8,128)(2,1)} %all-gather.5.cloned.1.call-done, bf16[576,768]{1,0:T(8,128)(2,1)S(1)} %get-tuple-element.5, bf16[576,768]{1,0:T(8,128)(2,1)S(1)} %get-tuple-element.4), kind=kOutput, calls=%fused_computation.12 | convolution fusion | flops 7253655552 | bytes 19070976 | tf_op jit(solution)/shard_map/rc,nc->rn/dot_general | solution.py:72
  271.9 2.1 copy-done.2
  274.5 0.6 copy.29
  275.1 3.3 collective-permute-start.3
  278.4 10.3 %collective-permute-done.3 = bf16[32,3,4096]{2,0,1:T(8,128)(2,1)S(1)} collective-permute-done((bf16[32,3,4096]{2,0,1:T(8,128)(2,1)S(1)}, bf16[32,3,4096]{2,0,1:T(8,128)(2,1)S(1)}, u32[]{:S(2)}, u32[]{:S(2)}) %collective-permute-start.3) | collective-permute-done | bytes 786464 | tf_op jit(solution)/shard_map/ppermute | solution.py:13
  288.7 0.9 copy_select_fusion.2
  289.6 0.6 copy.31
  290.2 13.7 %collective-permute-start.4 = (bf16[32,3,4096]{2,0,1:T(8,128)(2,1)S(1)}, bf16[32,3,4096]{2,0,1:T(8,128)(2,1)S(1)}, u32[]{:S(2)}, u32[]{:S(2)}) collective-permute-start(bf16[32,3,4096]{2,0,1:T(8,128)(2,1)S(1)} %copy.31), channel_id=1, source_target_pairs={{0,192},{32,224},{64,0},{96,32},{128,64},{160,96},{192,128},{224,1... | collective-permute-start | bytes 2359304 | tf_op jit(solution)/shard_map/ppermute | solution.py:13
  303.8 18.2 %collective-permute-done.4 = bf16[32,3,4096]{2,0,1:T(8,128)(2,1)S(1)} collective-permute-done((bf16[32,3,4096]{2,0,1:T(8,128)(2,1)S(1)}, bf16[32,3,4096]{2,0,1:T(8,128)(2,1)S(1)}, u32[]{:S(2)}, u32[]{:S(2)}) %collective-permute-start.4) | collective-permute-done | bytes 786464 | tf_op jit(solution)/shard_map/ppermute | solution.py:13
  322.0 0.9 copy_select_fusion.1
  323.5 1.3 collective-permute-start.5
  324.8 2.1 slice.42
  326.9 5.1 reshape.149
  332.0 11.9 %collective-permute-done.5 = bf16[32,3,4096]{2,0,1:T(8,128)(2,1)} collective-permute-done((bf16[32,3,4096]{2,0,1:T(8,128)(2,1)S(1)}, bf16[32,3,4096]{2,0,1:T(8,128)(2,1)}, u32[]{:S(2)}, u32[]{:S(2)}) %collective-permute-start.5) | collective-permute-done | bytes 786464 | tf_op jit(solution)/shard_map/ppermute | solution.py:13
  343.9 2.0 copy_select_fusion
  345.9 6.5 %pad_maximum_fusion = bf16[32,18,4096]{2,1,0:T(8,128)(2,1)} fusion(bf16[32,3,4096]{2,1,0:T(4,128)(2,1)S(1)} %copy_select_fusion, bf16[32,15,4096]{2,1,0:T(8,128)(2,1)} %reshape.149), kind=kLoop, calls=%fused_computation.9 | loop fusion | flops 9437184 | bytes 9437184 | tf_op jit(solution)/shard_map/concatenate | solution.py:84
  352.4 5.2 all-to-all-start.1
  357.7 1.3 pad_maximum_fusion.1
  359.0 138.8 %all-to-all-done.1 = bf16[32,18,4096]{2,1,0:T(8,128)(2,1)} async-done(((bf16[32,18,4096]{2,1,0:T(8,128)(2,1)}), bf16[32,18,4096]{2,1,0:T(8,128)(2,1)}, u32[]{:S(2)}, u32[]{:S(2)}) %all-to-all-start.1) | async-done | bytes 4718624 | tf_op jit(solution)/shard_map/all_to_all | solution.py:83
  497.8 8.6 %reshape.153 = f32[576,4096]{1,0:T(8,128)} reshape(bf16[32,18,4096]{2,1,0:T(8,128)(2,1)} %all-to-all-done.1) | data formatting | bytes 14155776 | tf_op jit(solution)/shard_map/convert_element_type | solution.py:91
  506.5 27.9 %scatter_custom_fusion.1 = f32[192,4096]{1,0:T(8,128)} fusion(s32[576]{0:T(1024)S(1)} %compare_select_fusion.1, f32[576,4096]{1,0:T(8,128)} %reshape.153, f32[]{:T(128)} %constant.39.clone.1, pred[576]{0:T(1024)(128)(4,1)S(1)} %get-tuple-element.3), kind=kCustom, calls=%fused_computation.7 | custom fusion | flops 4718592 | bytes 12584960 | tf_op jit(solution)/shard_map/scatter-add | solution.py:92
  534.3 3.2 convert_element_type.54
  (50 shorter events, 3.7 us)
Async XLA Ops:
  7.2 10.7 %copy-start = (bf16[192,4096]{1,0:T(8,128)(2,1)S(1)}, bf16[192,4096]{1,0:T(8,128)(2,1)}, u32[]{:S(2)}) copy-start(bf16[192,4096]{1,0:T(8,128)(2,1)} %param.7) | copy-start | bytes 4718596
  7.2 3.4 copy-start.7
  7.2 244.3 %all-gather.3.cloned.1.call-start = ((), (), s32[]{:S(2)}) async-start(), calls=%async_computation.2 | async-start | bytes 7077888 | tf_op jit(solution)/shard_map/all_gather | solution.py:58
  7.9 253.1 %all-gather.5.cloned.1.call-start = ((), (), s32[]{:S(2)}) async-start(), calls=%async_computation.3 | async-start | bytes 14155776 | tf_op jit(solution)/shard_map/all_gather | solution.py:75
  23.0 8.7 %copy-start.8 = (f32[192,8]{0,1:T(8,128)S(1)}, f32[192,8]{0,1:T(8,128)}, u32[]{:S(2)}) copy-start(f32[192,8]{0,1:T(8,128)} %param.8) | copy-start | bytes 18436
  197.1 12.4 %collective-permute-start = (bf16[32,3,4096]{2,0,1:T(8,128)(2,1)S(1)}, bf16[32,3,4096]{2,0,1:T(8,128)(2,1)S(1)}, u32[]{:S(2)}, u32[]{:S(2)}) collective-permute-start(bf16[32,3,4096]{2,0,1:T(8,128)(2,1)S(1)} %copy.23), channel_id=1, source_target_pairs={{0,32},{32,64},{64,96},{96,128},{128,160},{160,192},{192,224},{224... | collective-permute-start | bytes 2359304 | tf_op jit(solution)/shard_map/ppermute | solution.py:13
  209.5 21.5 %copy-start.4 = (bf16[1,1,576,1536]{3,2,1,0:T(8,128)(2,1)S(1)}, bf16[1,1,576,1536]{3,2,1,0:T(8,128)(2,1)}, u32[]{:S(2)}) copy-start(bf16[1,1,576,1536]{3,2,1,0:T(8,128)(2,1)} %param.11) | copy-start | bytes 5308420
  211.6 17.9 %collective-permute-start.1 = (bf16[32,3,4096]{2,0,1:T(8,128)(2,1)S(1)}, bf16[32,3,4096]{2,0,1:T(8,128)(2,1)S(1)}, u32[]{:S(2)}, u32[]{:S(2)}) collective-permute-start(bf16[32,3,4096]{2,0,1:T(8,128)(2,1)S(1)} %copy.25), channel_id=1, source_target_pairs={{0,64},{32,96},{64,128},{96,160},{128,192},{160,224},{192,0},{224,... | collective-permute-start | bytes 2359304 | tf_op jit(solution)/shard_map/ppermute | solution.py:13
  230.9 18.3 %collective-permute-start.2 = (bf16[32,3,4096]{2,0,1:T(8,128)(2,1)S(1)}, bf16[32,3,4096]{2,0,1:T(8,128)(2,1)S(1)}, u32[]{:S(2)}, u32[]{:S(2)}) collective-permute-start(bf16[32,3,4096]{2,0,1:T(8,128)(2,1)S(1)} %copy.27), channel_id=1, source_target_pairs={{0,128},{32,160},{64,192},{96,224},{128,0},{160,32},{192,64},{224,... | collective-permute-start | bytes 2359304 | tf_op jit(solution)/shard_map/ppermute | solution.py:13
  261.0 10.9 %copy-start.5 = (bf16[576,768]{1,0:T(8,128)(2,1)}, bf16[576,768]{1,0:T(8,128)(2,1)S(1)}, u32[]{:S(2)}) copy-start(bf16[576,768]{1,0:T(8,128)(2,1)S(1)} %get-tuple-element.5) | copy-start | bytes 2654212
  271.8 2.1 copy-start.2
  275.1 49.6 %copy-start.3 = (bf16[576,4096]{1,0:T(8,128)(2,1)S(1)}, bf16[576,4096]{1,0:T(8,128)(2,1)}, u32[]{:S(2)}) copy-start(bf16[576,4096]{1,0:T(8,128)(2,1)} %copy-done.2) | copy-start | bytes 14155780
  275.1 13.6 %collective-permute-start.3 = (bf16[32,3,4096]{2,0,1:T(8,128)(2,1)S(1)}, bf16[32,3,4096]{2,0,1:T(8,128)(2,1)S(1)}, u32[]{:S(2)}, u32[]{:S(2)}) collective-permute-start(bf16[32,3,4096]{2,0,1:T(8,128)(2,1)S(1)} %copy.29), channel_id=1, source_target_pairs={{0,224},{32,0},{64,32},{96,64},{128,96},{160,128},{192,160},{224,1... | collective-permute-start | bytes 2359304 | tf_op jit(solution)/shard_map/ppermute | solution.py:13
  290.2 31.9 %collective-permute-start.4 = (bf16[32,3,4096]{2,0,1:T(8,128)(2,1)S(1)}, bf16[32,3,4096]{2,0,1:T(8,128)(2,1)S(1)}, u32[]{:S(2)}, u32[]{:S(2)}) collective-permute-start(bf16[32,3,4096]{2,0,1:T(8,128)(2,1)S(1)} %copy.31), channel_id=1, source_target_pairs={{0,192},{32,224},{64,0},{96,32},{128,64},{160,96},{192,128},{224,1... | collective-permute-start | bytes 2359304 | tf_op jit(solution)/shard_map/ppermute | solution.py:13
  323.5 20.4 %collective-permute-start.5 = (bf16[32,3,4096]{2,0,1:T(8,128)(2,1)S(1)}, bf16[32,3,4096]{2,0,1:T(8,128)(2,1)}, u32[]{:S(2)}, u32[]{:S(2)}) collective-permute-start(bf16[32,3,4096]{2,0,1:T(8,128)(2,1)S(1)} %copy.33), channel_id=1, source_target_pairs={{0,128},{32,160},{64,192},{96,224},{128,0},{160,32},{192,64},{224,... | collective-permute-start | bytes 2359304 | tf_op jit(solution)/shard_map/ppermute | solution.py:13
  352.4 5.2 copy-start.6
  352.4 145.4 %all-to-all-start.1 = ((bf16[32,18,4096]{2,1,0:T(8,128)(2,1)}), bf16[32,18,4096]{2,1,0:T(8,128)(2,1)}, u32[]{:S(2)}, u32[]{:S(2)}) async-start(bf16[32,18,4096]{2,1,0:T(8,128)(2,1)} %pad_maximum_fusion), calls=%async_computation.1 | async-start | bytes 12582912 | tf_op jit(solution)/shard_map/all_to_all | solution.py:83
  506.5 31.1 %copy-start.1 = (bf16[192,4096]{1,0:T(8,128)(2,1)S(1)}, bf16[192,4096]{1,0:T(8,128)(2,1)}, u32[]{:S(2)}) copy-start(bf16[192,4096]{1,0:T(8,128)(2,1)} %param.7) | copy-start | bytes 4718596
Sparse Core Ops, SparseCore 0:
  9.9 45.5 all-gather.2
  57.3 70.2 all-gather.4
where the time goes:
time: 550 us; the launch traced here: 545 us
  waiting for transfers between devices  214 us (39%)
  blocking collectives  151 us (27%)
  other arithmetic  58.7 us (11%)
  local copies, waits for them, and re-layouts  57.4 us (10%)
  starting transfers between devices  28.4 us (5%)
  matrix products  20.3 us (4%)
  between operations  15.3 us (3%)
    all_to_all x1, blocking collectives, body(): lax.all_to_all(outgoing, 'expert', split_axis=0, concat_axis=0, tiled=True)  151 us
    all_to_all x1, waiting for transfers between devices, body(): lax.all_to_all(jnp.concatenate([home_back, spill_back], 1), 'expert', spl...  139 us
    ppermute x6, waiting for transfers between devices, passed_along(): lax.ppermute(shard, axis, [(i, (i + by) % count) for i in range(count)])  73.8 us
    scatter-add x1, other arithmetic, body(): jnp.zeros((tok_rows, model_width), jnp.float32).at[token_of].add(live_rows)  27.9 us
    ppermute x6, starting transfers between devices, passed_along(): lax.ppermute(shard, axis, [(i, (i + by) % count) for i in range(count)])  23.1 us
  transfers between devices with their start and end apart: 9, of which 7 were waited for; matrix products, arithmetic and copies ran while one was open for 13% of the time, Pallas kernels for 0%

commit v1 on v0

v1 whole, which is shorter than its diff:
```python
import functools

import jax
import jax.numpy as jnp
from jax import lax
from jax.experimental import pallas as pl
from jax.experimental.pallas import tpu as pltpu
from jax.sharding import PartitionSpec as P

CAP = 15
OC = 3
MAIN = 16
CUTS = 8
F32 = jnp.float32
BF16 = jnp.bfloat16


def iota(shape, axis):
    return lax.broadcasted_iota(jnp.int32, shape, axis)


def rows_dot(left, right):
    return lax.dot_general(left, right, (((1,), (1,)), ((), ())), preferred_element_type=F32)


def plain_dot(left, right):
    return lax.dot_general(left, right, (((1,), (0,)), ((), ())), preferred_element_type=F32)


def whole(shape):
    return pl.BlockSpec(shape, lambda step: (0,) * len(shape))


def dispatch_kernel(experts, ids_ref, gates_ref, grad_ref, send_ref, rank_ref, main_ref, tail_ref, main_gate, tail_gate, tail_sum):
    step = pl.program_id(0)
    choices, tokens = ids_ref.shape
    rows = experts * MAIN

    @pl.when(step == 0)
    def _():
        expert = iota((experts, tokens), 0)
        hit = jnp.zeros((experts, tokens), F32)
        gate = jnp.zeros((experts, tokens), F32)
        for k in range(choices):
            same = ids_ref[k : k + 1, :] == expert
            hit = jnp.where(same, 1.0, hit)
            gate = jnp.where(same, gates_ref[k : k + 1, :], gate)
        earlier = (iota((tokens, tokens), 0) < iota((tokens, tokens), 1)).astype(F32).astype(BF16)
        rank = jnp.where(hit > 0.0, plain_dot(hit.astype(BF16), earlier), -1.0)
        rank_ref[...] = rank
        position = iota((experts, MAIN, tokens), 1)
        spread_rank = jnp.broadcast_to(rank[:, None, :], (experts, MAIN, tokens))
        spread_gate = jnp.broadcast_to(gate[:, None, :], (experts, MAIN, tokens))
        for wanted, pick_ref, scale_ref in (
            (position, main_ref, main_gate),
            (MAIN + (position >> 3), tail_ref, tail_gate),
        ):
            taken = spread_rank == wanted.astype(F32)
            pick_ref[...] = jnp.where(taken, 1.0, 0.0).reshape(rows, tokens).astype(BF16)
            scale = jnp.where(taken, spread_gate, 0.0).reshape(rows, tokens)
            scale_ref[...] = jnp.sum(scale, axis=1, keepdims=True)
        tail_sum[...] = jnp.zeros_like(tail_sum)

    width = grad_ref.shape[1]

    @pl.when(step < CUTS)
    def _():
        grad = grad_ref[...]
        picked = plain_dot(main_ref[...], grad) * main_gate[...]
        send_ref[...] = picked.astype(BF16).reshape(experts, MAIN, width)
        mine = (iota((rows, width), 0) & (CUTS - 1)) == step
        tail_sum[...] = jnp.where(mine, plain_dot(tail_ref[...], grad), tail_sum[...])

    @pl.when(step == CUTS)
    def _():
        send_ref[...] = (tail_sum[...] * tail_gate[...]).astype(BF16).reshape(experts, MAIN, width)


def dispatch(ids, gates, grad, experts):
    choices, tokens = ids.shape
    model = grad.shape[1]
    width = model // CUTS
    rows = experts * MAIN
    return pl.pallas_call(
        functools.partial(dispatch_kernel, experts),
        grid=(CUTS + 1,),
        in_specs=[
            whole((choices, tokens)),
            whole((choices, tokens)),
            pl.BlockSpec((tokens, width), lambda step: (0, jnp.minimum(step, CUTS - 1))),
        ],
        out_specs=[
            pl.BlockSpec((experts, MAIN, width), lambda step: (0, 0, step)),
            whole((experts, tokens)),
        ],
        out_shape=[
            jax.ShapeDtypeStruct((experts, MAIN, model + width), BF16),
            jax.ShapeDtypeStruct((experts, tokens), F32),
        ],
        scratch_shapes=[
            pltpu.VMEM((rows, tokens), BF16),
            pltpu.VMEM((rows, tokens), BF16),
            pltpu.VMEM((rows, 1), F32),
            pltpu.VMEM((rows, 1), F32),
            pltpu.VMEM((rows, width), F32),
        ],
        compiler_params=pltpu.CompilerParams(vmem_limit_bytes=32 << 20),
        cost_estimate=pl.CostEstimate(
            flops=4 * rows * tokens * model, bytes_accessed=2 * (tokens + rows) * model, transcendentals=0
        ),
        name="dispatch",
    )(ids, gates, grad)


def slot_row(index, experts):
    source, rank = index >> 4, index & (MAIN - 1)
    main = jnp.where(rank < CAP, source * CAP + rank, experts * CAP + source * OC)
    left = index - experts * MAIN
    tail = experts * CAP + (left >> 1) * OC + 1 + (left & 1)
    return jnp.where(index < experts * MAIN, main, tail)


def travel_kernel(experts, own_ref, spill_ref, out_ref, home_pick, spill_pick):
    @pl.when(pl.program_id(0) == 0)
    def _():
        for pick, first in ((home_pick, 0), (spill_pick, experts * CAP)):
            same = slot_row(iota(pick.shape, 0), experts) == first + iota(pick.shape, 1)
            pick[...] = jnp.where(same, 1.0, 0.0).astype(BF16)

    out = plain_dot(home_pick[...], own_ref[...]) + plain_dot(spill_pick[...], spill_ref[...])
    out_ref[...] = out.astype(BF16)


def to_travel_order(own, spill, experts):
    slots, columns = own.shape
    width = columns // 3
    home, rest = experts * CAP, experts * OC
    return pl.pallas_call(
        functools.partial(travel_kernel, experts),
        grid=(3,),
        in_specs=[
            pl.BlockSpec((home, width), lambda step: (0, step)),
            pl.BlockSpec((rest, width), lambda step: (0, step)),
        ],
        out_specs=pl.BlockSpec((slots, width), lambda step: (0, step)),
        out_shape=jax.ShapeDtypeStruct((slots, columns), BF16),
        scratch_shapes=[pltpu.VMEM((slots, home), BF16), pltpu.VMEM((slots, rest), BF16)],
        compiler_params=pltpu.CompilerParams(vmem_limit_bytes=16 << 20),
        cost_estimate=pl.CostEstimate(
            flops=2 * slots * slots * columns, bytes_accessed=4 * slots * columns, transcendentals=0
        ),
        name="to_travel",
    )(own, spill)


def slots_kernel(experts, rows_ref, out_ref, pick):
    @pl.when(pl.program_id(0) == 0)
    def _():
        same = slot_row(iota(pick.shape, 1), experts) == iota(pick.shape, 0)
        pick[...] = jnp.where(same, 1.0, 0.0).astype(BF16)

    out_ref[...] = plain_dot(pick[...], rows_ref[...]).astype(BF16)


def to_slot_order(rows, experts):
    slots, columns = rows.shape
    width = columns // 3
    return pl.pallas_call(
        functools.partial(slots_kernel, experts),
        grid=(3,),
        in_specs=[pl.BlockSpec((slots, width), lambda step: (0, step))],
        out_specs=pl.BlockSpec((slots, width), lambda step: (0, step)),
        out_shape=jax.ShapeDtypeStruct((slots, columns), BF16),
        scratch_shapes=[pltpu.VMEM((slots, slots), BF16)],
        compiler_params=pltpu.CompilerParams(vmem_limit_bytes=16 << 20),
        cost_estimate=pl.CostEstimate(
            flops=2 * slots * slots * columns, bytes_accessed=4 * slots * columns, transcendentals=0
        ),
        name="to_slots",
    )(rows)


def hidden_kernel(experts, main_ref, tail_ref, down_ref, gate_ref, up_ref, out_gate_ref, out_up_ref, rows_ref):
    model = down_ref.shape[1]
    width = model // CUTS
    full = experts * MAIN
    left = experts * 2

    @pl.when(pl.program_id(0) == 0)
    def _():
        rows_ref[pl.ds(0, full), :] = main_ref[...].reshape(full, model)
        tail = tail_ref[...].reshape(full, width)
        row, lane = iota((left, full), 0), iota((left, full), 1)
        for cut in range(CUTS):
            pick = jnp.where(lane == row * CUTS + cut, 1.0, 0.0).astype(BF16)
            rows_ref[pl.ds(full, left), pl.ds(cut * width, width)] = plain_dot(pick, tail).astype(BF16)

    hidden_cot = rows_dot(rows_ref[...], down_ref[...])
    gate = gate_ref[...].astype(F32)
    up = up_ref[...].astype(F32)
    sigma = jax.nn.sigmoid(gate)
    out_gate_ref[...] = (hidden_cot * up * sigma * (1.0 + gate * (1.0 - sigma))).astype(BF16)
    out_up_ref[...] = (hidden_cot * gate * sigma).astype(BF16)


def hidden_pass(arrived, down, pre_acts):
    experts = arrived.shape[0]
    hidden, model = down.shape
    slots = pre_acts.shape[0]
    parts = 3
    width = hidden // parts
    return pl.pallas_call(
        functools.partial(hidden_kernel, experts),
        grid=(parts,),
        in_specs=[
            pl.BlockSpec((experts, MAIN, model), lambda step: (0, 0, 0)),
            pl.BlockSpec((experts, MAIN, model // CUTS), lambda step: (0, 0, CUTS)),
            pl.BlockSpec((width, model), lambda step: (step, 0)),
            pl.BlockSpec((slots, width), lambda step: (0, step)),
            pl.BlockSpec((slots, width), lambda step: (0, parts + step)),
        ],
        out_specs=[pl.BlockSpec((slots, width), lambda step: (0, step))] * 2,
        out_shape=[jax.ShapeDtypeStruct((slots, hidden), BF16)] * 2,
        scratch_shapes=[pltpu.VMEM((slots, model), BF16)],
        compiler_params=pltpu.CompilerParams(vmem_limit_bytes=40 << 20),
        cost_estimate=pl.CostEstimate(
            flops=2 * slots * hidden * model,
            bytes_accessed=2 * (slots * model + hidden * model + 4 * slots * hidden),
            transcendentals=slots * hidden,
        ),
        name="hidden",
    )(arrived, arrived, down, pre_acts, pre_acts)


def back_kernel(experts, gate_ref, up_ref, weight_ref, out_ref, tail_sum):
    step = pl.program_id(0)
    full = experts * MAIN
    left = experts * 2
    width = weight_ref.shape[0]
    hidden = gate_ref.shape[1]

    @pl.when(step == 0)
    def _():
        tail_sum[...] = jnp.zeros_like(tail_sum)

    @pl.when(step < CUTS)
    def _():
        back = rows_dot(gate_ref[...], weight_ref[:, :hidden]) + rows_dot(up_ref[...], weight_ref[:, hidden:])
        back = back.astype(BF16)
        out_ref[...] = back[:full].reshape(experts, MAIN, width)
        spread = jnp.where((iota((full, left), 0) >> 3) == iota((full, left), 1), 1.0, 0.0).astype(BF16)
        mine = (iota((full, width), 0) & (CUTS - 1)) == step
        tail_sum[...] = jnp.where(mine, plain_dot(spread, back[full:]), tail_sum[...])

    @pl.when(step == CUTS)
    def _():
        out_ref[...] = tail_sum[...].astype(BF16).reshape(experts, MAIN, width)


def back_pass(gate_grad, up_grad, weight, experts):
    slots, hidden = gate_grad.shape
    model = weight.shape[0]
    width = model // CUTS
    return pl.pallas_call(
        functools.partial(back_kernel, experts),
        grid=(CUTS + 1,),
        in_specs=[
            whole((slots, hidden)),
            whole((slots, hidden)),
            pl.BlockSpec((width, 2 * hidden), lambda step: (jnp.minimum(step, CUTS - 1), 0)),
        ],
        out_specs=pl.BlockSpec((experts, MAIN, width), lambda step: (0, 0, step)),
        out_shape=jax.ShapeDtypeStruct((experts, MAIN, model + width), BF16),
        scratch_shapes=[pltpu.VMEM((experts * MAIN, width), F32)],
        compiler_params=pltpu.CompilerParams(vmem_limit_bytes=32 << 20),
        cost_estimate=pl.CostEstimate(
            flops=4 * slots * hidden * model,
            bytes_accessed=2 * (slots * model + 2 * hidden * model + 2 * slots * hidden),
            transcendentals=0,
        ),
        name="back",
    )(gate_grad, up_grad, weight)


def combine_kernel(experts, rank_ref, main_ref, tail_ref, out_ref, pick, spread):
    step = pl.program_id(0)
    tokens = rank_ref.shape[1]
    full = experts * MAIN
    width = out_ref.shape[1]

    @pl.when(step == 0)
    def _():
        same = jnp.where(iota((tokens, tokens), 0) == iota((tokens, tokens), 1), 1.0, 0.0).astype(BF16)
        by_token = rows_dot(same, rank_ref[...].astype(BF16)).astype(BF16)
        widen = jnp.where((iota((experts, full), 1) >> 4) == iota((experts, full), 0), 1.0, 0.0).astype(BF16)
        spread[...] = plain_dot(by_token, widen)
        place = (iota((tokens, full), 1) & (MAIN - 1)).astype(F32)
        pick[...] = jnp.where(spread[...] == place, 1.0, 0.0).astype(BF16)

    lane = iota((tokens, full), 1)
    place = (MAIN + ((lane >> 3) & 1)).astype(F32)
    mine = (spread[...] == place) & ((lane & (CUTS - 1)) == step)
    total = plain_dot(pick[...], main_ref[...].reshape(full, width))
    total += plain_dot(jnp.where(mine, 1.0, 0.0).astype(BF16), tail_ref[...].reshape(full, width))
    out_ref[...] = total.astype(BF16)


def combine(rank, returned):
    experts, tokens = rank.shape
    width = returned.shape[2] // (CUTS + 1)
    model = width * CUTS
    full = experts * MAIN
    return pl.pallas_call(
        functools.partial(combine_kernel, experts),
        grid=(CUTS,),
        in_specs=[
            whole((experts, tokens)),
            pl.BlockSpec((experts, MAIN, width), lambda step: (0, 0, step)),
            pl.BlockSpec((experts, MAIN, width), lambda step: (0, 0, CUTS)),
        ],
        out_specs=pl.BlockSpec((tokens, width), lambda step: (0, step)),
        out_shape=jax.ShapeDtypeStruct((tokens, model), BF16),
        scratch_shapes=[pltpu.VMEM((tokens, full), BF16), pltpu.VMEM((tokens, full), F32)],
        compiler_params=pltpu.CompilerParams(vmem_limit_bytes=32 << 20),
        cost_estimate=pl.CostEstimate(
            flops=4 * full * tokens * model, bytes_accessed=2 * (tokens + full) * model, transcendentals=0
        ),
        name="combine",
    )(rank, returned, returned)


def moved(rows, offset, sign):
    replicas = lax.axis_size("dp")
    for bit in range(replicas.bit_length() - 1):
        by = sign * (1 << bit)
        shifted = lax.ppermute(rows, "dp", [(i, (i + by) % replicas) for i in range(replicas)])
        rows = jnp.where(offset >> bit & 1 == 1, shifted, rows)
    return rows


def exchange(blocks):
    return lax.all_to_all(blocks, "expert", split_axis=0, concat_axis=0, tiled=True)


def body(out_grad, route_gates, expert_ids, partner_offset, saved_pre, down_weight, gate_up_weight):
    experts = lax.axis_size("expert")
    home = experts * CAP
    offset = partner_offset[0]
    own_pre = saved_pre[0, 0]
    down = lax.all_gather(down_weight[0], "dp", axis=1, tiled=True)
    gate_up = lax.all_gather(gate_up_weight[0], "dp", axis=0, tiled=True)
    sent, rank = dispatch(expert_ids.T, route_gates.T, out_grad, experts)
    arrived = exchange(sent)
    spill_pre = moved(own_pre[home:], offset, -1)
    pre_acts = to_travel_order(own_pre, spill_pre, experts)
    gate_grad, up_grad = hidden_pass(arrived, down, pre_acts)
    back = back_pass(gate_grad, up_grad, gate_up, experts)
    returned = exchange(back)
    by_slot = to_slot_order(jnp.concatenate([gate_grad, up_grad], 1), experts)
    spill_grad = moved(by_slot[home:], offset, 1)
    hidden_grad = lax.dynamic_update_slice(by_slot, spill_grad, (home, 0))
    token_grad = combine(rank, returned)
    return token_grad, hidden_grad.reshape(saved_pre.shape)


def solution(mesh):
    placed = (
        P(("dp", "expert"), None),
        P(("dp", "expert"), None),
        P(("dp", "expert"), None),
        P("expert"),
        P("dp", "expert", None, None),
        P("expert", None, "dp"),
        P("expert", "dp", None),
    )
    return jax.shard_map(
        body,
        mesh=mesh,
        in_specs=placed,
        out_specs=(P(("dp", "expert"), None), P("dp", "expert", None, None)),
        check_vma=False,
    )
```

time: 550 us -> 296 us (0.54)
  blocking collectives: 151 us -> 0 us
  other arithmetic: 58.7 us -> 2.06 us
  local copies, waits for them, and re-layouts: 57.4 us -> 13.5 us
  Pallas kernels: 0 us -> 37.9 us
  matrix products: 20.3 us -> 0 us
  waiting for transfers between devices: 214 us -> 195 us
    all_to_all x1 -> x0, blocking collectives: 151 us -> none  [body(): lax.all_to_all(outgoing, 'expert', split_axis=0, concat_axis=0, tiled=True)]
    pallas_call x0 -> x6, Pallas kernels: none -> 37.9 us  [the longest x1 11.6 us: back_pass(): pl.pallas_call(functools.partial(back_kernel, experts), grid=(CUTS + 1,),...]
    scatter-add x1 -> x0, other arithmetic: 27.9 us -> none  [body(): jnp.zeros((tok_rows, model_width), jnp.float32).at[token_of].add(live_rows)]
    dot_general x2 -> x0, matrix products: 20.3 us -> none  [the longest x1 10.8 us: body(): jnp.einsum('rc,nc->rn', hidden_grad, lax.all_gather(gate_up_weight, 'dp',...]
    ppermute x6, waiting for transfers between devices: 73.8 us -> 54.8 us  [moved(): lax.ppermute(rows, 'dp', [(i, (i + by) % replicas) for i in range(replica...]
    convert_element_type x2 -> x0, local copies, waits for them, and re-layouts: 17.4 us -> none  [the longest x1 8.73 us: body(): out_grad[token_of].astype(jnp.float32)]
    convert_element_type x3 -> x0, other arithmetic: 15 us -> none  [the longest x1 9.52 us: body(): (gate_of[:, None] * out_grad[token_of].astype(jnp.float32)).astype(jnp.bf...]
    ppermute x6, starting transfers between devices: 23.1 us -> 8.86 us  [moved(): lax.ppermute(rows, 'dp', [(i, (i + by) % replicas) for i in range(replica...]
  transfers between devices with their start and end apart: 9 -> 10, of which waited for: 7 -> 8; matrix products, arithmetic and copies ran while one was open for 13% -> 1% of each run, Pallas kernels for 0% -> 6%
where the time goes in v1:
time: 296 us; the launch traced here: 292 us
  waiting for transfers between devices  195 us (66%)
  Pallas kernels  37.9 us (13%)
  starting transfers between devices  28.2 us (10%)
  between operations  14.9 us (5%)
  local copies, waits for them, and re-layouts  13.5 us (5%)
    all_to_all x2, waiting for transfers between devices, exchange(): lax.all_to_all(blocks, 'expert', split_axis=0, concat_axis=0, tiled=True)  139 us
    ppermute x6, waiting for transfers between devices, moved(): lax.ppermute(rows, 'dp', [(i, (i + by) % replicas) for i in range(replica...  54.8 us
    all_to_all x2, starting transfers between devices, exchange(): lax.all_to_all(blocks, 'expert', split_axis=0, concat_axis=0, tiled=True)  19.3 us
    unnamed x20, local copies, waits for them, and re-layouts  12.4 us
    pallas_call x1, Pallas kernels, back_pass(): pl.pallas_call(functools.partial(back_kernel, experts), grid=(CUTS + 1,),...  11.6 us
    ppermute x6, starting transfers between devices, moved(): lax.ppermute(rows, 'dp', [(i, (i + by) % replicas) for i in range(replica...  8.86 us
    pallas_call x1, Pallas kernels, hidden_pass(): pl.pallas_call(functools.partial(hidden_kernel, experts), grid=(parts,),...  8.31 us
    pallas_call x1, Pallas kernels, combine(): pl.pallas_call(functools.partial(combine_kernel, experts), grid=(CUTS,),...  7.84 us
  transfers between devices with their start and end apart: 10, of which 8 were waited for; matrix products, arithmetic and copies ran while one was open for 1% of the time, Pallas kernels for 6%

profile of v1, /device:TPU:35, one launch (start us, length us, event | category | flops | bytes accessed | tf_op | source)
XLA Modules:
  0.0 291.8 jit_solution(13464830772795120411)
XLA Ops:
  7.2 0.0 copy-start.8
  7.2 0.0 copy-start.9
  7.2 0.0 copy-start.7
  7.2 0.0 all-gather.5.cloned.1.call-start
  7.2 0.7 all-gather.5.cloned.1.call-update
  7.9 0.0 all-gather.7.cloned.1.call-start
  8.0 0.7 all-gather.7.cloned.1.call-update
  8.7 0.0 copy-done.8
  8.7 0.0 copy-done.9
  8.7 0.0 copy-done.7
  8.7 4.7 %dispatch.1 = (bf16[32,16,4608]{2,1,0:T(8,128)(2,1)S(1)}, f32[32,192]{1,0:T(8,128)S(1)}) custom-call(s32[8,192]{1,0:T(8,128)S(1)} %bitcast.18, f32[8,192]{1,0:T(8,128)S(1)} %bitcast.19, bf16[192,4096]{1,0:T(8,128)(2,1)S(1)} %copy-done.7), custom_call_target="tpu_custom_call" | custom-call | flops 1610612736 | bytes 5767168 | tf_op jit(solution)/shard_map/dispatch/pallas_call | solution.py:84
  13.4 0.0 copy-start.1
  13.4 2.2 copy-done.1
  15.6 0.0 copy-start.4
  15.6 0.6 copy-done.4
  16.2 11.0 %all-to-all-start = ((bf16[32,16,4608]{2,1,0:T(8,128)(2,1)}), bf16[32,16,4608]{2,1,0:T(8,128)(2,1)}, u32[]{:S(2)}, u32[]{:S(2)}) async-start(bf16[32,16,4608]{2,1,0:T(8,128)(2,1)} %copy-done.1), calls=%async_computation | async-start | bytes 9437184 | tf_op jit(solution)/shard_map/all_to_all | solution.py:342
  27.2 0.0 copy-done.3
  27.3 1.2 collective-permute-start
  29.2 11.5 %collective-permute-done = bf16[96,1536]{1,0:T(8,128)(2,1)S(1)} collective-permute-done((bf16[96,1536]{1,0:T(8,128)(2,1)S(1)}, bf16[96,1536]{1,0:T(8,128)(2,1)S(1)}, u32[]{:S(2)}, u32[]{:S(2)}) %collective-permute-start) | collective-permute-done | bytes 294944 | tf_op jit(solution)/shard_map/ppermute | solution.py:336
  40.7 0.3 collective-permute-start.1
  41.1 14.8 %collective-permute-done.1 = bf16[96,1536]{1,0:T(8,128)(2,1)S(1)} collective-permute-done((bf16[96,1536]{1,0:T(8,128)(2,1)S(1)}, bf16[96,1536]{1,0:T(8,128)(2,1)S(1)}, u32[]{:S(2)}, u32[]{:S(2)}) %collective-permute-start.1) | collective-permute-done | bytes 294944 | tf_op jit(solution)/shard_map/ppermute | solution.py:336
  55.9 3.6 %collective-permute-start.2 = (bf16[96,1536]{1,0:T(8,128)(2,1)S(1)}, bf16[96,1536]{1,0:T(8,128)(2,1)S(1)}, u32[]{:S(2)}, u32[]{:S(2)}) collective-permute-start(bf16[96,1536]{1,0:T(8,128)(2,1)S(1)} %broadcast_select_fusion.3), channel_id=1, source_target_pairs={{0,128},{32,160},{64,192},{96,224},{128,0},{160,32},{192,64},{224,... | collective-permute-start | bytes 884744 | tf_op jit(solution)/shard_map/ppermute | solution.py:336
  59.4 10.8 %collective-permute-done.2 = bf16[96,1536]{1,0:T(8,128)(2,1)S(1)} collective-permute-done((bf16[96,1536]{1,0:T(8,128)(2,1)S(1)}, bf16[96,1536]{1,0:T(8,128)(2,1)S(1)}, u32[]{:S(2)}, u32[]{:S(2)}) %collective-permute-start.2) | collective-permute-done | bytes 294944 | tf_op jit(solution)/shard_map/ppermute | solution.py:336
  70.2 2.3 to_travel.1.gate_ref.up_ref
  72.5 61.0 %all-to-all-done.main_ref.tail_ref = bf16[32,16,4608]{2,1,0:T(8,128)(2,1)} async-done(((bf16[32,16,4608]{2,1,0:T(8,128)(2,1)}), bf16[32,16,4608]{2,1,0:T(8,128)(2,1)}, u32[]{:S(2)}, u32[]{:S(2)}) %all-to-all-start) | async-done | bytes 4718624 | tf_op jit(solution)/shard_map/all_to_all | solution.py:342
  133.6 2.9 copy-done
  136.5 8.3 %hidden.1 = (bf16[576,768]{1,0:T(8,128)(2,1)S(1)}, bf16[576,768]{1,0:T(8,128)(2,1)S(1)}) custom-call(bf16[32,16,4608]{2,1,0:T(8,128)(2,1)} %all-to-all-done.main_ref.tail_ref, bf16[32,16,4608]{2,1,0:T(8,128)(2,1)} %all-to-all-done.main_ref.tail_ref, bf16[768,4096]{1,0:T(8,128)(2,1)S(1)} %bitcast.15, bf16[576,1536]{1,0:T(8,128)(2,1)S(1)} %to_travel.1.gate_ref.up_ref, ...), custom_call_target="tpu_custom_call" | custom-call | flops 3623878656 | bytes 14548992 | tf_op jit(solution)/shard_map/hidden/pallas_call | solution.py:212
  144.8 0.0 all-gather.7.cloned.1.call-done
  144.8 0.0 copy-start.6
  144.8 4.6 %copy-done.6 = bf16[1,4096,1536]{2,1,0:T(8,128)(2,1)S(1)} copy-done((bf16[1,4096,1536]{2,1,0:T(8,128)(2,1)S(1)}, bf16[1,4096,1536]{2,1,0:T(8,128)(2,1)}, u32[]{:S(2)}) %copy-start.6) | copy-done | bytes 12582936
  149.4 11.6 %back.1 = bf16[32,16,4608]{2,1,0:T(8,128)(2,1)S(1)} custom-call(bf16[576,768]{1,0:T(8,128)(2,1)S(1)} %get-tuple-element.8.gate_ref, bf16[576,768]{1,0:T(8,128)(2,1)S(1)} %get-tuple-element.9.up_ref, bf16[4096,1536]{1,0:T(8,128)(2,1)S(1)} %bitcast.17), custom_call_target="tpu_custom_call" | custom-call | flops 7247757312 | bytes 19070976 | tf_op jit(solution)/shard_map/back/pallas_call | solution.py:264
  161.0 0.0 copy-start.2
  161.0 2.2 copy-done.2
  163.2 8.3 %all-to-all-start.1 = ((bf16[32,16,4608]{2,1,0:T(8,128)(2,1)}), bf16[32,16,4608]{2,1,0:T(8,128)(2,1)}, u32[]{:S(2)}, u32[]{:S(2)}) async-start(bf16[32,16,4608]{2,1,0:T(8,128)(2,1)} %copy-done.2), calls=%async_computation.1 | async-start | bytes 9437184 | tf_op jit(solution)/shard_map/all_to_all | solution.py:342
  171.5 0.1 pad_maximum_fusion.rows_ref
  171.7 3.1 %to_slots.1 = bf16[576,1536]{1,0:T(8,128)(2,1)} custom-call(bf16[576,1536]{1,0:T(8,128)(2,1)S(1)} %pad_maximum_fusion.rows_ref), custom_call_target="tpu_custom_call" | custom-call | flops 1019215872 | bytes 3538944 | tf_op jit(solution)/shard_map/to_slots/pallas_call | solution.py:168
  174.8 1.0 slice.12
  175.8 2.5 collective-permute-start.3
  178.3 3.7 %collective-permute-done.3 = bf16[96,1536]{1,0:T(8,128)(2,1)S(1)} collective-permute-done((bf16[96,1536]{1,0:T(8,128)(2,1)S(1)}, bf16[96,1536]{1,0:T(8,128)(2,1)S(1)}, u32[]{:S(2)}, u32[]{:S(2)}) %collective-permute-start.3) | collective-permute-done | bytes 294944 | tf_op jit(solution)/shard_map/ppermute | solution.py:336
  181.9 1.0 broadcast_select_fusion
  182.9 1.1 collective-permute-start.4
  184.1 6.2 %collective-permute-done.4 = bf16[96,1536]{1,0:T(8,128)(2,1)S(1)} collective-permute-done((bf16[96,1536]{1,0:T(8,128)(2,1)S(1)}, bf16[96,1536]{1,0:T(8,128)(2,1)S(1)}, u32[]{:S(2)}, u32[]{:S(2)}) %collective-permute-start.4) | collective-permute-done | bytes 294944 | tf_op jit(solution)/shard_map/ppermute | solution.py:336
  190.3 0.1 collective-permute-start.5
  190.4 7.9 %collective-permute-done.5 = bf16[96,1536]{1,0:T(8,128)(2,1)S(1)} collective-permute-done((bf16[96,1536]{1,0:T(8,128)(2,1)S(1)}, bf16[96,1536]{1,0:T(8,128)(2,1)S(1)}, u32[]{:S(2)}, u32[]{:S(2)}) %collective-permute-start.5) | collective-permute-done | bytes 294944 | tf_op jit(solution)/shard_map/ppermute | solution.py:336
  198.3 0.8 bitcast_dynamic-update-slice_fusion
  199.1 78.0 %all-to-all-done.1.main_ref.tail_ref = bf16[32,16,4608]{2,1,0:T(8,128)(2,1)} async-done(((bf16[32,16,4608]{2,1,0:T(8,128)(2,1)}), bf16[32,16,4608]{2,1,0:T(8,128)(2,1)}, u32[]{:S(2)}, u32[]{:S(2)}) %all-to-all-start.1) | async-done | bytes 4718624 | tf_op jit(solution)/shard_map/all_to_all | solution.py:342
  277.1 0.0 copy-done.5
  277.1 7.8 %combine.1 = bf16[192,4096]{1,0:T(8,128)(2,1)} custom-call(f32[32,192]{1,0:T(8,128)S(1)} %copy-done.5, bf16[32,16,4608]{2,1,0:T(8,128)(2,1)} %all-to-all-done.1.main_ref.tail_ref, bf16[32,16,4608]{2,1,0:T(8,128)(2,1)} %all-to-all-done.1.main_ref.tail_ref), custom_call_target="tpu_custom_call" | custom-call | flops 1610612736 | bytes 5767168 | tf_op jit(solution)/shard_map/combine/pallas_call | solution.py:313
  (9 shorter events, 0.2 us)
Async XLA Ops:
  7.2 1.5 copy-start.8
  7.2 1.5 copy-start.9
  7.2 1.5 copy-start.7
  7.2 126.4 %all-gather.5.cloned.1.call-start = ((), (), s32[]{:S(2)}) async-start(), calls=%async_computation.2 | async-start | bytes 7077888 | tf_op jit(solution)/shard_map/all_gather | solution.py:350
  7.9 136.9 %all-gather.7.cloned.1.call-start = ((), (), s32[]{:S(2)}) async-start(), calls=%async_computation.3 | async-start | bytes 14155776 | tf_op jit(solution)/shard_map/all_gather | solution.py:351
  13.4 2.2 copy-start.1
  15.6 0.6 copy-start.4
  16.2 11.0 %copy-start.3 = (bf16[1,1,576,1536]{3,2,1,0:T(8,128)(2,1)S(1)}, bf16[1,1,576,1536]{3,2,1,0:T(8,128)(2,1)}, u32[]{:S(2)}) copy-start(bf16[1,1,576,1536]{3,2,1,0:T(8,128)(2,1)} %param.11) | copy-start | bytes 5308420
  16.2 117.4 %all-to-all-start = ((bf16[32,16,4608]{2,1,0:T(8,128)(2,1)}), bf16[32,16,4608]{2,1,0:T(8,128)(2,1)}, u32[]{:S(2)}, u32[]{:S(2)}) async-start(bf16[32,16,4608]{2,1,0:T(8,128)(2,1)} %copy-done.1), calls=%async_computation | async-start | bytes 9437184 | tf_op jit(solution)/shard_map/all_to_all | solution.py:342
  27.3 13.4 %collective-permute-start = (bf16[96,1536]{1,0:T(8,128)(2,1)S(1)}, bf16[96,1536]{1,0:T(8,128)(2,1)S(1)}, u32[]{:S(2)}, u32[]{:S(2)}) collective-permute-start(bf16[96,1536]{1,0:T(8,128)(2,1)S(1)} %slice_bitcast_fusion), channel_id=1, source_target_pairs={{0,224},{32,0},{64,32},{96,64},{128,96},{160,128},{192,160},{224,1... | collective-permute-start | bytes 884744 | tf_op jit(solution)/shard_map/ppermute | solution.py:336
  40.7 15.1 %collective-permute-start.1 = (bf16[96,1536]{1,0:T(8,128)(2,1)S(1)}, bf16[96,1536]{1,0:T(8,128)(2,1)S(1)}, u32[]{:S(2)}, u32[]{:S(2)}) collective-permute-start(bf16[96,1536]{1,0:T(8,128)(2,1)S(1)} %broadcast_select_fusion.1), channel_id=1, source_target_pairs={{0,192},{32,224},{64,0},{96,32},{128,64},{160,96},{192,128},{224,1... | collective-permute-start | bytes 884744 | tf_op jit(solution)/shard_map/ppermute | solution.py:336
  55.9 14.3 %collective-permute-start.2 = (bf16[96,1536]{1,0:T(8,128)(2,1)S(1)}, bf16[96,1536]{1,0:T(8,128)(2,1)S(1)}, u32[]{:S(2)}, u32[]{:S(2)}) collective-permute-start(bf16[96,1536]{1,0:T(8,128)(2,1)S(1)} %broadcast_select_fusion.3), channel_id=1, source_target_pairs={{0,128},{32,160},{64,192},{96,224},{128,0},{160,32},{192,64},{224,... | collective-permute-start | bytes 884744 | tf_op jit(solution)/shard_map/ppermute | solution.py:336
  133.6 2.9 copy-start
  144.8 4.6 %copy-start.6 = (bf16[1,4096,1536]{2,1,0:T(8,128)(2,1)S(1)}, bf16[1,4096,1536]{2,1,0:T(8,128)(2,1)}, u32[]{:S(2)}) copy-start(bf16[1,4096,1536]{2,1,0:T(8,128)(2,1)} %all-gather.7.cloned.1.call-done) | copy-start | bytes 37748740
  161.0 2.2 copy-start.2
  163.2 113.9 %all-to-all-start.1 = ((bf16[32,16,4608]{2,1,0:T(8,128)(2,1)}), bf16[32,16,4608]{2,1,0:T(8,128)(2,1)}, u32[]{:S(2)}, u32[]{:S(2)}) async-start(bf16[32,16,4608]{2,1,0:T(8,128)(2,1)} %copy-done.2), calls=%async_computation.1 | async-start | bytes 9437184 | tf_op jit(solution)/shard_map/all_to_all | solution.py:342
  174.8 102.3 %copy-start.5 = (f32[32,192]{1,0:T(8,128)S(1)}, f32[32,192]{1,0:T(8,128)}, u32[]{:S(2)}) copy-start(f32[32,192]{1,0:T(8,128)} %copy-done.4) | copy-start | bytes 73732
  175.8 6.2 %collective-permute-start.3 = (bf16[96,1536]{1,0:T(8,128)(2,1)S(1)}, bf16[96,1536]{1,0:T(8,128)(2,1)S(1)}, u32[]{:S(2)}, u32[]{:S(2)}) collective-permute-start(bf16[96,1536]{1,0:T(8,128)(2,1)S(1)} %slice.12), channel_id=1, source_target_pairs={{0,32},{32,64},{64,96},{96,128},{128,160},{160,192},{192,224},{224... | collective-permute-start | bytes 884744 | tf_op jit(solution)/shard_map/ppermute | solution.py:336
  182.9 7.3 %collective-permute-start.4 = (bf16[96,1536]{1,0:T(8,128)(2,1)S(1)}, bf16[96,1536]{1,0:T(8,128)(2,1)S(1)}, u32[]{:S(2)}, u32[]{:S(2)}) collective-permute-start(bf16[96,1536]{1,0:T(8,128)(2,1)S(1)} %broadcast_select_fusion), channel_id=1, source_target_pairs={{0,64},{32,96},{64,128},{96,160},{128,192},{160,224},{192,0},{224,... | collective-permute-start | bytes 884744 | tf_op jit(solution)/shard_map/ppermute | solution.py:336
  190.3 8.0 %collective-permute-start.5 = (bf16[96,1536]{1,0:T(8,128)(2,1)S(1)}, bf16[96,1536]{1,0:T(8,128)(2,1)S(1)}, u32[]{:S(2)}, u32[]{:S(2)}) collective-permute-start(bf16[96,1536]{1,0:T(8,128)(2,1)S(1)} %broadcast_select_fusion.2), channel_id=1, source_target_pairs={{0,128},{32,160},{64,192},{96,224},{128,0},{160,32},{192,64},{224,... | collective-permute-start | bytes 884744 | tf_op jit(solution)/shard_map/ppermute | solution.py:336
Sparse Core Ops, SparseCore 0:
  9.9 58.1 all-gather.4
  69.9 71.4 all-gather.6

commit v2 on v0

v2 whole, which is shorter than its diff:
```python
import functools

import jax
import jax.numpy as jnp
from jax import lax
from jax.experimental import pallas as pl
from jax.experimental.pallas import tpu as pltpu
from jax.sharding import PartitionSpec as P

CAP = 15
OC = 3
MAIN = 16
CUTS = 8
F32 = jnp.float32
BF16 = jnp.bfloat16


def iota(shape, axis):
    return lax.broadcasted_iota(jnp.int32, shape, axis)


def rows_dot(left, right):
    return lax.dot_general(left, right, (((1,), (1,)), ((), ())), preferred_element_type=F32)


def plain_dot(left, right):
    return lax.dot_general(left, right, (((1,), (0,)), ((), ())), preferred_element_type=F32)


def whole(shape):
    return pl.BlockSpec(shape, lambda step: (0,) * len(shape))


def piece_rows(shape, travel_axis, left):
    travelling, by_piece = iota(shape, travel_axis), iota(shape, 1 - travel_axis)
    same = travelling == ((by_piece & (left - 1)) << 3) + (by_piece >> (left.bit_length() - 1))
    return jnp.where(same, 1.0, 0.0).astype(BF16)


def anywhere():
    return pl.BlockSpec(memory_space=pl.ANY)


def in_vmem():
    return pl.BlockSpec(memory_space=pltpu.VMEM)


def columns(cut, width):
    return pl.ds(pl.multiple_of(cut * width, width), width)


def dispatch_kernel(
    experts, ids_ref, gates_ref, grad_ref, send_ref, rank_ref, main_pick, tail_pick, main_gate, tail_gate, stage, pieces, sems
):
    choices, tokens = ids_ref.shape
    full, left = experts * MAIN, experts * 2
    width = grad_ref.shape[1] // CUTS
    expert = iota((experts, tokens), 0)
    hit = jnp.zeros((experts, tokens), F32)
    gate = jnp.zeros((experts, tokens), F32)
    for k in range(choices):
        same = ids_ref[k : k + 1, :] == expert
        hit = jnp.where(same, 1.0, hit)
        gate = jnp.where(same, gates_ref[k : k + 1, :], gate)
    earlier = (iota((tokens, tokens), 0) < iota((tokens, tokens), 1)).astype(F32).astype(BF16)
    rank = jnp.where(hit > 0.0, plain_dot(hit.astype(BF16), earlier), -1.0)
    rank_ref[...] = rank
    for deep, first, pick_ref, scale_ref in ((MAIN, 0, main_pick, main_gate), (8, MAIN, tail_pick, tail_gate)):
        position = iota((experts, deep, tokens), 1)
        wanted = (first + position).astype(F32)
        taken = jnp.broadcast_to(rank[:, None, :], wanted.shape) == wanted
        scale = jnp.where(taken, jnp.broadcast_to(gate[:, None, :], wanted.shape), 0.0)
        one = jnp.where(taken, 1.0, 0.0)
        if deep == MAIN:
            pick_ref[...] = one.reshape(full, tokens).astype(BF16)
            scale_ref[...] = jnp.sum(scale.reshape(full, tokens), axis=1, keepdims=True)
        else:
            row = iota((left, experts * deep), 0)
            keep = iota((left, experts * deep), 1) == ((row >> 1) << 3) + (row & 1)
            keep = jnp.where(keep, 1.0, 0.0)
            pick_ref[...] = plain_dot(keep.astype(BF16), one.reshape(experts * deep, tokens).astype(BF16)).astype(BF16)
            by_row = rows_by(gate, left)
            scale_ref[...] = jnp.sum(jnp.where(pick_ref[...].astype(F32) > 0.0, by_row, 0.0), axis=1, keepdims=True)

    def one_cut(cut, carry):
        grad = grad_ref[:, columns(cut, width)]
        picked = plain_dot(main_pick[...], grad) * main_gate[...]
        stage[cut] = picked.astype(BF16)
        pltpu.make_async_copy(stage.at[cut], send_ref.at[:, columns(cut, width)], sems.at[cut]).start()
        pieces[cut] = (plain_dot(tail_pick[...], grad) * tail_gate[...]).astype(BF16)
        return carry

    lax.fori_loop(0, CUTS, one_cut, 0)
    stage[CUTS] = plain_dot(piece_rows((full, full), 0, left), pieces[...].reshape(full, width)).astype(BF16)
    pltpu.make_async_copy(stage.at[CUTS], send_ref.at[:, columns(CUTS, width)], sems.at[CUTS]).start()

    def finish(cut, carry):
        pltpu.make_async_copy(stage.at[cut], send_ref.at[:, columns(cut, width)], sems.at[cut]).wait()
        return carry

    lax.fori_loop(0, CUTS + 1, finish, 0)


def rows_by(values, rows):
    n, m = values.shape
    return jnp.broadcast_to(values[:, None, :], (n, rows // n, m)).reshape(rows, m)


def dispatch(ids, gates, grad, experts):
    choices, tokens = ids.shape
    model = grad.shape[1]
    width = model // CUTS
    full, left = experts * MAIN, experts * 2
    return pl.pallas_call(
        functools.partial(dispatch_kernel, experts),
        in_specs=[in_vmem()] * 3,
        out_specs=[anywhere(), in_vmem()],
        out_shape=[
            jax.ShapeDtypeStruct((full, model + width), BF16),
            jax.ShapeDtypeStruct((experts, tokens), F32),
        ],
        scratch_shapes=[
            pltpu.VMEM((full, tokens), BF16),
            pltpu.VMEM((left, tokens), BF16),
            pltpu.VMEM((full, 1), F32),
            pltpu.VMEM((left, 1), F32),
            pltpu.VMEM((CUTS + 1, full, width), BF16),
            pltpu.VMEM((CUTS, left, width), BF16),
            pltpu.SemaphoreType.DMA((CUTS + 1,)),
        ],
        compiler_params=pltpu.CompilerParams(vmem_limit_bytes=56 << 20),
        cost_estimate=pl.CostEstimate(
            flops=2 * full * tokens * model, bytes_accessed=2 * (tokens + full) * model, transcendentals=0
        ),
        name="dispatch",
    )(ids, gates, grad)


def slot_row(index, experts):
    source, rank = index >> 4, index & (MAIN - 1)
    main = jnp.where(rank < CAP, source * CAP + rank, experts * CAP + source * OC)
    left = index - experts * MAIN
    tail = experts * CAP + (left >> 1) * OC + 1 + (left & 1)
    return jnp.where(index < experts * MAIN, main, tail)


def travel_kernel(experts, rank_ref, own_ref, spill_ref, out_ref, place_ref, home_pick, spill_pick):
    @pl.when(pl.program_id(0) == 0)
    def _():
        for pick, first in ((home_pick, 0), (spill_pick, experts * CAP)):
            same = slot_row(iota(pick.shape, 0), experts) == first + iota(pick.shape, 1)
            pick[...] = jnp.where(same, 1.0, 0.0).astype(BF16)
        tokens, slots = place_ref.shape
        same = jnp.where(iota((tokens, tokens), 0) == iota((tokens, tokens), 1), 1.0, 0.0).astype(BF16)
        by_token = rows_dot(same, rank_ref[...].astype(BF16)).astype(BF16)
        full = experts * MAIN

        def named(shape):
            lane = iota(shape, 1)
            left = lane - full
            of = jnp.where(lane < full, lane >> 4, left >> 1)
            at = jnp.where(lane < full, lane & (MAIN - 1), MAIN + (left & 1))
            return of, at

        of, _ = named((experts, slots))
        widen = jnp.where(of == iota((experts, slots), 0), 1.0, 0.0).astype(BF16)
        _, at = named((tokens, slots))
        place_ref[...] = jnp.where(plain_dot(by_token, widen) == at.astype(F32), 1.0, 0.0).astype(BF16)

    out = plain_dot(home_pick[...], own_ref[...]) + plain_dot(spill_pick[...], spill_ref[...])
    out_ref[...] = out.astype(BF16)


def to_travel_order(rank, own, spill, experts):
    slots, columns = own.shape
    tokens = rank.shape[1]
    width = columns // 3
    home, rest = experts * CAP, experts * OC
    return pl.pallas_call(
        functools.partial(travel_kernel, experts),
        grid=(3,),
        in_specs=[
            whole((experts, tokens)),
            pl.BlockSpec((home, width), lambda step: (0, step)),
            pl.BlockSpec((rest, width), lambda step: (0, step)),
        ],
        out_specs=[pl.BlockSpec((slots, width), lambda step: (0, step)), whole((tokens, slots))],
        out_shape=[jax.ShapeDtypeStruct((slots, columns), BF16), jax.ShapeDtypeStruct((tokens, slots), BF16)],
        scratch_shapes=[pltpu.VMEM((slots, home), BF16), pltpu.VMEM((slots, rest), BF16)],
        compiler_params=pltpu.CompilerParams(vmem_limit_bytes=16 << 20),
        cost_estimate=pl.CostEstimate(
            flops=2 * slots * slots * columns, bytes_accessed=4 * slots * columns, transcendentals=0
        ),
        name="to_travel",
    )(rank, own, spill)


def slots_kernel(experts, rows_ref, out_ref, pick):
    @pl.when(pl.program_id(0) == 0)
    def _():
        same = slot_row(iota(pick.shape, 1), experts) == iota(pick.shape, 0)
        pick[...] = jnp.where(same, 1.0, 0.0).astype(BF16)

    out_ref[...] = plain_dot(pick[...], rows_ref[...]).astype(BF16)


def to_slot_order(rows, experts):
    slots, columns = rows.shape
    width = columns // 3
    return pl.pallas_call(
        functools.partial(slots_kernel, experts),
        grid=(3,),
        in_specs=[pl.BlockSpec((slots, width), lambda step: (0, step))],
        out_specs=pl.BlockSpec((slots, width), lambda step: (0, step)),
        out_shape=jax.ShapeDtypeStruct((slots, columns), BF16),
        scratch_shapes=[pltpu.VMEM((slots, slots), BF16)],
        compiler_params=pltpu.CompilerParams(vmem_limit_bytes=16 << 20),
        cost_estimate=pl.CostEstimate(
            flops=2 * slots * slots * columns, bytes_accessed=4 * slots * columns, transcendentals=0
        ),
        name="to_slots",
    )(rows)


def expert_kernel(experts, *refs):
    where_ref, arrived, pre_ref = refs[:3]
    downs, gate_ups = refs[3 : 3 + CUTS], refs[3 + CUTS : 3 + 2 * CUTS]
    grad_ref, back_ref = refs[3 + 2 * CUTS : 5 + 2 * CUTS]
    rows, tail, pieces, down, gate_up, total, stage, row_sem, down_sem, up_sem, out_sem = refs[5 + 2 * CUTS :]
    full, left = experts * MAIN, experts * 2
    hidden, width = down.shape[1:]

    def rows_copy(k):
        return pltpu.make_async_copy(
            arrived.at[:, columns(where_ref[k], width)], rows.at[k, pl.ds(0, full)], row_sem.at[k]
        )

    def out_copy(k, cut):
        return pltpu.make_async_copy(stage.at[k], back_ref.at[:, columns(cut, width)], out_sem.at[k])

    tail_copy = pltpu.make_async_copy(arrived.at[:, columns(CUTS, width)], tail, row_sem.at[CUTS])
    tail_copy.start()
    for k in range(CUTS):
        rows_copy(k).start()
        pltpu.make_async_copy(downs[k], down.at[k], down_sem.at[k]).start()
    for k in range(CUTS):
        pltpu.make_async_copy(gate_ups[k], gate_up.at[k], up_sem.at[k]).start()
    total[...] = jnp.zeros_like(total)
    order = piece_rows((full, full), 1, left)
    tail_copy.wait()
    pieces[...] = plain_dot(order, tail[...]).astype(BF16).reshape(CUTS, left, width)

    def first_product(k, carry):
        rows_copy(k).wait()
        pltpu.make_async_copy(downs[0], down.at[k], down_sem.at[k]).wait()
        rows[k, pl.ds(full, left)] = pieces[where_ref[k]]
        total[...] += rows_dot(rows[k], down[k])
        return carry

    lax.fori_loop(0, CUTS, first_product, 0)
    part = hidden // 3
    for n in range(3):
        own, other = pl.ds(n * part, part), pl.ds(hidden + n * part, part)
        hidden_cot = total[:, own]
        gate = pre_ref[:, own].astype(F32)
        up = pre_ref[:, other].astype(F32)
        sigma = jax.nn.sigmoid(gate)
        grad_ref[:, own] = (hidden_cot * up * sigma * (1.0 + gate * (1.0 - sigma))).astype(BF16)
        grad_ref[:, other] = (hidden_cot * gate * sigma).astype(BF16)

    def second_product(k, carry):
        pltpu.make_async_copy(gate_ups[0], gate_up.at[k], up_sem.at[k]).wait()
        back = rows_dot(grad_ref[...], gate_up[k]).astype(BF16)
        stage[k] = back[:full]
        pieces[where_ref[k]] = back[full:]
        out_copy(k, where_ref[k]).start()
        return carry

    lax.fori_loop(0, CUTS, second_product, 0)
    order = piece_rows((full, full), 0, left)
    stage[CUTS] = plain_dot(order, pieces[...].reshape(full, width)).astype(BF16)
    out_copy(CUTS, CUTS).start()

    def finish(k, carry):
        out_copy(k, where_ref[k]).wait()
        return carry

    lax.fori_loop(0, CUTS, finish, 0)
    out_copy(CUTS, CUTS).wait()


def expert_pass(where, arrived, pre_acts, downs, gate_ups):
    full, length = arrived.shape
    hidden, width = downs[0].shape
    slots, both = pre_acts.shape
    model = length - width
    experts = full // MAIN
    left = experts * 2
    return pl.pallas_call(
        functools.partial(expert_kernel, experts),
        in_specs=[pl.BlockSpec(memory_space=pltpu.SMEM), anywhere(), in_vmem()] + [anywhere()] * (2 * CUTS),
        out_specs=[in_vmem(), anywhere()],
        out_shape=[jax.ShapeDtypeStruct((slots, both), BF16), jax.ShapeDtypeStruct((full, length), BF16)],
        scratch_shapes=[
            pltpu.VMEM((CUTS, slots, width), BF16),
            pltpu.VMEM((full, width), BF16),
            pltpu.VMEM((CUTS, left, width), BF16),
            pltpu.VMEM((CUTS, hidden, width), BF16),
            pltpu.VMEM((CUTS, width, both), BF16),
            pltpu.VMEM((slots, hidden), F32),
            pltpu.VMEM((CUTS + 1, full, width), BF16),
            pltpu.SemaphoreType.DMA((CUTS + 1,)),
            pltpu.SemaphoreType.DMA((CUTS,)),
            pltpu.SemaphoreType.DMA((CUTS,)),
            pltpu.SemaphoreType.DMA((CUTS + 1,)),
        ],
        compiler_params=pltpu.CompilerParams(vmem_limit_bytes=56 << 20),
        cost_estimate=pl.CostEstimate(
            flops=6 * slots * hidden * model,
            bytes_accessed=2 * (2 * slots * model + 3 * hidden * model + 2 * slots * both),
            transcendentals=slots * hidden,
        ),
        name="experts",
    )(where, arrived, pre_acts, *downs, *gate_ups)


def combine_kernel(place_ref, main_ref, tail_ref, out_ref, pieces):
    step = pl.program_id(0)
    full, width = tail_ref.shape
    left = pieces.shape[1]

    @pl.when(step == 0)
    def _():
        order = piece_rows((full, full), 1, left)
        pieces[...] = plain_dot(order, tail_ref[...]).astype(BF16).reshape(CUTS, left, width)

    for half in range(2):
        part = pl.ds(half * width, width)
        total = plain_dot(place_ref[:, :full], main_ref[:, part])
        total += plain_dot(place_ref[:, full:], pieces[2 * step + half])
        out_ref[:, part] = total.astype(BF16)


def combine(place, returned):
    full, length = returned.shape
    tokens, slots = place.shape
    width = length // (CUTS + 1)
    model = width * CUTS
    left = slots - full
    return pl.pallas_call(
        combine_kernel,
        grid=(CUTS // 2,),
        in_specs=[
            whole((tokens, slots)),
            pl.BlockSpec((full, 2 * width), lambda step: (0, step)),
            pl.BlockSpec((full, width), lambda step: (0, CUTS)),
        ],
        out_specs=pl.BlockSpec((tokens, 2 * width), lambda step: (0, step)),
        out_shape=jax.ShapeDtypeStruct((tokens, model), BF16),
        scratch_shapes=[pltpu.VMEM((CUTS, left, width), BF16)],
        compiler_params=pltpu.CompilerParams(vmem_limit_bytes=56 << 20),
        cost_estimate=pl.CostEstimate(
            flops=2 * slots * tokens * model, bytes_accessed=2 * (tokens + slots) * model, transcendentals=0
        ),
        name="combine",
    )(place, returned, returned)


def along_dp(shard, target):
    return lax.ppermute(shard, "dp", [(i, target(i)) for i in range(lax.axis_size("dp"))])


def gathered(shard):
    count = lax.axis_size("dp")
    core = lax.axis_index("dp") & 1
    below = along_dp(shard, lambda i: (i + 2) % count)
    above = along_dp(shard, lambda i: (i - 2) % count)
    across = along_dp(jnp.where(core == 0, below, above), lambda i: (i + 2 - 4 * (i & 1)) % count)
    held = [shard, below, above, across]
    return held + [along_dp(part, lambda i: i ^ 1) for part in held]


def shard_places():
    count = lax.axis_size("dp")
    me = lax.axis_index("dp")
    steps = jnp.array([0, -2, 2, 4], jnp.int32)
    return jnp.concatenate([(me + steps + count) % count, ((me ^ 1) + steps + count) % count]).astype(jnp.int32)


def moved(rows, offset, sign):
    replicas = lax.axis_size("dp")
    for bit in range(replicas.bit_length() - 1):
        by = sign * (1 << bit)
        shifted = lax.ppermute(rows, "dp", [(i, (i + by) % replicas) for i in range(replicas)])
        rows = jnp.where(offset >> bit & 1 == 1, shifted, rows)
    return rows


def exchange(rows, experts):
    blocks = rows.reshape(experts, MAIN, rows.shape[1])
    return lax.all_to_all(blocks, "expert", split_axis=0, concat_axis=0, tiled=True).reshape(rows.shape)


def body(out_grad, route_gates, expert_ids, partner_offset, saved_pre, down_weight, gate_up_weight):
    experts = lax.axis_size("expert")
    home = experts * CAP
    offset = partner_offset[0]
    own_pre = saved_pre[0, 0]
    sent, rank = dispatch(expert_ids.T, route_gates.T, out_grad, experts)
    arrived = exchange(sent, experts)
    downs, gate_ups = gathered(down_weight[0]), gathered(gate_up_weight[0])
    spill_pre = moved(own_pre[home:], offset, -1)
    pre_acts, place = to_travel_order(rank, own_pre, spill_pre, experts)
    travel_grad, back = expert_pass(shard_places(), arrived, pre_acts, downs, gate_ups)
    returned = exchange(back, experts)
    by_slot = to_slot_order(travel_grad, experts)
    spill_grad = moved(by_slot[home:], offset, 1)
    hidden_grad = lax.dynamic_update_slice(by_slot, spill_grad, (home, 0))
    token_grad = combine(place, returned)
    return token_grad, hidden_grad.reshape(saved_pre.shape)


def solution(mesh):
    placed = (
        P(("dp", "expert"), None),
        P(("dp", "expert"), None),
        P(("dp", "expert"), None),
        P("expert"),
        P("dp", "expert", None, None),
        P("expert", None, "dp"),
        P("expert", "dp", None),
    )
    return jax.shard_map(
        body,
        mesh=mesh,
        in_specs=placed,
        out_specs=(P(("dp", "expert"), None), P("dp", "expert", None, None)),
        check_vma=False,
    )
```

time: 550 us -> 271 us (0.49)
  blocking collectives: 151 us -> 0 us
  local copies, waits for them, and re-layouts: 57.4 us -> 4.79 us
  other arithmetic: 58.7 us -> 7.24 us
  Pallas kernels: 0 us -> 39.8 us
  waiting for transfers between devices: 214 us -> 177 us
  matrix products: 20.3 us -> 0 us
  between operations: 15.3 us -> 1.49 us
  starting transfers between devices: 28.4 us -> 39.6 us
    all_to_all x1 -> x0, blocking collectives: 151 us -> none  [body(): lax.all_to_all(outgoing, 'expert', split_axis=0, concat_axis=0, tiled=True)]
    all_to_all x1 -> x2, waiting for transfers between devices: 139 us -> 81.9 us  [exchange(): lax.all_to_all(blocks, 'expert', split_axis=0, concat_axis=0, tiled=True)]
    pallas_call x0 -> x5, Pallas kernels: none -> 39.8 us  [the longest x1 21.9 us: expert_pass(): pl.pallas_call(functools.partial(expert_kernel, experts), in_specs=[pl.Bl...]
    scatter-add x1 -> x0, other arithmetic: 27.9 us -> none  [body(): jnp.zeros((tok_rows, model_width), jnp.float32).at[token_of].add(live_rows)]
    ppermute x6 -> x20, waiting for transfers between devices: 73.8 us -> 95.2 us  [the longest x6 62.4 us: moved(): lax.ppermute(rows, 'dp', [(i, (i + by) % replicas) for i in range(replica...]
    dot_general x2 -> x0, matrix products: 20.3 us -> none  [the longest x1 10.8 us: body(): jnp.einsum('rc,nc->rn', hidden_grad, lax.all_gather(gate_up_weight, 'dp',...]
    convert_element_type x2 -> x0, local copies, waits for them, and re-layouts: 17.4 us -> none  [the longest x1 8.73 us: body(): out_grad[token_of].astype(jnp.float32)]
    all_to_all x1 -> x2, starting transfers between devices: 5.2 us -> 20.4 us  [exchange(): lax.all_to_all(blocks, 'expert', split_axis=0, concat_axis=0, tiled=True)]
  transfers between devices with their start and end apart: 9 -> 22, of which waited for: 7 -> 12; matrix products, arithmetic and copies ran while one was open for 13% -> 3% of each run, Pallas kernels for 0% -> 2%
where the time goes in v2:
time: 271 us; the launch traced here: 270 us
  waiting for transfers between devices  177 us (65%)
  Pallas kernels  39.8 us (15%)
  starting transfers between devices  39.6 us (15%)
  other arithmetic  7.24 us (3%)
  local copies, waits for them, and re-layouts  4.79 us (2%)
    all_to_all x2, waiting for transfers between devices, exchange(): lax.all_to_all(blocks, 'expert', split_axis=0, concat_axis=0, tiled=True)  81.9 us
    ppermute x6, waiting for transfers between devices, moved(): lax.ppermute(rows, 'dp', [(i, (i + by) % replicas) for i in range(replica...  62.4 us
    ppermute x14, waiting for transfers between devices, along_dp(): lax.ppermute(shard, 'dp', [(i, target(i)) for i in range(lax.axis_size('d...  32.9 us
    pallas_call x1, Pallas kernels, expert_pass(): pl.pallas_call(functools.partial(expert_kernel, experts), in_specs=[pl.Bl...  21.9 us
    all_to_all x2, starting transfers between devices, exchange(): lax.all_to_all(blocks, 'expert', split_axis=0, concat_axis=0, tiled=True)  20.4 us
    ppermute x14, starting transfers between devices, along_dp(): lax.ppermute(shard, 'dp', [(i, target(i)) for i in range(lax.axis_size('d...  11.3 us
    ppermute x6, starting transfers between devices, moved(): lax.ppermute(rows, 'dp', [(i, (i + by) % replicas) for i in range(replica...  7.9 us
    pallas_call x1, Pallas kernels, dispatch(): pl.pallas_call(functools.partial(dispatch_kernel, experts), in_specs=[in_...  6.41 us
  transfers between devices with their start and end apart: 22, of which 12 were waited for; matrix products, arithmetic and copies ran while one was open for 3% of the time, Pallas kernels for 2%

profile of v2, /device:TPU:35, one launch (start us, length us, event | category | flops | bytes accessed | tf_op | source)
XLA Modules:
  0.0 270.1 jit_solution(16817478722890580133)
XLA Ops:
  0.6 6.4 %dispatch.1 = (bf16[512,4608]{1,0:T(8,128)(2,1)}, f32[32,192]{1,0:T(8,128)}) custom-call(s32[8,192]{1,0:T(8,128)} %bitcast.27, f32[8,192]{1,0:T(8,128)} %bitcast.28, bf16[192,4096]{1,0:T(8,128)(2,1)} %grad_ref.1), custom_call_target="tpu_custom_call" | custom-call | flops 805306368 | bytes 5767168 | tf_op jit(solution)/shard_map/dispatch/pallas_call | solution.py:114
  7.1 11.0 %all-to-all-start = ((bf16[32,16,4608]{2,1,0:T(8,128)(2,1)}), bf16[32,16,4608]{2,1,0:T(8,128)(2,1)}, u32[]{:S(2)}, u32[]{:S(2)}) async-start(bf16[32,16,4608]{2,1,0:T(8,128)(2,1)} %bitcast.20), calls=%async_computation | async-start | bytes 9437184 | tf_op jit(solution)/shard_map/all_to_all | solution.py:401
  18.1 1.3 collective-permute-start.10
  19.3 0.3 collective-permute-start.11
  19.6 1.2 collective-permute-start.3
  20.8 0.3 collective-permute-start.4
  21.1 0.7 slice_bitcast_fusion
  21.8 2.4 collective-permute-start
  24.2 28.9 %collective-permute-done.10.refs_12_ = bf16[512,1536]{1,0:T(8,128)(2,1)S(1)} collective-permute-done((bf16[512,1536]{1,0:T(8,128)(2,1)}, bf16[512,1536]{1,0:T(8,128)(2,1)S(1)}, u32[]{:S(2)}, u32[]{:S(2)}) %collective-permute-start.10) | collective-permute-done | bytes 1572896 | tf_op jit(solution)/shard_map/ppermute | solution.py:370
  53.1 0.9 collective-permute-done.11.refs_13_
  54.0 1.6 broadcast_select_fusion
  55.6 1.2 collective-permute-start.12
  56.8 3.2 %collective-permute-start.6 = (bf16[768,512]{1,0:T(8,128)(2,1)S(1)}, bf16[768,512]{1,0:T(8,128)(2,1)S(1)}, u32[]{:S(2)}, u32[]{:S(2)}) collective-permute-start(bf16[768,512]{1,0:T(8,128)(2,1)S(1)} %bitcast.26), channel_id=1, source_target_pairs={{0,32},{32,0},{64,96},{96,64},{128,160},{160,128},{192,224},{224,1... | collective-permute-start | bytes 2359304 | tf_op jit(solution)/shard_map/ppermute | solution.py:370
  60.6 20.7 %collective-permute-done = bf16[96,1536]{1,0:T(8,128)(2,1)} collective-permute-done((bf16[96,1536]{1,0:T(8,128)(2,1)}, bf16[96,1536]{1,0:T(8,128)(2,1)}, u32[]{:S(2)}, u32[]{:S(2)}) %collective-permute-start) | collective-permute-done | bytes 294944 | tf_op jit(solution)/shard_map/ppermute | solution.py:394
  81.3 1.0 broadcast_select_fusion.3
  82.3 0.3 collective-permute-start.1
  82.7 1.2 broadcast_select_fusion.1
  83.9 2.7 %collective-permute-start.5 = (bf16[768,512]{1,0:T(8,128)(2,1)S(1)}, bf16[768,512]{1,0:T(8,128)(2,1)S(1)}, u32[]{:S(2)}, u32[]{:S(2)}) collective-permute-start(bf16[768,512]{1,0:T(8,128)(2,1)S(1)} %broadcast_select_fusion.1), channel_id=1, source_target_pairs={{0,64},{32,224},{64,128},{96,32},{128,192},{160,96},{192,0},{224,1... | collective-permute-start | bytes 2359304 | tf_op jit(solution)/shard_map/ppermute | solution.py:370
  86.6 15.8 %collective-permute-done.1 = bf16[96,1536]{1,0:T(8,128)(2,1)S(1)} collective-permute-done((bf16[96,1536]{1,0:T(8,128)(2,1)S(1)}, bf16[96,1536]{1,0:T(8,128)(2,1)S(1)}, u32[]{:S(2)}, u32[]{:S(2)}) %collective-permute-start.1) | collective-permute-done | bytes 294944 | tf_op jit(solution)/shard_map/ppermute | solution.py:394
  102.5 1.5 collective-permute-start.2
  103.9 10.7 %collective-permute-done.2 = bf16[96,1536]{1,0:T(8,128)(2,1)S(1)} collective-permute-done((bf16[96,1536]{1,0:T(8,128)(2,1)S(1)}, bf16[96,1536]{1,0:T(8,128)(2,1)S(1)}, u32[]{:S(2)}, u32[]{:S(2)}) %collective-permute-start.2) | collective-permute-done | bytes 294944 | tf_op jit(solution)/shard_map/ppermute | solution.py:394
  114.7 0.6 collective-permute-start.14
  115.4 0.2 copy-done.11
  115.6 0.5 copy-done.12
  116.2 0.2 collective-permute-start.16
  116.3 0.3 collective-permute-start.9
  116.7 0.6 pad_add_fusion.refs_0_
  117.3 1.0 broadcast_select_fusion.6.spill_ref
  118.3 2.7 to_travel.1
  121.0 0.7 copy-done
  121.7 1.2 copy-done.3
  122.9 0.5 collective-permute-done.14.refs_16_
  123.4 0.3 copy-done.13
  123.8 0.2 collective-permute-done.15.refs_17_
  124.0 2.2 collective-permute-done.16.refs_18_
  126.3 21.9 %experts.1 = (bf16[576,1536]{1,0:T(8,128)(2,1)}, bf16[512,4608]{1,0:T(8,128)(2,1)}) custom-call(s32[8]{0:T(128)} %pad_add_fusion.refs_0_, bf16[512,4608]{1,0:T(8,128)(2,1)} %bitcast.8.refs_1_, bf16[576,1536]{1,0:T(8,128)(2,1)} %copy-done.3, bf16[768,512]{1,0:T(8,128)(2,1)} %bitcast.25, bf16[768,512]{1,0:T(8,128)(2,1)} %collective-permute-done.3.refs_4_, ...), custom_call_target="tpu_custom_call" | custom-call | flops 10871635968 | bytes 31850496 | tf_op jit(solution)/shard_map/experts/pallas_call | solution.py:299
  148.2 9.4 %all-to-all-start.1 = ((bf16[32,16,4608]{2,1,0:T(8,128)(2,1)}), bf16[32,16,4608]{2,1,0:T(8,128)(2,1)}, u32[]{:S(2)}, u32[]{:S(2)}) async-start(bf16[32,16,4608]{2,1,0:T(8,128)(2,1)} %bitcast.21), calls=%async_computation.1 | async-start | bytes 9437184 | tf_op jit(solution)/shard_map/all_to_all | solution.py:401
  157.7 3.1 %to_slots.1 = bf16[576,1536]{1,0:T(8,128)(2,1)} custom-call(bf16[576,1536]{1,0:T(8,128)(2,1)S(1)} %copy-done.2), custom_call_target="tpu_custom_call" | custom-call | flops 1019215872 | bytes 3538944 | tf_op jit(solution)/shard_map/to_slots/pallas_call | solution.py:210
  160.8 1.0 slice.12
  161.8 3.7 %collective-permute-done.17 = bf16[96,1536]{1,0:T(8,128)(2,1)S(1)} collective-permute-done((bf16[96,1536]{1,0:T(8,128)(2,1)S(1)}, bf16[96,1536]{1,0:T(8,128)(2,1)S(1)}, u32[]{:S(2)}, u32[]{:S(2)}) %collective-permute-start.17) | collective-permute-done | bytes 294944 | tf_op jit(solution)/shard_map/ppermute | solution.py:394
  165.5 1.0 broadcast_select_fusion.2
  166.5 2.1 collective-permute-start.18
  168.6 5.5 %collective-permute-done.18 = bf16[96,1536]{1,0:T(8,128)(2,1)S(1)} collective-permute-done((bf16[96,1536]{1,0:T(8,128)(2,1)S(1)}, bf16[96,1536]{1,0:T(8,128)(2,1)S(1)}, u32[]{:S(2)}, u32[]{:S(2)}) %collective-permute-start.18) | collective-permute-done | bytes 294944 | tf_op jit(solution)/shard_map/ppermute | solution.py:394
  174.1 1.6 collective-permute-start.19
  175.7 6.1 %collective-permute-done.19 = bf16[96,1536]{1,0:T(8,128)(2,1)S(1)} collective-permute-done((bf16[96,1536]{1,0:T(8,128)(2,1)S(1)}, bf16[96,1536]{1,0:T(8,128)(2,1)S(1)}, u32[]{:S(2)}, u32[]{:S(2)}) %collective-permute-start.19) | collective-permute-done | bytes 294944 | tf_op jit(solution)/shard_map/ppermute | solution.py:394
  181.8 0.8 bitcast_dynamic-update-slice_fusion
  182.5 81.9 %all-to-all-done.1 = bf16[32,16,4608]{2,1,0:T(8,128)(2,1)} async-done(((bf16[32,16,4608]{2,1,0:T(8,128)(2,1)}), bf16[32,16,4608]{2,1,0:T(8,128)(2,1)}, u32[]{:S(2)}, u32[]{:S(2)}) %all-to-all-start.1) | async-done | bytes 4718624 | tf_op jit(solution)/shard_map/all_to_all | solution.py:401
  264.5 5.6 %combine.1 = bf16[192,4096]{1,0:T(8,128)(2,1)} custom-call(bf16[192,576]{1,0:T(8,128)(2,1)} %copy-done, bf16[512,4608]{1,0:T(8,128)(2,1)} %bitcast.12.main_ref.tail_ref, bf16[512,4608]{1,0:T(8,128)(2,1)} %bitcast.12.main_ref.tail_ref), custom_call_target="tpu_custom_call" | custom-call | flops 905969664 | bytes 6291456 | tf_op jit(solution)/shard_map/combine/pallas_call | solution.py:350
  (41 shorter events, 0.3 us)
Async XLA Ops:
  7.0 14.0 %copy-start.1 = (bf16[1,1,576,1536]{3,2,1,0:T(8,128)(2,1)S(1)}, bf16[1,1,576,1536]{3,2,1,0:T(8,128)(2,1)}, u32[]{:S(2)}) copy-start(bf16[1,1,576,1536]{3,2,1,0:T(8,128)(2,1)} %param.12) | copy-start | bytes 5308420
  7.1 119.2 %all-to-all-start = ((bf16[32,16,4608]{2,1,0:T(8,128)(2,1)}), bf16[32,16,4608]{2,1,0:T(8,128)(2,1)}, u32[]{:S(2)}, u32[]{:S(2)}) async-start(bf16[32,16,4608]{2,1,0:T(8,128)(2,1)} %bitcast.20), calls=%async_computation | async-start | bytes 9437184 | tf_op jit(solution)/shard_map/all_to_all | solution.py:401
  18.1 35.0 %collective-permute-start.10 = (bf16[512,1536]{1,0:T(8,128)(2,1)}, bf16[512,1536]{1,0:T(8,128)(2,1)S(1)}, u32[]{:S(2)}, u32[]{:S(2)}) collective-permute-start(bf16[512,1536]{1,0:T(8,128)(2,1)} %bitcast.10.refs_11_), channel_id=1, source_target_pairs={{0,64},{32,96},{64,128},{96,160},{128,192},{160,224},{192,0},{224,... | collective-permute-start | bytes 4718600 | tf_op jit(solution)/shard_map/ppermute | solution.py:370
  19.3 34.7 %collective-permute-start.11 = (bf16[512,1536]{1,0:T(8,128)(2,1)}, bf16[512,1536]{1,0:T(8,128)(2,1)}, u32[]{:S(2)}, u32[]{:S(2)}) collective-permute-start(bf16[512,1536]{1,0:T(8,128)(2,1)} %bitcast.10.refs_11_), channel_id=1, source_target_pairs={{0,192},{32,224},{64,0},{96,32},{128,64},{160,96},{192,128},{224,1... | collective-permute-start | bytes 4718600 | tf_op jit(solution)/shard_map/ppermute | solution.py:370
  19.6 63.0 %collective-permute-start.3 = (bf16[768,512]{1,0:T(8,128)(2,1)}, bf16[768,512]{1,0:T(8,128)(2,1)}, u32[]{:S(2)}, u32[]{:S(2)}) collective-permute-start(bf16[768,512]{1,0:T(8,128)(2,1)} %bitcast.23), channel_id=1, source_target_pairs={{0,64},{32,96},{64,128},{96,160},{128,192},{160,224},{192,0},{224,... | collective-permute-start | bytes 2359304 | tf_op jit(solution)/shard_map/ppermute | solution.py:370
  20.8 61.8 %collective-permute-start.4 = (bf16[768,512]{1,0:T(8,128)(2,1)}, bf16[768,512]{1,0:T(8,128)(2,1)}, u32[]{:S(2)}, u32[]{:S(2)}) collective-permute-start(bf16[768,512]{1,0:T(8,128)(2,1)} %bitcast.24), channel_id=1, source_target_pairs={{0,192},{32,224},{64,0},{96,32},{128,64},{160,96},{192,128},{224,1... | collective-permute-start | bytes 2359304 | tf_op jit(solution)/shard_map/ppermute | solution.py:370
  21.8 59.5 %collective-permute-start = (bf16[96,1536]{1,0:T(8,128)(2,1)}, bf16[96,1536]{1,0:T(8,128)(2,1)}, u32[]{:S(2)}, u32[]{:S(2)}) collective-permute-start(bf16[96,1536]{1,0:T(8,128)(2,1)} %slice_bitcast_fusion), channel_id=1, source_target_pairs={{0,224},{32,0},{64,32},{96,64},{128,96},{160,128},{192,160},{224,1... | collective-permute-start | bytes 884744 | tf_op jit(solution)/shard_map/ppermute | solution.py:394
  24.2 32.6 %copy-start.9 = (bf16[1,768,512]{2,1,0:T(8,128)(2,1)S(1)}, bf16[1,768,512]{2,1,0:T(8,128)(2,1)}, u32[]{:S(2)}) copy-start(bf16[1,768,512]{2,1,0:T(8,128)(2,1)} %param.13) | copy-start | bytes 2359300
  53.1 61.6 %copy-start.5 = (bf16[512,1536]{1,0:T(8,128)(2,1)}, bf16[512,1536]{1,0:T(8,128)(2,1)S(1)}, u32[]{:S(2)}) copy-start(bf16[512,1536]{1,0:T(8,128)(2,1)S(1)} %collective-permute-done.10.refs_12_) | copy-start | bytes 4718596
  55.6 59.8 %collective-permute-start.12 = (bf16[512,1536]{1,0:T(8,128)(2,1)S(1)}, bf16[512,1536]{1,0:T(8,128)(2,1)}, u32[]{:S(2)}, u32[]{:S(2)}) collective-permute-start(bf16[512,1536]{1,0:T(8,128)(2,1)S(1)} %broadcast_select_fusion), channel_id=1, source_target_pairs={{0,64},{32,224},{64,128},{96,32},{128,192},{160,96},{192,0},{224,1... | collective-permute-start | bytes 4718600 | tf_op jit(solution)/shard_map/ppermute | solution.py:370
  56.8 47.1 %collective-permute-start.6 = (bf16[768,512]{1,0:T(8,128)(2,1)S(1)}, bf16[768,512]{1,0:T(8,128)(2,1)S(1)}, u32[]{:S(2)}, u32[]{:S(2)}) collective-permute-start(bf16[768,512]{1,0:T(8,128)(2,1)S(1)} %bitcast.26), channel_id=1, source_target_pairs={{0,32},{32,0},{64,96},{96,64},{128,160},{160,128},{192,224},{224,1... | collective-permute-start | bytes 2359304 | tf_op jit(solution)/shard_map/ppermute | solution.py:370
  82.3 34.4 %copy-start.8 = (s32[4]{0:T(128)S(1)}, s32[4]{0:T(128)}, u32[]{:S(2)}) copy-start(s32[4]{0:T(128)} %constant.48.clone) | copy-start | bytes 52
  82.3 36.0 %copy-start.4 = (f32[32,192]{1,0:T(8,128)S(1)}, f32[32,192]{1,0:T(8,128)}, u32[]{:S(2)}) copy-start(f32[32,192]{1,0:T(8,128)} %get-tuple-element.8.rank_ref) | copy-start | bytes 73732
  82.3 20.1 %collective-permute-start.1 = (bf16[96,1536]{1,0:T(8,128)(2,1)S(1)}, bf16[96,1536]{1,0:T(8,128)(2,1)S(1)}, u32[]{:S(2)}, u32[]{:S(2)}) collective-permute-start(bf16[96,1536]{1,0:T(8,128)(2,1)S(1)} %broadcast_select_fusion.3), channel_id=1, source_target_pairs={{0,192},{32,224},{64,0},{96,32},{128,64},{160,96},{192,128},{224,1... | collective-permute-start | bytes 884744 | tf_op jit(solution)/shard_map/ppermute | solution.py:394
  83.9 30.8 %collective-permute-start.5 = (bf16[768,512]{1,0:T(8,128)(2,1)S(1)}, bf16[768,512]{1,0:T(8,128)(2,1)S(1)}, u32[]{:S(2)}, u32[]{:S(2)}) collective-permute-start(bf16[768,512]{1,0:T(8,128)(2,1)S(1)} %broadcast_select_fusion.1), channel_id=1, source_target_pairs={{0,64},{32,224},{64,128},{96,32},{128,192},{160,96},{192,0},{224,1... | collective-permute-start | bytes 2359304 | tf_op jit(solution)/shard_map/ppermute | solution.py:370
  86.6 28.6 %collective-permute-start.7 = (bf16[768,512]{1,0:T(8,128)(2,1)}, bf16[768,512]{1,0:T(8,128)(2,1)S(1)}, u32[]{:S(2)}, u32[]{:S(2)}) collective-permute-start(bf16[768,512]{1,0:T(8,128)(2,1)} %collective-permute-done.3.refs_4_), channel_id=1, source_target_pairs={{0,32},{32,0},{64,96},{96,64},{128,160},{160,128},{192,224},{224,1... | collective-permute-start | bytes 2359304 | tf_op jit(solution)/shard_map/ppermute | solution.py:370
  102.5 12.9 %copy-start.6 = (bf16[96,1536]{1,0:T(8,128)(2,1)}, bf16[96,1536]{1,0:T(8,128)(2,1)S(1)}, u32[]{:S(2)}) copy-start(bf16[96,1536]{1,0:T(8,128)(2,1)S(1)} %broadcast_select_fusion.5) | copy-start | bytes 884740
  102.5 12.2 %collective-permute-start.2 = (bf16[96,1536]{1,0:T(8,128)(2,1)S(1)}, bf16[96,1536]{1,0:T(8,128)(2,1)S(1)}, u32[]{:S(2)}, u32[]{:S(2)}) collective-permute-start(bf16[96,1536]{1,0:T(8,128)(2,1)S(1)} %broadcast_select_fusion.5), channel_id=1, source_target_pairs={{0,128},{32,160},{64,192},{96,224},{128,0},{160,32},{192,64},{224,... | collective-permute-start | bytes 884744 | tf_op jit(solution)/shard_map/ppermute | solution.py:394
  103.9 11.4 %copy-start.10 = (bf16[768,512]{1,0:T(8,128)(2,1)}, bf16[768,512]{1,0:T(8,128)(2,1)S(1)}, u32[]{:S(2)}) copy-start(bf16[768,512]{1,0:T(8,128)(2,1)S(1)} %collective-permute-done.6.refs_7_) | copy-start | bytes 2359300
  103.9 12.4 %collective-permute-start.8 = (bf16[768,512]{1,0:T(8,128)(2,1)}, bf16[768,512]{1,0:T(8,128)(2,1)}, u32[]{:S(2)}, u32[]{:S(2)}) collective-permute-start(bf16[768,512]{1,0:T(8,128)(2,1)} %collective-permute-done.4.refs_5_), channel_id=1, source_target_pairs={{0,32},{32,0},{64,96},{96,64},{128,160},{160,128},{192,224},{224,1... | collective-permute-start | bytes 2359304 | tf_op jit(solution)/shard_map/ppermute | solution.py:370
  114.6 0.7 copy-start.7
  114.6 8.3 %collective-permute-start.13 = (bf16[512,1536]{1,0:T(8,128)(2,1)}, bf16[512,1536]{1,0:T(8,128)(2,1)}, u32[]{:S(2)}, u32[]{:S(2)}) collective-permute-start(bf16[512,1536]{1,0:T(8,128)(2,1)} %bitcast.10.refs_11_), channel_id=1, source_target_pairs={{0,32},{32,0},{64,96},{96,64},{128,160},{160,128},{192,224},{224,1... | collective-permute-start | bytes 4718600 | tf_op jit(solution)/shard_map/ppermute | solution.py:370
  114.7 1.0 copy-start.11
  114.7 8.8 %collective-permute-start.14 = (bf16[512,1536]{1,0:T(8,128)(2,1)S(1)}, bf16[512,1536]{1,0:T(8,128)(2,1)}, u32[]{:S(2)}, u32[]{:S(2)}) collective-permute-start(bf16[512,1536]{1,0:T(8,128)(2,1)S(1)} %collective-permute-done.10.refs_12_), channel_id=1, source_target_pairs={{0,32},{32,0},{64,96},{96,64},{128,160},{160,128},{192,224},{224,1... | collective-permute-start | bytes 4718600 | tf_op jit(solution)/shard_map/ppermute | solution.py:370
  115.2 0.9 copy-start.12
  115.3 8.8 %collective-permute-start.15 = (bf16[512,1536]{1,0:T(8,128)(2,1)}, bf16[512,1536]{1,0:T(8,128)(2,1)}, u32[]{:S(2)}, u32[]{:S(2)}) collective-permute-start(bf16[512,1536]{1,0:T(8,128)(2,1)} %collective-permute-done.11.refs_13_), channel_id=1, source_target_pairs={{0,32},{32,0},{64,96},{96,64},{128,160},{160,128},{192,224},{224,1... | collective-permute-start | bytes 4718600 | tf_op jit(solution)/shard_map/ppermute | solution.py:370
  116.2 10.1 %collective-permute-start.16 = (bf16[512,1536]{1,0:T(8,128)(2,1)}, bf16[512,1536]{1,0:T(8,128)(2,1)}, u32[]{:S(2)}, u32[]{:S(2)}) collective-permute-start(bf16[512,1536]{1,0:T(8,128)(2,1)} %collective-permute-done.12.refs_14_), channel_id=1, source_target_pairs={{0,32},{32,0},{64,96},{96,64},{128,160},{160,128},{192,224},{224,1... | collective-permute-start | bytes 4718600 | tf_op jit(solution)/shard_map/ppermute | solution.py:370
  116.3 6.6 %collective-permute-start.9 = (bf16[768,512]{1,0:T(8,128)(2,1)}, bf16[768,512]{1,0:T(8,128)(2,1)S(1)}, u32[]{:S(2)}, u32[]{:S(2)}) collective-permute-start(bf16[768,512]{1,0:T(8,128)(2,1)} %copy-done.11), channel_id=1, source_target_pairs={{0,32},{32,0},{64,96},{96,64},{128,160},{160,128},{192,224},{224,1... | collective-permute-start | bytes 2359304 | tf_op jit(solution)/shard_map/ppermute | solution.py:370
  121.0 0.7 copy-start
  121.7 1.2 copy-start.3
  122.9 0.9 copy-start.13
  148.2 9.4 %copy-start.2 = (bf16[576,1536]{1,0:T(8,128)(2,1)S(1)}, bf16[576,1536]{1,0:T(8,128)(2,1)}, u32[]{:S(2)}) copy-start(bf16[576,1536]{1,0:T(8,128)(2,1)} %get-tuple-element.13.rows_ref) | copy-start | bytes 5308420
  148.2 116.2 %all-to-all-start.1 = ((bf16[32,16,4608]{2,1,0:T(8,128)(2,1)}), bf16[32,16,4608]{2,1,0:T(8,128)(2,1)}, u32[]{:S(2)}, u32[]{:S(2)}) async-start(bf16[32,16,4608]{2,1,0:T(8,128)(2,1)} %bitcast.21), calls=%async_computation.1 | async-start | bytes 9437184 | tf_op jit(solution)/shard_map/all_to_all | solution.py:401
  161.8 3.7 %collective-permute-start.17 = (bf16[96,1536]{1,0:T(8,128)(2,1)S(1)}, bf16[96,1536]{1,0:T(8,128)(2,1)S(1)}, u32[]{:S(2)}, u32[]{:S(2)}) collective-permute-start(bf16[96,1536]{1,0:T(8,128)(2,1)S(1)} %slice.12), channel_id=1, source_target_pairs={{0,32},{32,64},{64,96},{96,128},{128,160},{160,192},{192,224},{224... | collective-permute-start | bytes 884744 | tf_op jit(solution)/shard_map/ppermute | solution.py:394
  166.5 7.6 %collective-permute-start.18 = (bf16[96,1536]{1,0:T(8,128)(2,1)S(1)}, bf16[96,1536]{1,0:T(8,128)(2,1)S(1)}, u32[]{:S(2)}, u32[]{:S(2)}) collective-permute-start(bf16[96,1536]{1,0:T(8,128)(2,1)S(1)} %broadcast_select_fusion.2), channel_id=1, source_target_pairs={{0,64},{32,96},{64,128},{96,160},{128,192},{160,224},{192,0},{224,... | collective-permute-start | bytes 884744 | tf_op jit(solution)/shard_map/ppermute | solution.py:394
  174.1 7.7 %collective-permute-start.19 = (bf16[96,1536]{1,0:T(8,128)(2,1)S(1)}, bf16[96,1536]{1,0:T(8,128)(2,1)S(1)}, u32[]{:S(2)}, u32[]{:S(2)}) collective-permute-start(bf16[96,1536]{1,0:T(8,128)(2,1)S(1)} %broadcast_select_fusion.4), channel_id=1, source_target_pairs={{0,128},{32,160},{64,192},{96,224},{128,0},{160,32},{192,64},{224,... | collective-permute-start | bytes 884744 | tf_op jit(solution)/shard_map/ppermute | solution.py:394

commit v3 on v2

--- a/solution.py
+++ b/solution.py
@@ -50,11 +50,20 @@
 
 
 def dispatch_kernel(
-    experts, ids_ref, gates_ref, grad_ref, send_ref, rank_ref, main_pick, tail_pick, main_gate, tail_gate, stage, pieces, sems
+    experts, ids_ref, gates_ref, grad_ref, send_ref, rank_ref, main_pick, tail_pick, main_gate, tail_gate, grads, stage, pieces, grad_sem, sems
 ):
     choices, tokens = ids_ref.shape
     full, left = experts * MAIN, experts * 2
-    width = grad_ref.shape[1] // CUTS
+    width = grads.shape[2]
+
+    def grad_copy(cut):
+        return pltpu.make_async_copy(grad_ref.at[:, pl.ds(cut * width, width)], grads.at[cut], grad_sem.at[cut])
+
+    def send_copy(cut):
+        return pltpu.make_async_copy(stage.at[cut], send_ref.at[:, pl.ds(cut * width, width)], sems.at[cut])
+
+    for cut in range(CUTS):
+        grad_copy(cut).start()
     expert = iota((experts, tokens), 0)
     hit = jnp.zeros((experts, tokens), F32)
     gate = jnp.zeros((experts, tokens), F32)
@@ -82,23 +91,16 @@
             by_row = rows_by(gate, left)
             scale_ref[...] = jnp.sum(jnp.where(pick_ref[...].astype(F32) > 0.0, by_row, 0.0), axis=1, keepdims=True)
 
-    def one_cut(cut, carry):
-        grad = grad_ref[:, columns(cut, width)]
-        picked = plain_dot(main_pick[...], grad) * main_gate[...]
-        stage[cut] = picked.astype(BF16)
-        pltpu.make_async_copy(stage.at[cut], send_ref.at[:, columns(cut, width)], sems.at[cut]).start()
+    for cut in range(CUTS):
+        grad_copy(cut).wait()
+        grad = grads[cut]
+        stage[cut] = (plain_dot(main_pick[...], grad) * main_gate[...]).astype(BF16)
+        send_copy(cut).start()
         pieces[cut] = (plain_dot(tail_pick[...], grad) * tail_gate[...]).astype(BF16)
-        return carry
-
-    lax.fori_loop(0, CUTS, one_cut, 0)
     stage[CUTS] = plain_dot(piece_rows((full, full), 0, left), pieces[...].reshape(full, width)).astype(BF16)
-    pltpu.make_async_copy(stage.at[CUTS], send_ref.at[:, columns(CUTS, width)], sems.at[CUTS]).start()
-
-    def finish(cut, carry):
-        pltpu.make_async_copy(stage.at[cut], send_ref.at[:, columns(cut, width)], sems.at[cut]).wait()
-        return carry
-
-    lax.fori_loop(0, CUTS + 1, finish, 0)
+    send_copy(CUTS).start()
+    for cut in range(CUTS + 1):
+        send_copy(cut).wait()
 
 
 def rows_by(values, rows):
@@ -113,7 +115,7 @@
     full, left = experts * MAIN, experts * 2
     return pl.pallas_call(
         functools.partial(dispatch_kernel, experts),
-        in_specs=[in_vmem()] * 3,
+        in_specs=[in_vmem(), in_vmem(), anywhere()],
         out_specs=[anywhere(), in_vmem()],
         out_shape=[
             jax.ShapeDtypeStruct((full, model + width), BF16),
@@ -124,11 +126,13 @@
             pltpu.VMEM((left, tokens), BF16),
             pltpu.VMEM((full, 1), F32),
             pltpu.VMEM((left, 1), F32),
+            pltpu.VMEM((CUTS, tokens, width), BF16),
             pltpu.VMEM((CUTS + 1, full, width), BF16),
             pltpu.VMEM((CUTS, left, width), BF16),
+            pltpu.SemaphoreType.DMA((CUTS,)),
             pltpu.SemaphoreType.DMA((CUTS + 1,)),
         ],
-        compiler_params=pltpu.CompilerParams(vmem_limit_bytes=56 << 20),
+        compiler_params=pltpu.CompilerParams(vmem_limit_bytes=60 << 20),
         cost_estimate=pl.CostEstimate(
             flops=2 * full * tokens * model, bytes_accessed=2 * (tokens + full) * model, transcendentals=0
         ),
@@ -144,7 +148,9 @@
     return jnp.where(index < experts * MAIN, main, tail)
 
 
-def travel_kernel(experts, rank_ref, own_ref, spill_ref, out_ref, place_ref, home_pick, spill_pick):
+def travel_kernel(experts, rank_ref, *refs):
+    pres, (gate_ref, up_ref, place_ref, home_pick, spill_pick) = refs[:4], refs[4:]
+
     @pl.when(pl.program_id(0) == 0)
     def _():
         for pick, first in ((home_pick, 0), (spill_pick, experts * CAP)):
@@ -167,32 +173,42 @@
         _, at = named((tokens, slots))
         place_ref[...] = jnp.where(plain_dot(by_token, widen) == at.astype(F32), 1.0, 0.0).astype(BF16)
 
-    out = plain_dot(home_pick[...], own_ref[...]) + plain_dot(spill_pick[...], spill_ref[...])
-    out_ref[...] = out.astype(BF16)
-
-
-def to_travel_order(rank, own, spill, experts):
-    slots, columns = own.shape
+    gate, up = (
+        plain_dot(home_pick[...], own[...]) + plain_dot(spill_pick[...], spill[...])
+        for own, spill in (pres[:2], pres[2:])
+    )
+    sigma = jax.nn.sigmoid(gate)
+    gate_ref[...] = up * sigma * (1.0 + gate * (1.0 - sigma))
+    up_ref[...] = gate * sigma
+
+
+def travel_factors(rank, own, spill, experts):
+    slots = own.shape[0]
     tokens = rank.shape[1]
-    width = columns // 3
+    hidden = own.shape[1] // 2
+    parts = 3
+    width = hidden // parts
     home, rest = experts * CAP, experts * OC
+    gate_block, up_block = (lambda step: (0, step)), (lambda step: (0, parts + step))
     return pl.pallas_call(
         functools.partial(travel_kernel, experts),
-        grid=(3,),
+        grid=(parts,),
         in_specs=[
             whole((experts, tokens)),
-            pl.BlockSpec((home, width), lambda step: (0, step)),
-            pl.BlockSpec((rest, width), lambda step: (0, step)),
+            pl.BlockSpec((home, width), gate_block),
+            pl.BlockSpec((rest, width), gate_block),
+            pl.BlockSpec((home, width), up_block),
+            pl.BlockSpec((rest, width), up_block),
         ],
-        out_specs=[pl.BlockSpec((slots, width), lambda step: (0, step)), whole((tokens, slots))],
-        out_shape=[jax.ShapeDtypeStruct((slots, columns), BF16), jax.ShapeDtypeStruct((tokens, slots), BF16)],
+        out_specs=[pl.BlockSpec((slots, width), gate_block)] * 2 + [whole((tokens, slots))],
+        out_shape=[jax.ShapeDtypeStruct((slots, hidden), F32)] * 2 + [jax.ShapeDtypeStruct((tokens, slots), BF16)],
         scratch_shapes=[pltpu.VMEM((slots, home), BF16), pltpu.VMEM((slots, rest), BF16)],
         compiler_params=pltpu.CompilerParams(vmem_limit_bytes=16 << 20),
         cost_estimate=pl.CostEstimate(
-            flops=2 * slots * slots * columns, bytes_accessed=4 * slots * columns, transcendentals=0
+            flops=4 * slots * slots * hidden, bytes_accessed=12 * slots * hidden, transcendentals=slots * hidden
         ),
-        name="to_travel",
-    )(rank, own, spill)
+        name="factors",
+    )(rank, own, spill, own, spill)
 
 
 def slots_kernel(experts, rows_ref, out_ref, pick):
@@ -223,122 +239,154 @@
 
 
 def expert_kernel(experts, *refs):
-    where_ref, arrived, pre_ref = refs[:3]
-    downs, gate_ups = refs[3 : 3 + CUTS], refs[3 + CUTS : 3 + 2 * CUTS]
-    grad_ref, back_ref = refs[3 + 2 * CUTS : 5 + 2 * CUTS]
-    rows, tail, pieces, down, gate_up, total, stage, row_sem, down_sem, up_sem, out_sem = refs[5 + 2 * CUTS :]
+    where_ref, arrived, gate_hbm, up_hbm = refs[:4]
+    downs, gate_ups = refs[4 : 4 + CUTS], refs[4 + CUTS : 4 + 2 * CUTS]
+    grad_ref, back_ref = refs[4 + 2 * CUTS : 6 + 2 * CUTS]
+    rows, tail, pieces, down, gate_up, total, gate_factor, up_factor, grad, back_order, stage = refs[6 + 2 * CUTS : 17 + 2 * CUTS]
+    row_sem, down_sem, up_sem, factor_sem, out_sem = refs[17 + 2 * CUTS :]
     full, left = experts * MAIN, experts * 2
-    hidden, width = down.shape[1:]
+    width = tail.shape[1]
+    hidden = total.shape[1]
+
+    def half(k):
+        return pl.ds((k % 2) * width, width)
 
     def rows_copy(k):
         return pltpu.make_async_copy(
-            arrived.at[:, columns(where_ref[k], width)], rows.at[k, pl.ds(0, full)], row_sem.at[k]
+            arrived.at[:, columns(where_ref[k], width)], rows.at[k // 2, pl.ds(0, full), half(k)], row_sem.at[k]
         )
+
+    def down_copy(k):
+        return pltpu.make_async_copy(downs[k], down.at[k // 2, :, half(k)], down_sem.at[k])
+
+    def gate_up_copy(k):
+        return pltpu.make_async_copy(gate_ups[k], gate_up.at[k // 2, half(k)], up_sem.at[k])
 
     def out_copy(k, cut):
         return pltpu.make_async_copy(stage.at[k], back_ref.at[:, columns(cut, width)], out_sem.at[k])
 
     tail_copy = pltpu.make_async_copy(arrived.at[:, columns(CUTS, width)], tail, row_sem.at[CUTS])
+    gate_copy = pltpu.make_async_copy(gate_hbm, gate_factor, factor_sem.at[0])
+    up_copy = pltpu.make_async_copy(up_hbm, up_factor, factor_sem.at[1])
     tail_copy.start()
     for k in range(CUTS):
         rows_copy(k).start()
-        pltpu.make_async_copy(downs[k], down.at[k], down_sem.at[k]).start()
-    for k in range(CUTS):
-        pltpu.make_async_copy(gate_ups[k], gate_up.at[k], up_sem.at[k]).start()
-    total[...] = jnp.zeros_like(total)
+        down_copy(k).start()
+    gate_copy.start()
+    up_copy.start()
     order = piece_rows((full, full), 1, left)
+    back_order[...] = piece_rows((full, full), 0, left)
     tail_copy.wait()
     pieces[...] = plain_dot(order, tail[...]).astype(BF16).reshape(CUTS, left, width)
-
-    def first_product(k, carry):
-        rows_copy(k).wait()
-        pltpu.make_async_copy(downs[0], down.at[k], down_sem.at[k]).wait()
-        rows[k, pl.ds(full, left)] = pieces[where_ref[k]]
-        total[...] += rows_dot(rows[k], down[k])
-        return carry
-
-    lax.fori_loop(0, CUTS, first_product, 0)
-    part = hidden // 3
-    for n in range(3):
-        own, other = pl.ds(n * part, part), pl.ds(hidden + n * part, part)
-        hidden_cot = total[:, own]
-        gate = pre_ref[:, own].astype(F32)
-        up = pre_ref[:, other].astype(F32)
-        sigma = jax.nn.sigmoid(gate)
-        grad_ref[:, own] = (hidden_cot * up * sigma * (1.0 + gate * (1.0 - sigma))).astype(BF16)
-        grad_ref[:, other] = (hidden_cot * gate * sigma).astype(BF16)
-
-    def second_product(k, carry):
-        pltpu.make_async_copy(gate_ups[0], gate_up.at[k], up_sem.at[k]).wait()
-        back = rows_dot(grad_ref[...], gate_up[k]).astype(BF16)
-        stage[k] = back[:full]
-        pieces[where_ref[k]] = back[full:]
-        out_copy(k, where_ref[k]).start()
-        return carry
-
-    lax.fori_loop(0, CUTS, second_product, 0)
-    order = piece_rows((full, full), 0, left)
-    stage[CUTS] = plain_dot(order, pieces[...].reshape(full, width)).astype(BF16)
+    for pair in range(CUTS // 2):
+        for k in (2 * pair, 2 * pair + 1):
+            rows_copy(k).wait()
+            down_copy(k).wait()
+            rows[pair, pl.ds(full, left), half(k)] = pieces[where_ref[k]]
+            if pair > 0:
+                gate_up_copy(k - 2).start()
+        product = rows_dot(rows[pair], down[pair])
+        if pair == 0:
+            total[...] = product
+        elif pair < CUTS // 2 - 1:
+            total[...] += product
+        else:
+            gate_copy.wait()
+            up_copy.wait()
+            for k in (2 * pair, 2 * pair + 1):
+                gate_up_copy(k).start()
+            hidden_cot = total[...] + product
+            grad[:, :hidden] = (hidden_cot * gate_factor[...]).astype(BF16)
+            grad[:, hidden:] = (hidden_cot * up_factor[...]).astype(BF16)
+    grad_copy = pltpu.make_async_copy(grad, grad_ref, factor_sem.at[2])
+    grad_copy.start()
+    for pair in range(CUTS // 2):
+        for k in (2 * pair, 2 * pair + 1):
+            gate_up_copy(k).wait()
+        back = rows_dot(grad[...], gate_up[pair]).astype(BF16)
+        for k in (2 * pair, 2 * pair + 1):
+            own = back[:, (k % 2) * width : (k % 2 + 1) * width]
+            stage[k] = own[:full]
+            out_copy(k, where_ref[k]).start()
+            pieces[where_ref[k]] = own[full:]
+    stage[CUTS] = plain_dot(back_order[...], pieces[...].reshape(full, width)).astype(BF16)
     out_copy(CUTS, CUTS).start()
-
-    def finish(k, carry):
+    grad_copy.wait()
+    for k in range(CUTS):
         out_copy(k, where_ref[k]).wait()
-        return carry
-
-    lax.fori_loop(0, CUTS, finish, 0)
     out_copy(CUTS, CUTS).wait()
 
 
-def expert_pass(where, arrived, pre_acts, downs, gate_ups):
+def expert_pass(where, arrived, gate_factor, up_factor, downs, gate_ups):
     full, length = arrived.shape
     hidden, width = downs[0].shape
-    slots, both = pre_acts.shape
+    slots = gate_factor.shape[0]
+    both = 2 * hidden
     model = length - width
     experts = full // MAIN
     left = experts * 2
     return pl.pallas_call(
         functools.partial(expert_kernel, experts),
-        in_specs=[pl.BlockSpec(memory_space=pltpu.SMEM), anywhere(), in_vmem()] + [anywhere()] * (2 * CUTS),
-        out_specs=[in_vmem(), anywhere()],
+        in_specs=[pl.BlockSpec(memory_space=pltpu.SMEM)] + [anywhere()] * (3 + 2 * CUTS),
+        out_specs=[anywhere(), anywhere()],
         out_shape=[jax.ShapeDtypeStruct((slots, both), BF16), jax.ShapeDtypeStruct((full, length), BF16)],
         scratch_shapes=[
-            pltpu.VMEM((CUTS, slots, width), BF16),
+            pltpu.VMEM((CUTS // 2, slots, 2 * width), BF16),
             pltpu.VMEM((full, width), BF16),
             pltpu.VMEM((CUTS, left, width), BF16),
-            pltpu.VMEM((CUTS, hidden, width), BF16),
-            pltpu.VMEM((CUTS, width, both), BF16),
+            pltpu.VMEM((CUTS // 2, hidden, 2 * width), BF16),
+            pltpu.VMEM((CUTS // 2, 2 * width, both), BF16),
             pltpu.VMEM((slots, hidden), F32),
+            pltpu.VMEM((slots, hidden), F32),
+            pltpu.VMEM((slots, hidden), F32),
+            pltpu.VMEM((slots, both), BF16),
+            pltpu.VMEM((full, full), BF16),
             pltpu.VMEM((CUTS + 1, full, width), BF16),
             pltpu.SemaphoreType.DMA((CUTS + 1,)),
             pltpu.SemaphoreType.DMA((CUTS,)),
             pltpu.SemaphoreType.DMA((CUTS,)),
+            pltpu.SemaphoreType.DMA((3,)),
             pltpu.SemaphoreType.DMA((CUTS + 1,)),
         ],
-        compiler_params=pltpu.CompilerParams(vmem_limit_bytes=56 << 20),
+        compiler_params=pltpu.CompilerParams(vmem_limit_bytes=60 << 20),
         cost_estimate=pl.CostEstimate(
             flops=6 * slots * hidden * model,
             bytes_accessed=2 * (2 * slots * model + 3 * hidden * model + 2 * slots * both),
-            transcendentals=slots * hidden,
+            transcendentals=0,
         ),
         name="experts",
-    )(where, arrived, pre_acts, *downs, *gate_ups)
-
-
-def combine_kernel(place_ref, main_ref, tail_ref, out_ref, pieces):
-    step = pl.program_id(0)
-    full, width = tail_ref.shape
+    )(where, arrived, gate_factor, up_factor, *downs, *gate_ups)
+
+
+def combine_kernel(place_ref, returned, out_ref, rows, tail, pieces, stage, row_sem, out_sem):
+    full, width = tail.shape
     left = pieces.shape[1]
 
-    @pl.when(step == 0)
-    def _():
-        order = piece_rows((full, full), 1, left)
-        pieces[...] = plain_dot(order, tail_ref[...]).astype(BF16).reshape(CUTS, left, width)
-
-    for half in range(2):
-        part = pl.ds(half * width, width)
-        total = plain_dot(place_ref[:, :full], main_ref[:, part])
-        total += plain_dot(place_ref[:, full:], pieces[2 * step + half])
-        out_ref[:, part] = total.astype(BF16)
+    def rows_copy(pair):
+        return pltpu.make_async_copy(
+            returned.at[:, pl.ds(pair * 2 * width, 2 * width)], rows.at[pair], row_sem.at[pair]
+        )
+
+    def out_copy(pair):
+        return pltpu.make_async_copy(stage.at[pair], out_ref.at[:, pl.ds(pair * 2 * width, 2 * width)], out_sem.at[pair])
+
+    tail_copy = pltpu.make_async_copy(returned.at[:, pl.ds(CUTS * width, width)], tail, row_sem.at[CUTS // 2])
+    tail_copy.start()
+    for pair in range(CUTS // 2):
+        rows_copy(pair).start()
+    order = piece_rows((full, full), 1, left)
+    tail_copy.wait()
+    pieces[...] = plain_dot(order, tail[...]).astype(BF16).reshape(CUTS, left, width)
+    for pair in range(CUTS // 2):
+        rows_copy(pair).wait()
+        for cut in range(2):
+            part = pl.ds(cut * width, width)
+            total = plain_dot(place_ref[:, :full], rows[pair, :, part])
+            total += plain_dot(place_ref[:, full:], pieces[2 * pair + cut])
+            stage[pair, :, part] = total.astype(BF16)
+        out_copy(pair).start()
+    for pair in range(CUTS // 2):
+        out_copy(pair).wait()
 
 
 def combine(place, returned):
@@ -349,21 +397,23 @@
     left = slots - full
     return pl.pallas_call(
         combine_kernel,
-        grid=(CUTS // 2,),
-        in_specs=[
-            whole((tokens, slots)),
-            pl.BlockSpec((full, 2 * width), lambda step: (0, step)),
-            pl.BlockSpec((full, width), lambda step: (0, CUTS)),
+        in_specs=[in_vmem(), anywhere()],
+        out_specs=anywhere(),
+        out_shape=jax.ShapeDtypeStruct((tokens, model), BF16),
+        scratch_shapes=[
+            pltpu.VMEM((CUTS // 2, full, 2 * width), BF16),
+            pltpu.VMEM((full, width), BF16),
+            pltpu.VMEM((CUTS, left, width), BF16),
+            pltpu.VMEM((CUTS // 2, tokens, 2 * width), BF16),
+            pltpu.SemaphoreType.DMA((CUTS // 2 + 1,)),
+            pltpu.SemaphoreType.DMA((CUTS // 2,)),
         ],
-        out_specs=pl.BlockSpec((tokens, 2 * width), lambda step: (0, step)),
-        out_shape=jax.ShapeDtypeStruct((tokens, model), BF16),
-        scratch_shapes=[pltpu.VMEM((CUTS, left, width), BF16)],
-        compiler_params=pltpu.CompilerParams(vmem_limit_bytes=56 << 20),
+        compiler_params=pltpu.CompilerParams(vmem_limit_bytes=60 << 20),
         cost_estimate=pl.CostEstimate(
             flops=2 * slots * tokens * model, bytes_accessed=2 * (tokens + slots) * model, transcendentals=0
         ),
         name="combine",
-    )(place, returned, returned)
+    )(place, returned)
 
 
 def along_dp(shard, target):
@@ -410,8 +460,8 @@
     arrived = exchange(sent, experts)
     downs, gate_ups = gathered(down_weight[0]), gathered(gate_up_weight[0])
     spill_pre = moved(own_pre[home:], offset, -1)
-    pre_acts, place = to_travel_order(rank, own_pre, spill_pre, experts)
-    travel_grad, back = expert_pass(shard_places(), arrived, pre_acts, downs, gate_ups)
+    gate_factor, up_factor, place = travel_factors(rank, own_pre, spill_pre, experts)
+    travel_grad, back = expert_pass(shard_places(), arrived, gate_factor, up_factor, downs, gate_ups)
     returned = exchange(back, experts)
     by_slot = to_slot_order(travel_grad, experts)
     spill_grad = moved(by_slot[home:], offset, 1)

time: 271 us -> 268 us (0.989)
  Pallas kernels: 39.8 us -> 36.6 us
  transfers between devices with their start and end apart: 22 -> 22, of which waited for: 12 -> 10; matrix products, arithmetic and copies ran while one was open for 3% -> 3% of each run, Pallas kernels for 2% -> 2%
where the time goes in v3:
time: 268 us
  waiting for transfers between devices  176 us (66%)
  starting transfers between devices  40.5 us (15%)
  Pallas kernels  36.6 us (14%)
  local copies, waits for them, and re-layouts  6.28 us (2%)
  other arithmetic  6.27 us (2%)
    all_to_all x2, waiting for transfers between devices, exchange(): lax.all_to_all(blocks, 'expert', split_axis=0, concat_axis=0, tiled=True)  82.6 us
    ppermute x6, waiting for transfers between devices, moved(): lax.ppermute(rows, 'dp', [(i, (i + by) % replicas) for i in range(replica...  62.6 us
    ppermute x14, waiting for transfers between devices, along_dp(): lax.ppermute(shard, 'dp', [(i, target(i)) for i in range(lax.axis_size('d...  30.9 us
    all_to_all x2, starting transfers between devices, exchange(): lax.all_to_all(blocks, 'expert', split_axis=0, concat_axis=0, tiled=True)  20.4 us
    pallas_call x1, Pallas kernels, expert_pass(): pl.pallas_call(functools.partial(expert_kernel, experts), in_specs=[pl.Bl...  19.3 us
    ppermute x14, starting transfers between devices, along_dp(): lax.ppermute(shard, 'dp', [(i, target(i)) for i in range(lax.axis_size('d...  11.5 us
    ppermute x6, starting transfers between devices, moved(): lax.ppermute(rows, 'dp', [(i, (i + by) % replicas) for i in range(replica...  8.56 us
    pallas_call x1, Pallas kernels, dispatch(): pl.pallas_call(functools.partial(dispatch_kernel, experts), in_specs=[in_...  6.11 us
  transfers between devices with their start and end apart: 22, of which 10 were waited for; matrix products, arithmetic and copies ran while one was open for 3% of the time, Pallas kernels for 2%

profile of v3, /device:TPU:35, one launch (start us, length us, event | category | flops | bytes accessed | tf_op | source)
XLA Modules:
  0.0 267.5 jit_solution(4295160057818404978)
XLA Ops:
  0.6 6.1 %dispatch.1 = (bf16[512,4608]{1,0:T(8,128)(2,1)}, f32[32,192]{1,0:T(8,128)}) custom-call(s32[8,192]{1,0:T(8,128)} %bitcast.28, f32[8,192]{1,0:T(8,128)} %bitcast.29, bf16[192,4096]{1,0:T(8,128)(2,1)} %grad_ref.1), custom_call_target="tpu_custom_call" | custom-call | flops 805306368 | bytes 5767168 | tf_op jit(solution)/shard_map/dispatch/pallas_call | solution.py:116
  6.8 11.0 %all-to-all-start = ((bf16[32,16,4608]{2,1,0:T(8,128)(2,1)}), bf16[32,16,4608]{2,1,0:T(8,128)(2,1)}, u32[]{:S(2)}, u32[]{:S(2)}) async-start(bf16[32,16,4608]{2,1,0:T(8,128)(2,1)} %bitcast.21), calls=%async_computation | async-start | bytes 9437184 | tf_op jit(solution)/shard_map/all_to_all | solution.py:451
  17.7 1.3 collective-permute-start.10
  19.0 0.2 collective-permute-start.11
  19.3 1.2 collective-permute-start.3
  20.5 0.3 collective-permute-start.4
  20.8 0.7 slice_bitcast_fusion
  21.5 2.4 collective-permute-start
  23.9 28.9 %collective-permute-done.10.refs_13_ = bf16[512,1536]{1,0:T(8,128)(2,1)S(1)} collective-permute-done((bf16[512,1536]{1,0:T(8,128)(2,1)}, bf16[512,1536]{1,0:T(8,128)(2,1)S(1)}, u32[]{:S(2)}, u32[]{:S(2)}) %collective-permute-start.10) | collective-permute-done | bytes 1572896 | tf_op jit(solution)/shard_map/ppermute | solution.py:420
  52.8 0.9 collective-permute-done.11.refs_14_
  53.7 1.6 broadcast_select_fusion
  55.3 1.2 collective-permute-start.12
  56.5 3.2 %collective-permute-start.6 = (bf16[768,512]{1,0:T(8,128)(2,1)S(1)}, bf16[768,512]{1,0:T(8,128)(2,1)S(1)}, u32[]{:S(2)}, u32[]{:S(2)}) collective-permute-start(bf16[768,512]{1,0:T(8,128)(2,1)S(1)} %bitcast.27), channel_id=1, source_target_pairs={{0,32},{32,0},{64,96},{96,64},{128,160},{160,128},{192,224},{224,1... | collective-permute-start | bytes 2359304 | tf_op jit(solution)/shard_map/ppermute | solution.py:420
  60.3 20.7 %collective-permute-done = bf16[96,1536]{1,0:T(8,128)(2,1)} collective-permute-done((bf16[96,1536]{1,0:T(8,128)(2,1)}, bf16[96,1536]{1,0:T(8,128)(2,1)}, u32[]{:S(2)}, u32[]{:S(2)}) %collective-permute-start) | collective-permute-done | bytes 294944 | tf_op jit(solution)/shard_map/ppermute | solution.py:444
  81.0 0.3 collective-permute-start.1
  81.4 1.2 broadcast_select_fusion.1
  82.6 2.7 %collective-permute-start.5 = (bf16[768,512]{1,0:T(8,128)(2,1)S(1)}, bf16[768,512]{1,0:T(8,128)(2,1)S(1)}, u32[]{:S(2)}, u32[]{:S(2)}) collective-permute-start(bf16[768,512]{1,0:T(8,128)(2,1)S(1)} %broadcast_select_fusion.1), channel_id=1, source_target_pairs={{0,64},{32,224},{64,128},{96,32},{128,192},{160,96},{192,0},{224,1... | collective-permute-start | bytes 2359304 | tf_op jit(solution)/shard_map/ppermute | solution.py:420
  85.4 16.8 %collective-permute-done.1 = bf16[96,1536]{1,0:T(8,128)(2,1)S(1)} collective-permute-done((bf16[96,1536]{1,0:T(8,128)(2,1)S(1)}, bf16[96,1536]{1,0:T(8,128)(2,1)S(1)}, u32[]{:S(2)}, u32[]{:S(2)}) %collective-permute-start.1) | collective-permute-done | bytes 294944 | tf_op jit(solution)/shard_map/ppermute | solution.py:444
  102.2 2.1 collective-permute-start.2
  104.3 10.0 %collective-permute-done.2 = bf16[96,1536]{1,0:T(8,128)(2,1)S(1)} collective-permute-done((bf16[96,1536]{1,0:T(8,128)(2,1)S(1)}, bf16[96,1536]{1,0:T(8,128)(2,1)S(1)}, u32[]{:S(2)}, u32[]{:S(2)}) %collective-permute-start.2) | collective-permute-done | bytes 294944 | tf_op jit(solution)/shard_map/ppermute | solution.py:444
  114.4 0.6 collective-permute-start.14
  115.0 0.3 collective-permute-start.15
  115.3 0.1 copy-done.12
  115.4 0.4 copy-done.13
  115.8 0.2 collective-permute-start.16
  116.1 0.3 collective-permute-start.9
  116.4 0.6 pad_add_fusion.refs_0_
  117.0 1.0 broadcast_select_fusion.6.refs_1_.refs_3_
  118.0 3.0 %factors.1 = (f32[576,768]{1,0:T(8,128)S(1)}, f32[576,768]{1,0:T(8,128)S(1)}, bf16[192,576]{1,0:T(8,128)(2,1)S(1)}) custom-call(f32[32,192]{1,0:T(8,128)S(1)} %copy-done.2, bf16[576,1536]{1,0:T(8,128)(2,1)S(1)} %bitcast.19, bf16[96,1536]{1,0:T(8,128)(2,1)S(1)} %broadcast_select_fusion.6.refs_1_.refs_3_, bf16[576,1536]{1,0:T(8,128)(2,1)S(1)} %bitcast.20, ...), custom_call_target="tpu_custom_call" | custom-call | flops 1019215872 | bytes 5308416 | tf_op jit(solution)/shard_map/factors/pallas_call | solution.py:193
  120.9 0.7 copy-done.1
  121.6 1.2 copy-done.3
  122.8 1.2 copy-done.4
  124.0 0.9 copy-done.14
  124.9 1.1 collective-permute-done.16.refs_19_
  126.0 19.3 %experts.1 = (bf16[576,1536]{1,0:T(8,128)(2,1)}, bf16[512,4608]{1,0:T(8,128)(2,1)}) custom-call(s32[8]{0:T(128)} %pad_add_fusion.refs_0_, bf16[512,4608]{1,0:T(8,128)(2,1)} %bitcast.8.refs_1_, f32[576,768]{1,0:T(8,128)} %copy-done.3, f32[576,768]{1,0:T(8,128)} %copy-done.4, bf16[768,512]{1,0:T(8,128)(2,1)} %bitcast.26, ...), custom_call_target="tpu_custom_call" | custom-call | flops 10871635968 | bytes 31850496 | tf_op jit(solution)/shard_map/experts/pallas_call | solution.py:328
  145.3 9.4 %all-to-all-start.1 = ((bf16[32,16,4608]{2,1,0:T(8,128)(2,1)}), bf16[32,16,4608]{2,1,0:T(8,128)(2,1)}, u32[]{:S(2)}, u32[]{:S(2)}) async-start(bf16[32,16,4608]{2,1,0:T(8,128)(2,1)} %bitcast.22), calls=%async_computation.1 | async-start | bytes 9437184 | tf_op jit(solution)/shard_map/all_to_all | solution.py:451
  154.8 3.1 %to_slots.1 = bf16[576,1536]{1,0:T(8,128)(2,1)} custom-call(bf16[576,1536]{1,0:T(8,128)(2,1)S(1)} %copy-done.5), custom_call_target="tpu_custom_call" | custom-call | flops 1019215872 | bytes 3538944 | tf_op jit(solution)/shard_map/to_slots/pallas_call | solution.py:226
  157.9 1.0 slice.12
  158.9 0.0 collective-permute-start.17
  158.9 3.7 %collective-permute-done.17 = bf16[96,1536]{1,0:T(8,128)(2,1)S(1)} collective-permute-done((bf16[96,1536]{1,0:T(8,128)(2,1)S(1)}, bf16[96,1536]{1,0:T(8,128)(2,1)S(1)}, u32[]{:S(2)}, u32[]{:S(2)}) %collective-permute-start.17) | collective-permute-done | bytes 294944 | tf_op jit(solution)/shard_map/ppermute | solution.py:444
  162.6 1.0 broadcast_select_fusion.2
  163.6 2.1 collective-permute-start.18
  165.7 5.5 %collective-permute-done.18 = bf16[96,1536]{1,0:T(8,128)(2,1)S(1)} collective-permute-done((bf16[96,1536]{1,0:T(8,128)(2,1)S(1)}, bf16[96,1536]{1,0:T(8,128)(2,1)S(1)}, u32[]{:S(2)}, u32[]{:S(2)}) %collective-permute-start.18) | collective-permute-done | bytes 294944 | tf_op jit(solution)/shard_map/ppermute | solution.py:444
  171.2 1.6 collective-permute-start.19
  172.8 6.1 %collective-permute-done.19 = bf16[96,1536]{1,0:T(8,128)(2,1)S(1)} collective-permute-done((bf16[96,1536]{1,0:T(8,128)(2,1)S(1)}, bf16[96,1536]{1,0:T(8,128)(2,1)S(1)}, u32[]{:S(2)}, u32[]{:S(2)}) %collective-permute-start.19) | collective-permute-done | bytes 294944 | tf_op jit(solution)/shard_map/ppermute | solution.py:444
  178.8 0.8 bitcast_dynamic-update-slice_fusion
  179.6 82.6 %all-to-all-done.1 = bf16[32,16,4608]{2,1,0:T(8,128)(2,1)} async-done(((bf16[32,16,4608]{2,1,0:T(8,128)(2,1)}), bf16[32,16,4608]{2,1,0:T(8,128)(2,1)}, u32[]{:S(2)}, u32[]{:S(2)}) %all-to-all-start.1) | async-done | bytes 4718624 | tf_op jit(solution)/shard_map/all_to_all | solution.py:451
  262.3 5.1 %combine.1 = bf16[192,4096]{1,0:T(8,128)(2,1)} custom-call(bf16[192,576]{1,0:T(8,128)(2,1)} %copy-done.1, bf16[512,4608]{1,0:T(8,128)(2,1)} %bitcast.12.returned), custom_call_target="tpu_custom_call" | custom-call | flops 905969664 | bytes 6291456 | tf_op jit(solution)/shard_map/combine/pallas_call | solution.py:398
  (43 shorter events, 0.2 us)
Async XLA Ops:
  6.7 14.0 %copy-start = (bf16[1,1,576,1536]{3,2,1,0:T(8,128)(2,1)S(1)}, bf16[1,1,576,1536]{3,2,1,0:T(8,128)(2,1)}, u32[]{:S(2)}) copy-start(bf16[1,1,576,1536]{3,2,1,0:T(8,128)(2,1)} %param.12) | copy-start | bytes 5308420
  6.8 119.2 %all-to-all-start = ((bf16[32,16,4608]{2,1,0:T(8,128)(2,1)}), bf16[32,16,4608]{2,1,0:T(8,128)(2,1)}, u32[]{:S(2)}, u32[]{:S(2)}) async-start(bf16[32,16,4608]{2,1,0:T(8,128)(2,1)} %bitcast.21), calls=%async_computation | async-start | bytes 9437184 | tf_op jit(solution)/shard_map/all_to_all | solution.py:451
  17.7 35.0 %collective-permute-start.10 = (bf16[512,1536]{1,0:T(8,128)(2,1)}, bf16[512,1536]{1,0:T(8,128)(2,1)S(1)}, u32[]{:S(2)}, u32[]{:S(2)}) collective-permute-start(bf16[512,1536]{1,0:T(8,128)(2,1)} %bitcast.10.refs_12_), channel_id=1, source_target_pairs={{0,64},{32,96},{64,128},{96,160},{128,192},{160,224},{192,0},{224,... | collective-permute-start | bytes 4718600 | tf_op jit(solution)/shard_map/ppermute | solution.py:420
  19.0 34.7 %collective-permute-start.11 = (bf16[512,1536]{1,0:T(8,128)(2,1)}, bf16[512,1536]{1,0:T(8,128)(2,1)}, u32[]{:S(2)}, u32[]{:S(2)}) collective-permute-start(bf16[512,1536]{1,0:T(8,128)(2,1)} %bitcast.10.refs_12_), channel_id=1, source_target_pairs={{0,192},{32,224},{64,0},{96,32},{128,64},{160,96},{192,128},{224,1... | collective-permute-start | bytes 4718600 | tf_op jit(solution)/shard_map/ppermute | solution.py:420
  19.3 62.1 %collective-permute-start.3 = (bf16[768,512]{1,0:T(8,128)(2,1)}, bf16[768,512]{1,0:T(8,128)(2,1)}, u32[]{:S(2)}, u32[]{:S(2)}) collective-permute-start(bf16[768,512]{1,0:T(8,128)(2,1)} %bitcast.24), channel_id=1, source_target_pairs={{0,64},{32,96},{64,128},{96,160},{128,192},{160,224},{192,0},{224,... | collective-permute-start | bytes 2359304 | tf_op jit(solution)/shard_map/ppermute | solution.py:420
  20.5 60.9 %collective-permute-start.4 = (bf16[768,512]{1,0:T(8,128)(2,1)}, bf16[768,512]{1,0:T(8,128)(2,1)}, u32[]{:S(2)}, u32[]{:S(2)}) collective-permute-start(bf16[768,512]{1,0:T(8,128)(2,1)} %bitcast.25), channel_id=1, source_target_pairs={{0,192},{32,224},{64,0},{96,32},{128,64},{160,96},{192,128},{224,1... | collective-permute-start | bytes 2359304 | tf_op jit(solution)/shard_map/ppermute | solution.py:420
  21.5 59.5 %collective-permute-start = (bf16[96,1536]{1,0:T(8,128)(2,1)}, bf16[96,1536]{1,0:T(8,128)(2,1)}, u32[]{:S(2)}, u32[]{:S(2)}) collective-permute-start(bf16[96,1536]{1,0:T(8,128)(2,1)} %slice_bitcast_fusion), channel_id=1, source_target_pairs={{0,224},{32,0},{64,32},{96,64},{128,96},{160,128},{192,160},{224,1... | collective-permute-start | bytes 884744 | tf_op jit(solution)/shard_map/ppermute | solution.py:444
  23.9 32.6 %copy-start.10 = (bf16[1,768,512]{2,1,0:T(8,128)(2,1)S(1)}, bf16[1,768,512]{2,1,0:T(8,128)(2,1)}, u32[]{:S(2)}) copy-start(bf16[1,768,512]{2,1,0:T(8,128)(2,1)} %param.13) | copy-start | bytes 2359300
  52.8 61.6 %copy-start.6 = (bf16[512,1536]{1,0:T(8,128)(2,1)}, bf16[512,1536]{1,0:T(8,128)(2,1)S(1)}, u32[]{:S(2)}) copy-start(bf16[512,1536]{1,0:T(8,128)(2,1)S(1)} %collective-permute-done.10.refs_13_) | copy-start | bytes 4718596
  55.3 59.9 %collective-permute-start.12 = (bf16[512,1536]{1,0:T(8,128)(2,1)S(1)}, bf16[512,1536]{1,0:T(8,128)(2,1)}, u32[]{:S(2)}, u32[]{:S(2)}) collective-permute-start(bf16[512,1536]{1,0:T(8,128)(2,1)S(1)} %broadcast_select_fusion), channel_id=1, source_target_pairs={{0,64},{32,224},{64,128},{96,32},{128,192},{160,96},{192,0},{224,1... | collective-permute-start | bytes 4718600 | tf_op jit(solution)/shard_map/ppermute | solution.py:420
  56.5 47.8 %collective-permute-start.6 = (bf16[768,512]{1,0:T(8,128)(2,1)S(1)}, bf16[768,512]{1,0:T(8,128)(2,1)S(1)}, u32[]{:S(2)}, u32[]{:S(2)}) collective-permute-start(bf16[768,512]{1,0:T(8,128)(2,1)S(1)} %bitcast.27), channel_id=1, source_target_pairs={{0,32},{32,0},{64,96},{96,64},{128,160},{160,128},{192,224},{224,1... | collective-permute-start | bytes 2359304 | tf_op jit(solution)/shard_map/ppermute | solution.py:420
  81.0 35.3 %copy-start.9 = (s32[4]{0:T(128)S(1)}, s32[4]{0:T(128)}, u32[]{:S(2)}) copy-start(s32[4]{0:T(128)} %constant.48.clone) | copy-start | bytes 52
  81.0 36.9 %copy-start.2 = (f32[32,192]{1,0:T(8,128)S(1)}, f32[32,192]{1,0:T(8,128)}, u32[]{:S(2)}) copy-start(f32[32,192]{1,0:T(8,128)} %get-tuple-element.9.rank_ref) | copy-start | bytes 73732
  81.0 21.1 %collective-permute-start.1 = (bf16[96,1536]{1,0:T(8,128)(2,1)S(1)}, bf16[96,1536]{1,0:T(8,128)(2,1)S(1)}, u32[]{:S(2)}, u32[]{:S(2)}) collective-permute-start(bf16[96,1536]{1,0:T(8,128)(2,1)S(1)} %broadcast_select_fusion.3), channel_id=1, source_target_pairs={{0,192},{32,224},{64,0},{96,32},{128,64},{160,96},{192,128},{224,1... | collective-permute-start | bytes 884744 | tf_op jit(solution)/shard_map/ppermute | solution.py:444
  82.6 31.7 %collective-permute-start.5 = (bf16[768,512]{1,0:T(8,128)(2,1)S(1)}, bf16[768,512]{1,0:T(8,128)(2,1)S(1)}, u32[]{:S(2)}, u32[]{:S(2)}) collective-permute-start(bf16[768,512]{1,0:T(8,128)(2,1)S(1)} %broadcast_select_fusion.1), channel_id=1, source_target_pairs={{0,64},{32,224},{64,128},{96,32},{128,192},{160,96},{192,0},{224,1... | collective-permute-start | bytes 2359304 | tf_op jit(solution)/shard_map/ppermute | solution.py:420
  85.4 29.6 %collective-permute-start.7 = (bf16[768,512]{1,0:T(8,128)(2,1)}, bf16[768,512]{1,0:T(8,128)(2,1)S(1)}, u32[]{:S(2)}, u32[]{:S(2)}) collective-permute-start(bf16[768,512]{1,0:T(8,128)(2,1)} %collective-permute-done.3.refs_5_), channel_id=1, source_target_pairs={{0,32},{32,0},{64,96},{96,64},{128,160},{160,128},{192,224},{224,1... | collective-permute-start | bytes 2359304 | tf_op jit(solution)/shard_map/ppermute | solution.py:420
  102.2 13.1 %copy-start.7 = (bf16[96,1536]{1,0:T(8,128)(2,1)}, bf16[96,1536]{1,0:T(8,128)(2,1)S(1)}, u32[]{:S(2)}) copy-start(bf16[96,1536]{1,0:T(8,128)(2,1)S(1)} %broadcast_select_fusion.5) | copy-start | bytes 884740
  102.2 12.2 %collective-permute-start.2 = (bf16[96,1536]{1,0:T(8,128)(2,1)S(1)}, bf16[96,1536]{1,0:T(8,128)(2,1)S(1)}, u32[]{:S(2)}, u32[]{:S(2)}) collective-permute-start(bf16[96,1536]{1,0:T(8,128)(2,1)S(1)} %broadcast_select_fusion.5), channel_id=1, source_target_pairs={{0,128},{32,160},{64,192},{96,224},{128,0},{160,32},{192,64},{224,... | collective-permute-start | bytes 884744 | tf_op jit(solution)/shard_map/ppermute | solution.py:444
  104.3 11.0 %copy-start.11 = (bf16[768,512]{1,0:T(8,128)(2,1)}, bf16[768,512]{1,0:T(8,128)(2,1)S(1)}, u32[]{:S(2)}) copy-start(bf16[768,512]{1,0:T(8,128)(2,1)S(1)} %collective-permute-done.6.refs_8_) | copy-start | bytes 2359300
  104.3 11.8 %collective-permute-start.8 = (bf16[768,512]{1,0:T(8,128)(2,1)}, bf16[768,512]{1,0:T(8,128)(2,1)}, u32[]{:S(2)}, u32[]{:S(2)}) collective-permute-start(bf16[768,512]{1,0:T(8,128)(2,1)} %collective-permute-done.4.refs_6_), channel_id=1, source_target_pairs={{0,32},{32,0},{64,96},{96,64},{128,160},{160,128},{192,224},{224,1... | collective-permute-start | bytes 2359304 | tf_op jit(solution)/shard_map/ppermute | solution.py:420
  114.3 0.9 copy-start.8
  114.3 9.7 %collective-permute-start.13 = (bf16[512,1536]{1,0:T(8,128)(2,1)}, bf16[512,1536]{1,0:T(8,128)(2,1)}, u32[]{:S(2)}, u32[]{:S(2)}) collective-permute-start(bf16[512,1536]{1,0:T(8,128)(2,1)} %bitcast.10.refs_12_), channel_id=1, source_target_pairs={{0,32},{32,0},{64,96},{96,64},{128,160},{160,128},{192,224},{224,1... | collective-permute-start | bytes 4718600 | tf_op jit(solution)/shard_map/ppermute | solution.py:420
  114.4 1.0 copy-start.12
  114.4 9.7 %collective-permute-start.14 = (bf16[512,1536]{1,0:T(8,128)(2,1)S(1)}, bf16[512,1536]{1,0:T(8,128)(2,1)}, u32[]{:S(2)}, u32[]{:S(2)}) collective-permute-start(bf16[512,1536]{1,0:T(8,128)(2,1)S(1)} %collective-permute-done.10.refs_13_), channel_id=1, source_target_pairs={{0,32},{32,0},{64,96},{96,64},{128,160},{160,128},{192,224},{224,1... | collective-permute-start | bytes 4718600 | tf_op jit(solution)/shard_map/ppermute | solution.py:420
  115.0 0.9 copy-start.13
  115.0 10.0 %collective-permute-start.15 = (bf16[512,1536]{1,0:T(8,128)(2,1)}, bf16[512,1536]{1,0:T(8,128)(2,1)}, u32[]{:S(2)}, u32[]{:S(2)}) collective-permute-start(bf16[512,1536]{1,0:T(8,128)(2,1)} %collective-permute-done.11.refs_14_), channel_id=1, source_target_pairs={{0,32},{32,0},{64,96},{96,64},{128,160},{160,128},{192,224},{224,1... | collective-permute-start | bytes 4718600 | tf_op jit(solution)/shard_map/ppermute | solution.py:420
  115.8 10.1 %collective-permute-start.16 = (bf16[512,1536]{1,0:T(8,128)(2,1)}, bf16[512,1536]{1,0:T(8,128)(2,1)}, u32[]{:S(2)}, u32[]{:S(2)}) collective-permute-start(bf16[512,1536]{1,0:T(8,128)(2,1)} %collective-permute-done.12.refs_15_), channel_id=1, source_target_pairs={{0,32},{32,0},{64,96},{96,64},{128,160},{160,128},{192,224},{224,1... | collective-permute-start | bytes 4718600 | tf_op jit(solution)/shard_map/ppermute | solution.py:420
  116.1 8.0 %collective-permute-start.9 = (bf16[768,512]{1,0:T(8,128)(2,1)}, bf16[768,512]{1,0:T(8,128)(2,1)S(1)}, u32[]{:S(2)}, u32[]{:S(2)}) collective-permute-start(bf16[768,512]{1,0:T(8,128)(2,1)} %copy-done.12), channel_id=1, source_target_pairs={{0,32},{32,0},{64,96},{96,64},{128,160},{160,128},{192,224},{224,1... | collective-permute-start | bytes 2359304 | tf_op jit(solution)/shard_map/ppermute | solution.py:420
  120.9 0.7 copy-start.1
  121.6 1.2 copy-start.3
  122.8 1.2 copy-start.4
  124.0 0.9 copy-start.14
  145.3 9.4 %copy-start.5 = (bf16[576,1536]{1,0:T(8,128)(2,1)S(1)}, bf16[576,1536]{1,0:T(8,128)(2,1)}, u32[]{:S(2)}) copy-start(bf16[576,1536]{1,0:T(8,128)(2,1)} %get-tuple-element.15.rows_ref) | copy-start | bytes 5308420
  145.3 116.9 %all-to-all-start.1 = ((bf16[32,16,4608]{2,1,0:T(8,128)(2,1)}), bf16[32,16,4608]{2,1,0:T(8,128)(2,1)}, u32[]{:S(2)}, u32[]{:S(2)}) async-start(bf16[32,16,4608]{2,1,0:T(8,128)(2,1)} %bitcast.22), calls=%async_computation.1 | async-start | bytes 9437184 | tf_op jit(solution)/shard_map/all_to_all | solution.py:451
  158.9 3.7 %collective-permute-start.17 = (bf16[96,1536]{1,0:T(8,128)(2,1)S(1)}, bf16[96,1536]{1,0:T(8,128)(2,1)S(1)}, u32[]{:S(2)}, u32[]{:S(2)}) collective-permute-start(bf16[96,1536]{1,0:T(8,128)(2,1)S(1)} %slice.12), channel_id=1, source_target_pairs={{0,32},{32,64},{64,96},{96,128},{128,160},{160,192},{192,224},{224... | collective-permute-start | bytes 884744 | tf_op jit(solution)/shard_map/ppermute | solution.py:444
  163.6 7.6 %collective-permute-start.18 = (bf16[96,1536]{1,0:T(8,128)(2,1)S(1)}, bf16[96,1536]{1,0:T(8,128)(2,1)S(1)}, u32[]{:S(2)}, u32[]{:S(2)}) collective-permute-start(bf16[96,1536]{1,0:T(8,128)(2,1)S(1)} %broadcast_select_fusion.2), channel_id=1, source_target_pairs={{0,64},{32,96},{64,128},{96,160},{128,192},{160,224},{192,0},{224,... | collective-permute-start | bytes 884744 | tf_op jit(solution)/shard_map/ppermute | solution.py:444
  171.2 7.7 %collective-permute-start.19 = (bf16[96,1536]{1,0:T(8,128)(2,1)S(1)}, bf16[96,1536]{1,0:T(8,128)(2,1)S(1)}, u32[]{:S(2)}, u32[]{:S(2)}) collective-permute-start(bf16[96,1536]{1,0:T(8,128)(2,1)S(1)} %broadcast_select_fusion.4), channel_id=1, source_target_pairs={{0,128},{32,160},{64,192},{96,224},{128,0},{160,32},{192,64},{224,... | collective-permute-start | bytes 884744 | tf_op jit(solution)/shard_map/ppermute | solution.py:444

commit v4 on v3

--- a/solution.py
+++ b/solution.py
@@ -11,6 +11,7 @@
 OC = 3
 MAIN = 16
 CUTS = 8
+AHEAD = 6
 F32 = jnp.float32
 BF16 = jnp.bfloat16
 
@@ -50,9 +51,9 @@
 
 
 def dispatch_kernel(
-    experts, ids_ref, gates_ref, grad_ref, send_ref, rank_ref, main_pick, tail_pick, main_gate, tail_gate, grads, stage, pieces, grad_sem, sems
+    experts, ids_hbm, gates_hbm, grad_ref, send_ref, rank_hbm, ids_ref, gates_ref, rank_ref, pick, scale_of, grads, stage, pieces, grad_sem, sems, small_sem
 ):
-    choices, tokens = ids_ref.shape
+    choices, tokens = ids_hbm.shape
     full, left = experts * MAIN, experts * 2
     width = grads.shape[2]
 
@@ -62,8 +63,16 @@
     def send_copy(cut):
         return pltpu.make_async_copy(stage.at[cut], send_ref.at[:, pl.ds(cut * width, width)], sems.at[cut])
 
+    ids_copy = pltpu.make_async_copy(ids_hbm, ids_ref, small_sem.at[0])
+    gates_copy = pltpu.make_async_copy(gates_hbm, gates_ref, small_sem.at[1])
+    rank_copy = pltpu.make_async_copy(rank_ref, rank_hbm, small_sem.at[2])
+    ids_copy.start()
+    gates_copy.start()
     for cut in range(CUTS):
         grad_copy(cut).start()
+    earlier = (iota((tokens, tokens), 0) < iota((tokens, tokens), 1)).astype(F32).astype(BF16)
+    ids_copy.wait()
+    gates_copy.wait()
     expert = iota((experts, tokens), 0)
     hit = jnp.zeros((experts, tokens), F32)
     gate = jnp.zeros((experts, tokens), F32)
@@ -71,36 +80,29 @@
         same = ids_ref[k : k + 1, :] == expert
         hit = jnp.where(same, 1.0, hit)
         gate = jnp.where(same, gates_ref[k : k + 1, :], gate)
-    earlier = (iota((tokens, tokens), 0) < iota((tokens, tokens), 1)).astype(F32).astype(BF16)
     rank = jnp.where(hit > 0.0, plain_dot(hit.astype(BF16), earlier), -1.0)
     rank_ref[...] = rank
-    for deep, first, pick_ref, scale_ref in ((MAIN, 0, main_pick, main_gate), (8, MAIN, tail_pick, tail_gate)):
-        position = iota((experts, deep, tokens), 1)
-        wanted = (first + position).astype(F32)
-        taken = jnp.broadcast_to(rank[:, None, :], wanted.shape) == wanted
-        scale = jnp.where(taken, jnp.broadcast_to(gate[:, None, :], wanted.shape), 0.0)
-        one = jnp.where(taken, 1.0, 0.0)
-        if deep == MAIN:
-            pick_ref[...] = one.reshape(full, tokens).astype(BF16)
-            scale_ref[...] = jnp.sum(scale.reshape(full, tokens), axis=1, keepdims=True)
-        else:
-            row = iota((left, experts * deep), 0)
-            keep = iota((left, experts * deep), 1) == ((row >> 1) << 3) + (row & 1)
-            keep = jnp.where(keep, 1.0, 0.0)
-            pick_ref[...] = plain_dot(keep.astype(BF16), one.reshape(experts * deep, tokens).astype(BF16)).astype(BF16)
-            by_row = rows_by(gate, left)
-            scale_ref[...] = jnp.sum(jnp.where(pick_ref[...].astype(F32) > 0.0, by_row, 0.0), axis=1, keepdims=True)
-
+    rank_copy.start()
+    position = iota((experts, MAIN, tokens), 1).astype(F32)
+    taken = jnp.broadcast_to(rank[:, None, :], position.shape) == position
+    scale = jnp.where(taken, jnp.broadcast_to(gate[:, None, :], position.shape), 0.0)
+    pick[:full] = jnp.where(taken, 1.0, 0.0).reshape(full, tokens).astype(BF16)
+    scale_of[:full] = jnp.sum(scale.reshape(full, tokens), axis=1, keepdims=True)
+    last = (MAIN + (iota((left, tokens), 0) & 1)).astype(F32)
+    taken = rows_by(rank, left) == last
+    pick[full:] = jnp.where(taken, 1.0, 0.0).astype(BF16)
+    scale_of[full:] = jnp.sum(jnp.where(taken, rows_by(gate, left), 0.0), axis=1, keepdims=True)
     for cut in range(CUTS):
         grad_copy(cut).wait()
-        grad = grads[cut]
-        stage[cut] = (plain_dot(main_pick[...], grad) * main_gate[...]).astype(BF16)
+        scaled = (plain_dot(pick[...], grads[cut]) * scale_of[...]).astype(BF16)
+        stage[cut] = scaled[:full]
         send_copy(cut).start()
-        pieces[cut] = (plain_dot(tail_pick[...], grad) * tail_gate[...]).astype(BF16)
+        pieces[cut] = scaled[full:]
     stage[CUTS] = plain_dot(piece_rows((full, full), 0, left), pieces[...].reshape(full, width)).astype(BF16)
     send_copy(CUTS).start()
     for cut in range(CUTS + 1):
         send_copy(cut).wait()
+    rank_copy.wait()
 
 
 def rows_by(values, rows):
@@ -115,22 +117,24 @@
     full, left = experts * MAIN, experts * 2
     return pl.pallas_call(
         functools.partial(dispatch_kernel, experts),
-        in_specs=[in_vmem(), in_vmem(), anywhere()],
-        out_specs=[anywhere(), in_vmem()],
+        in_specs=[anywhere()] * 3,
+        out_specs=[anywhere()] * 2,
         out_shape=[
             jax.ShapeDtypeStruct((full, model + width), BF16),
             jax.ShapeDtypeStruct((experts, tokens), F32),
         ],
         scratch_shapes=[
-            pltpu.VMEM((full, tokens), BF16),
-            pltpu.VMEM((left, tokens), BF16),
-            pltpu.VMEM((full, 1), F32),
-            pltpu.VMEM((left, 1), F32),
+            pltpu.VMEM((choices, tokens), jnp.int32),
+            pltpu.VMEM((choices, tokens), F32),
+            pltpu.VMEM((experts, tokens), F32),
+            pltpu.VMEM((full + left, tokens), BF16),
+            pltpu.VMEM((full + left, 1), F32),
             pltpu.VMEM((CUTS, tokens, width), BF16),
             pltpu.VMEM((CUTS + 1, full, width), BF16),
             pltpu.VMEM((CUTS, left, width), BF16),
             pltpu.SemaphoreType.DMA((CUTS,)),
             pltpu.SemaphoreType.DMA((CUTS + 1,)),
+            pltpu.SemaphoreType.DMA((3,)),
         ],
         compiler_params=pltpu.CompilerParams(vmem_limit_bytes=60 << 20),
         cost_estimate=pl.CostEstimate(
@@ -239,11 +243,12 @@
 
 
 def expert_kernel(experts, *refs):
-    where_ref, arrived, gate_hbm, up_hbm = refs[:4]
-    downs, gate_ups = refs[4 : 4 + CUTS], refs[4 + CUTS : 4 + 2 * CUTS]
-    grad_ref, back_ref = refs[4 + 2 * CUTS : 6 + 2 * CUTS]
-    rows, tail, pieces, down, gate_up, total, gate_factor, up_factor, grad, back_order, stage = refs[6 + 2 * CUTS : 17 + 2 * CUTS]
-    row_sem, down_sem, up_sem, factor_sem, out_sem = refs[17 + 2 * CUTS :]
+    places = shard_places()
+    arrived, gate_hbm, up_hbm = refs[:3]
+    downs, gate_ups = refs[3 : 3 + CUTS], refs[3 + CUTS : 3 + 2 * CUTS]
+    grad_ref, back_ref = refs[3 + 2 * CUTS : 5 + 2 * CUTS]
+    rows, tail, pieces, down, gate_up, total, gate_factor, up_factor, grad, back_order, stage = refs[5 + 2 * CUTS : 16 + 2 * CUTS]
+    row_sem, down_sem, up_sem, factor_sem, out_sem = refs[16 + 2 * CUTS :]
     full, left = experts * MAIN, experts * 2
     width = tail.shape[1]
     hidden = total.shape[1]
@@ -253,7 +258,7 @@
 
     def rows_copy(k):
         return pltpu.make_async_copy(
-            arrived.at[:, columns(where_ref[k], width)], rows.at[k // 2, pl.ds(0, full), half(k)], row_sem.at[k]
+            arrived.at[:, columns(places[k], width)], rows.at[k // 2, pl.ds(0, full), half(k)], row_sem.at[k]
         )
 
     def down_copy(k):
@@ -268,56 +273,63 @@
     tail_copy = pltpu.make_async_copy(arrived.at[:, columns(CUTS, width)], tail, row_sem.at[CUTS])
     gate_copy = pltpu.make_async_copy(gate_hbm, gate_factor, factor_sem.at[0])
     up_copy = pltpu.make_async_copy(up_hbm, up_factor, factor_sem.at[1])
-    tail_copy.start()
-    for k in range(CUTS):
-        rows_copy(k).start()
-        down_copy(k).start()
-    gate_copy.start()
-    up_copy.start()
+    groups = [(rows_copy(k), down_copy(k)) for k in range(CUTS)]
+    groups += [(gate_copy, up_copy)] + [(gate_up_copy(k),) for k in range(CUTS)]
+    groups[0] = (tail_copy,) + groups[0]
+
+    def start(group):
+        for copy in groups[group] if group < len(groups) else ():
+            copy.start()
+
+    def wait(group):
+        for copy in groups[group]:
+            if copy is not tail_copy:
+                copy.wait()
+        start(group + AHEAD)
+
+    for group in range(AHEAD):
+        start(group)
     order = piece_rows((full, full), 1, left)
     back_order[...] = piece_rows((full, full), 0, left)
     tail_copy.wait()
     pieces[...] = plain_dot(order, tail[...]).astype(BF16).reshape(CUTS, left, width)
     for pair in range(CUTS // 2):
         for k in (2 * pair, 2 * pair + 1):
-            rows_copy(k).wait()
-            down_copy(k).wait()
-            rows[pair, pl.ds(full, left), half(k)] = pieces[where_ref[k]]
-            if pair > 0:
-                gate_up_copy(k - 2).start()
+            wait(k)
+            rows[pair, pl.ds(full, left), half(k)] = pieces[places[k]]
+            if pair == 0:
+                product = rows_dot(rows[pair, :, half(k)], down[pair, :, half(k)])
+                total[...] = product if k == 0 else total[...] + product
+        if pair == 0:
+            continue
         product = rows_dot(rows[pair], down[pair])
-        if pair == 0:
-            total[...] = product
-        elif pair < CUTS // 2 - 1:
+        if pair < CUTS // 2 - 1:
             total[...] += product
         else:
-            gate_copy.wait()
-            up_copy.wait()
-            for k in (2 * pair, 2 * pair + 1):
-                gate_up_copy(k).start()
+            wait(CUTS)
             hidden_cot = total[...] + product
             grad[:, :hidden] = (hidden_cot * gate_factor[...]).astype(BF16)
             grad[:, hidden:] = (hidden_cot * up_factor[...]).astype(BF16)
     grad_copy = pltpu.make_async_copy(grad, grad_ref, factor_sem.at[2])
     grad_copy.start()
     for pair in range(CUTS // 2):
-        for k in (2 * pair, 2 * pair + 1):
-            gate_up_copy(k).wait()
+        wait(CUTS + 1 + 2 * pair)
+        wait(CUTS + 2 + 2 * pair)
         back = rows_dot(grad[...], gate_up[pair]).astype(BF16)
         for k in (2 * pair, 2 * pair + 1):
             own = back[:, (k % 2) * width : (k % 2 + 1) * width]
             stage[k] = own[:full]
-            out_copy(k, where_ref[k]).start()
-            pieces[where_ref[k]] = own[full:]
+            out_copy(k, places[k]).start()
+            pieces[places[k]] = own[full:]
     stage[CUTS] = plain_dot(back_order[...], pieces[...].reshape(full, width)).astype(BF16)
     out_copy(CUTS, CUTS).start()
     grad_copy.wait()
     for k in range(CUTS):
-        out_copy(k, where_ref[k]).wait()
+        out_copy(k, places[k]).wait()
     out_copy(CUTS, CUTS).wait()
 
 
-def expert_pass(where, arrived, gate_factor, up_factor, downs, gate_ups):
+def expert_pass(arrived, gate_factor, up_factor, downs, gate_ups):
     full, length = arrived.shape
     hidden, width = downs[0].shape
     slots = gate_factor.shape[0]
@@ -327,7 +339,7 @@
     left = experts * 2
     return pl.pallas_call(
         functools.partial(expert_kernel, experts),
-        in_specs=[pl.BlockSpec(memory_space=pltpu.SMEM)] + [anywhere()] * (3 + 2 * CUTS),
+        in_specs=[anywhere()] * (3 + 2 * CUTS),
         out_specs=[anywhere(), anywhere()],
         out_shape=[jax.ShapeDtypeStruct((slots, both), BF16), jax.ShapeDtypeStruct((full, length), BF16)],
         scratch_shapes=[
@@ -355,10 +367,10 @@
             transcendentals=0,
         ),
         name="experts",
-    )(where, arrived, gate_factor, up_factor, *downs, *gate_ups)
-
-
-def combine_kernel(place_ref, returned, out_ref, rows, tail, pieces, stage, row_sem, out_sem):
+    )(arrived, gate_factor, up_factor, *downs, *gate_ups)
+
+
+def combine_kernel(place_hbm, returned, out_ref, place_ref, rows, tail, pieces, stage, row_sem, out_sem):
     full, width = tail.shape
     left = pieces.shape[1]
 
@@ -371,12 +383,15 @@
         return pltpu.make_async_copy(stage.at[pair], out_ref.at[:, pl.ds(pair * 2 * width, 2 * width)], out_sem.at[pair])
 
     tail_copy = pltpu.make_async_copy(returned.at[:, pl.ds(CUTS * width, width)], tail, row_sem.at[CUTS // 2])
+    place_copy = pltpu.make_async_copy(place_hbm, place_ref, row_sem.at[CUTS // 2 + 1])
     tail_copy.start()
+    place_copy.start()
     for pair in range(CUTS // 2):
         rows_copy(pair).start()
     order = piece_rows((full, full), 1, left)
     tail_copy.wait()
     pieces[...] = plain_dot(order, tail[...]).astype(BF16).reshape(CUTS, left, width)
+    place_copy.wait()
     for pair in range(CUTS // 2):
         rows_copy(pair).wait()
         for cut in range(2):
@@ -397,15 +412,16 @@
     left = slots - full
     return pl.pallas_call(
         combine_kernel,
-        in_specs=[in_vmem(), anywhere()],
+        in_specs=[anywhere()] * 2,
         out_specs=anywhere(),
         out_shape=jax.ShapeDtypeStruct((tokens, model), BF16),
         scratch_shapes=[
+            pltpu.VMEM((tokens, slots), BF16),
             pltpu.VMEM((CUTS // 2, full, 2 * width), BF16),
             pltpu.VMEM((full, width), BF16),
             pltpu.VMEM((CUTS, left, width), BF16),
             pltpu.VMEM((CUTS // 2, tokens, 2 * width), BF16),
-            pltpu.SemaphoreType.DMA((CUTS // 2 + 1,)),
+            pltpu.SemaphoreType.DMA((CUTS // 2 + 2,)),
             pltpu.SemaphoreType.DMA((CUTS // 2,)),
         ],
         compiler_params=pltpu.CompilerParams(vmem_limit_bytes=60 << 20),
@@ -433,8 +449,8 @@
 def shard_places():
     count = lax.axis_size("dp")
     me = lax.axis_index("dp")
-    steps = jnp.array([0, -2, 2, 4], jnp.int32)
-    return jnp.concatenate([(me + steps + count) % count, ((me ^ 1) + steps + count) % count]).astype(jnp.int32)
+    other = me + 1 - 2 * lax.rem(me, 2)
+    return [lax.rem(core + step + count, count) for core in (me, other) for step in (0, -2, 2, 4)]
 
 
 def moved(rows, offset, sign):
@@ -461,7 +477,7 @@
     downs, gate_ups = gathered(down_weight[0]), gathered(gate_up_weight[0])
     spill_pre = moved(own_pre[home:], offset, -1)
     gate_factor, up_factor, place = travel_factors(rank, own_pre, spill_pre, experts)
-    travel_grad, back = expert_pass(shard_places(), arrived, gate_factor, up_factor, downs, gate_ups)
+    travel_grad, back = expert_pass(arrived, gate_factor, up_factor, downs, gate_ups)
     returned = exchange(back, experts)
     by_slot = to_slot_order(travel_grad, experts)
     spill_grad = moved(by_slot[home:], offset, 1)

time: 268 us -> 267 us (level)
    unnamed x30 -> x36, local copies, waits for them, and re-layouts: 4.57 us -> 6.67 us
  transfers between devices with their start and end apart: 22 -> 22, of which waited for: 10 -> 11; matrix products, arithmetic and copies ran while one was open for 3% -> 3% of each run, Pallas kernels for 2% -> 2%
where the time goes in v4:
time: 267 us
  waiting for transfers between devices  177 us (66%)
  starting transfers between devices  39.7 us (15%)
  Pallas kernels  34.4 us (13%)
  local copies, waits for them, and re-layouts  8.38 us (3%)
  other arithmetic  5.8 us (2%)
    all_to_all x2, waiting for transfers between devices, exchange(): lax.all_to_all(blocks, 'expert', split_axis=0, concat_axis=0, tiled=True)  82.7 us
    ppermute x6, waiting for transfers between devices, moved(): lax.ppermute(rows, 'dp', [(i, (i + by) % replicas) for i in range(replica...  62.1 us
    ppermute x14, waiting for transfers between devices, along_dp(): lax.ppermute(shard, 'dp', [(i, target(i)) for i in range(lax.axis_size('d...  31.9 us
    all_to_all x2, starting transfers between devices, exchange(): lax.all_to_all(blocks, 'expert', split_axis=0, concat_axis=0, tiled=True)  20.4 us
    pallas_call x1, Pallas kernels, expert_pass(): pl.pallas_call(functools.partial(expert_kernel, experts), in_specs=[anywh...  18.7 us
    ppermute x14, starting transfers between devices, along_dp(): lax.ppermute(shard, 'dp', [(i, target(i)) for i in range(lax.axis_size('d...  11.3 us
    ppermute x6, starting transfers between devices, moved(): lax.ppermute(rows, 'dp', [(i, (i + by) % replicas) for i in range(replica...  7.89 us
    unnamed x36, local copies, waits for them, and re-layouts  6.67 us
  transfers between devices with their start and end apart: 22, of which 11 were waited for; matrix products, arithmetic and copies ran while one was open for 3% of the time, Pallas kernels for 2%

profile of v4, /device:TPU:35, one launch (start us, length us, event | category | flops | bytes accessed | tf_op | source)
XLA Modules:
  0.0 266.7 jit_solution(11209288145629903214)
XLA Ops:
  0.6 5.4 %dispatch.1 = (bf16[512,4608]{1,0:T(8,128)(2,1)}, f32[32,192]{1,0:T(8,128)}) custom-call(s32[8,192]{1,0:T(8,128)} %bitcast.32, f32[8,192]{1,0:T(8,128)} %bitcast.33, bf16[192,4096]{1,0:T(8,128)(2,1)} %grad_ref.1), custom_call_target="tpu_custom_call" | custom-call | flops 805306368 | bytes 5767168 | tf_op jit(solution)/shard_map/dispatch/pallas_call | solution.py:118
  6.1 11.0 %all-to-all-start = ((bf16[32,16,4608]{2,1,0:T(8,128)(2,1)}), bf16[32,16,4608]{2,1,0:T(8,128)(2,1)}, u32[]{:S(2)}, u32[]{:S(2)}) async-start(bf16[32,16,4608]{2,1,0:T(8,128)(2,1)} %bitcast.21), calls=%async_computation | async-start | bytes 9437184 | tf_op jit(solution)/shard_map/all_to_all | solution.py:467
  17.1 1.3 collective-permute-start.10
  18.4 0.3 collective-permute-start.11
  18.6 1.2 collective-permute-start.3
  19.8 0.3 collective-permute-start.4
  20.1 0.7 slice_bitcast_fusion
  20.8 2.3 collective-permute-start
  23.2 29.0 %collective-permute-done.10.refs_12_ = bf16[512,1536]{1,0:T(8,128)(2,1)S(1)} collective-permute-done((bf16[512,1536]{1,0:T(8,128)(2,1)}, bf16[512,1536]{1,0:T(8,128)(2,1)S(1)}, u32[]{:S(2)}, u32[]{:S(2)}) %collective-permute-start.10) | collective-permute-done | bytes 1572896 | tf_op jit(solution)/shard_map/ppermute | solution.py:436
  52.2 0.9 collective-permute-done.11.refs_13_
  53.0 1.6 broadcast_select_fusion
  54.6 1.2 collective-permute-start.12
  55.8 3.2 %collective-permute-start.6 = (bf16[768,512]{1,0:T(8,128)(2,1)S(1)}, bf16[768,512]{1,0:T(8,128)(2,1)S(1)}, u32[]{:S(2)}, u32[]{:S(2)}) collective-permute-start(bf16[768,512]{1,0:T(8,128)(2,1)S(1)} %bitcast.31), channel_id=1, source_target_pairs={{0,32},{32,0},{64,96},{96,64},{128,160},{160,128},{192,224},{224,1... | collective-permute-start | bytes 2359304 | tf_op jit(solution)/shard_map/ppermute | solution.py:436
  59.6 20.7 %collective-permute-done = bf16[96,1536]{1,0:T(8,128)(2,1)} collective-permute-done((bf16[96,1536]{1,0:T(8,128)(2,1)}, bf16[96,1536]{1,0:T(8,128)(2,1)}, u32[]{:S(2)}, u32[]{:S(2)}) %collective-permute-start) | collective-permute-done | bytes 294944 | tf_op jit(solution)/shard_map/ppermute | solution.py:460
  80.3 1.0 broadcast_select_fusion.3
  81.3 0.3 collective-permute-start.1
  81.7 1.4 broadcast_select_fusion.1
  83.0 2.6 collective-permute-start.5
  85.7 15.8 %collective-permute-done.1 = bf16[96,1536]{1,0:T(8,128)(2,1)S(1)} collective-permute-done((bf16[96,1536]{1,0:T(8,128)(2,1)S(1)}, bf16[96,1536]{1,0:T(8,128)(2,1)S(1)}, u32[]{:S(2)}, u32[]{:S(2)}) %collective-permute-start.1) | collective-permute-done | bytes 294944 | tf_op jit(solution)/shard_map/ppermute | solution.py:460
  101.5 1.5 collective-permute-start.2
  103.0 10.6 %collective-permute-done.2 = bf16[96,1536]{1,0:T(8,128)(2,1)S(1)} collective-permute-done((bf16[96,1536]{1,0:T(8,128)(2,1)S(1)}, bf16[96,1536]{1,0:T(8,128)(2,1)S(1)}, u32[]{:S(2)}, u32[]{:S(2)}) %collective-permute-start.2) | collective-permute-done | bytes 294944 | tf_op jit(solution)/shard_map/ppermute | solution.py:460
  113.7 0.6 collective-permute-start.14
  114.3 0.3 collective-permute-start.15
  114.6 0.2 collective-permute-start.16
  114.8 1.4 collective-permute-done.8.refs_9_
  116.4 0.7 copy-done.16
  117.1 2.9 %factors.1 = (f32[576,768]{1,0:T(8,128)S(1)}, f32[576,768]{1,0:T(8,128)S(1)}, bf16[192,576]{1,0:T(8,128)(2,1)S(1)}) custom-call(f32[32,192]{1,0:T(8,128)S(1)} %copy-done.2, bf16[576,1536]{1,0:T(8,128)(2,1)S(1)} %bitcast.19, bf16[96,1536]{1,0:T(8,128)(2,1)S(1)} %broadcast_select_fusion.6.refs_1_.refs_3_, bf16[576,1536]{1,0:T(8,128)(2,1)S(1)} %bitcast.20, ...), custom_call_target="tpu_custom_call" | custom-call | flops 1019215872 | bytes 5308416 | tf_op jit(solution)/shard_map/factors/pallas_call | solution.py:197
  120.1 0.7 copy-done.1
  120.8 1.2 copy-done.3
  122.0 1.2 copy-done.4
  123.2 0.6 collective-permute-done.9.refs_10_
  123.8 0.5 copy-done.9
  124.4 0.4 copy-done.17
  124.7 0.8 copy-done.10
  125.5 1.2 copy-done.11
  126.7 18.7 %experts.1 = (bf16[576,1536]{1,0:T(8,128)(2,1)}, bf16[512,4608]{1,0:T(8,128)(2,1)}) custom-call(bf16[512,4608]{1,0:T(8,128)(2,1)} %bitcast.8.refs_0_, f32[576,768]{1,0:T(8,128)} %copy-done.3, f32[576,768]{1,0:T(8,128)} %copy-done.4, bf16[768,512]{1,0:T(8,128)(2,1)} %bitcast.30, bf16[768,512]{1,0:T(8,128)(2,1)} %collective-permute-done.3.refs_4_, ...), custom_call_target="tpu_custom_call" | custom-call | flops 10871635968 | bytes 31850496 | tf_op jit(solution)/shard_map/experts/pallas_call | solution.py:340
  145.4 9.4 %all-to-all-start.1 = ((bf16[32,16,4608]{2,1,0:T(8,128)(2,1)}), bf16[32,16,4608]{2,1,0:T(8,128)(2,1)}, u32[]{:S(2)}, u32[]{:S(2)}) async-start(bf16[32,16,4608]{2,1,0:T(8,128)(2,1)} %bitcast.22), calls=%async_computation.1 | async-start | bytes 9437184 | tf_op jit(solution)/shard_map/all_to_all | solution.py:467
  154.8 3.1 %to_slots.1 = bf16[576,1536]{1,0:T(8,128)(2,1)} custom-call(bf16[576,1536]{1,0:T(8,128)(2,1)S(1)} %copy-done.5), custom_call_target="tpu_custom_call" | custom-call | flops 1019215872 | bytes 3538944 | tf_op jit(solution)/shard_map/to_slots/pallas_call | solution.py:230
  158.0 1.0 slice.12
  159.0 3.7 %collective-permute-done.17 = bf16[96,1536]{1,0:T(8,128)(2,1)S(1)} collective-permute-done((bf16[96,1536]{1,0:T(8,128)(2,1)S(1)}, bf16[96,1536]{1,0:T(8,128)(2,1)S(1)}, u32[]{:S(2)}, u32[]{:S(2)}) %collective-permute-start.17) | collective-permute-done | bytes 294944 | tf_op jit(solution)/shard_map/ppermute | solution.py:460
  162.6 1.0 broadcast_select_fusion.2
  163.6 2.1 collective-permute-start.18
  165.7 5.4 %collective-permute-done.18 = bf16[96,1536]{1,0:T(8,128)(2,1)S(1)} collective-permute-done((bf16[96,1536]{1,0:T(8,128)(2,1)S(1)}, bf16[96,1536]{1,0:T(8,128)(2,1)S(1)}, u32[]{:S(2)}, u32[]{:S(2)}) %collective-permute-start.18) | collective-permute-done | bytes 294944 | tf_op jit(solution)/shard_map/ppermute | solution.py:460
  171.2 1.7 collective-permute-start.19
  172.9 6.0 %collective-permute-done.19 = bf16[96,1536]{1,0:T(8,128)(2,1)S(1)} collective-permute-done((bf16[96,1536]{1,0:T(8,128)(2,1)S(1)}, bf16[96,1536]{1,0:T(8,128)(2,1)S(1)}, u32[]{:S(2)}, u32[]{:S(2)}) %collective-permute-start.19) | collective-permute-done | bytes 294944 | tf_op jit(solution)/shard_map/ppermute | solution.py:460
  178.8 0.8 bitcast_dynamic-update-slice_fusion
  179.6 82.7 %all-to-all-done.1 = bf16[32,16,4608]{2,1,0:T(8,128)(2,1)} async-done(((bf16[32,16,4608]{2,1,0:T(8,128)(2,1)}), bf16[32,16,4608]{2,1,0:T(8,128)(2,1)}, u32[]{:S(2)}, u32[]{:S(2)}) %all-to-all-start.1) | async-done | bytes 4718624 | tf_op jit(solution)/shard_map/all_to_all | solution.py:467
  262.3 4.2 %combine.1 = bf16[192,4096]{1,0:T(8,128)(2,1)} custom-call(bf16[192,576]{1,0:T(8,128)(2,1)} %copy-done.1, bf16[512,4608]{1,0:T(8,128)(2,1)} %bitcast.12.returned), custom_call_target="tpu_custom_call" | custom-call | flops 905969664 | bytes 6291456 | tf_op jit(solution)/shard_map/combine/pallas_call | solution.py:413
  (47 shorter events, 0.4 us)
Async XLA Ops:
  6.1 14.0 %copy-start = (bf16[1,1,576,1536]{3,2,1,0:T(8,128)(2,1)S(1)}, bf16[1,1,576,1536]{3,2,1,0:T(8,128)(2,1)}, u32[]{:S(2)}) copy-start(bf16[1,1,576,1536]{3,2,1,0:T(8,128)(2,1)} %param.11) | copy-start | bytes 5308420
  6.1 120.6 %all-to-all-start = ((bf16[32,16,4608]{2,1,0:T(8,128)(2,1)}), bf16[32,16,4608]{2,1,0:T(8,128)(2,1)}, u32[]{:S(2)}, u32[]{:S(2)}) async-start(bf16[32,16,4608]{2,1,0:T(8,128)(2,1)} %bitcast.21), calls=%async_computation | async-start | bytes 9437184 | tf_op jit(solution)/shard_map/all_to_all | solution.py:467
  17.1 35.1 %collective-permute-start.10 = (bf16[512,1536]{1,0:T(8,128)(2,1)}, bf16[512,1536]{1,0:T(8,128)(2,1)S(1)}, u32[]{:S(2)}, u32[]{:S(2)}) collective-permute-start(bf16[512,1536]{1,0:T(8,128)(2,1)} %bitcast.24), channel_id=1, source_target_pairs={{0,64},{32,96},{64,128},{96,160},{128,192},{160,224},{192,0},{224,... | collective-permute-start | bytes 4718600 | tf_op jit(solution)/shard_map/ppermute | solution.py:436
  18.4 34.7 %collective-permute-start.11 = (bf16[512,1536]{1,0:T(8,128)(2,1)}, bf16[512,1536]{1,0:T(8,128)(2,1)}, u32[]{:S(2)}, u32[]{:S(2)}) collective-permute-start(bf16[512,1536]{1,0:T(8,128)(2,1)} %bitcast.25), channel_id=1, source_target_pairs={{0,192},{32,224},{64,0},{96,32},{128,64},{160,96},{192,128},{224,1... | collective-permute-start | bytes 4718600 | tf_op jit(solution)/shard_map/ppermute | solution.py:436
  18.6 63.0 %collective-permute-start.3 = (bf16[768,512]{1,0:T(8,128)(2,1)}, bf16[768,512]{1,0:T(8,128)(2,1)}, u32[]{:S(2)}, u32[]{:S(2)}) collective-permute-start(bf16[768,512]{1,0:T(8,128)(2,1)} %bitcast.28), channel_id=1, source_target_pairs={{0,64},{32,96},{64,128},{96,160},{128,192},{160,224},{192,0},{224,... | collective-permute-start | bytes 2359304 | tf_op jit(solution)/shard_map/ppermute | solution.py:436
  19.8 61.8 %collective-permute-start.4 = (bf16[768,512]{1,0:T(8,128)(2,1)}, bf16[768,512]{1,0:T(8,128)(2,1)}, u32[]{:S(2)}, u32[]{:S(2)}) collective-permute-start(bf16[768,512]{1,0:T(8,128)(2,1)} %bitcast.29), channel_id=1, source_target_pairs={{0,192},{32,224},{64,0},{96,32},{128,64},{160,96},{192,128},{224,1... | collective-permute-start | bytes 2359304 | tf_op jit(solution)/shard_map/ppermute | solution.py:436
  20.8 59.5 %collective-permute-start = (bf16[96,1536]{1,0:T(8,128)(2,1)}, bf16[96,1536]{1,0:T(8,128)(2,1)}, u32[]{:S(2)}, u32[]{:S(2)}) collective-permute-start(bf16[96,1536]{1,0:T(8,128)(2,1)} %slice_bitcast_fusion), channel_id=1, source_target_pairs={{0,224},{32,0},{64,32},{96,64},{128,96},{160,128},{192,160},{224,1... | collective-permute-start | bytes 884744 | tf_op jit(solution)/shard_map/ppermute | solution.py:460
  23.2 32.6 %copy-start.12 = (bf16[1,768,512]{2,1,0:T(8,128)(2,1)S(1)}, bf16[1,768,512]{2,1,0:T(8,128)(2,1)}, u32[]{:S(2)}) copy-start(bf16[1,768,512]{2,1,0:T(8,128)(2,1)} %param.12) | copy-start | bytes 2359300
  52.2 61.5 %copy-start.6 = (bf16[512,1536]{1,0:T(8,128)(2,1)}, bf16[512,1536]{1,0:T(8,128)(2,1)S(1)}, u32[]{:S(2)}) copy-start(bf16[512,1536]{1,0:T(8,128)(2,1)S(1)} %collective-permute-done.10.refs_12_) | copy-start | bytes 4718596
  54.6 60.0 %collective-permute-start.12 = (bf16[512,1536]{1,0:T(8,128)(2,1)S(1)}, bf16[512,1536]{1,0:T(8,128)(2,1)S(1)}, u32[]{:S(2)}, u32[]{:S(2)}) collective-permute-start(bf16[512,1536]{1,0:T(8,128)(2,1)S(1)} %broadcast_select_fusion), channel_id=1, source_target_pairs={{0,64},{32,224},{64,128},{96,32},{128,192},{160,96},{192,0},{224,1... | collective-permute-start | bytes 4718600 | tf_op jit(solution)/shard_map/ppermute | solution.py:436
  55.8 47.1 %collective-permute-start.6 = (bf16[768,512]{1,0:T(8,128)(2,1)S(1)}, bf16[768,512]{1,0:T(8,128)(2,1)S(1)}, u32[]{:S(2)}, u32[]{:S(2)}) collective-permute-start(bf16[768,512]{1,0:T(8,128)(2,1)S(1)} %bitcast.31), channel_id=1, source_target_pairs={{0,32},{32,0},{64,96},{96,64},{128,160},{160,128},{192,224},{224,1... | collective-permute-start | bytes 2359304 | tf_op jit(solution)/shard_map/ppermute | solution.py:436
  81.3 21.6 %copy-start.7 = (bf16[1,512,1536]{2,1,0:T(8,128)(2,1)S(1)}, bf16[1,512,1536]{2,1,0:T(8,128)(2,1)}, u32[]{:S(2)}) copy-start(bf16[1,512,1536]{2,1,0:T(8,128)(2,1)} %param.13) | copy-start | bytes 4718596
  81.3 35.8 %copy-start.2 = (f32[32,192]{1,0:T(8,128)S(1)}, f32[32,192]{1,0:T(8,128)}, u32[]{:S(2)}) copy-start(f32[32,192]{1,0:T(8,128)} %get-tuple-element.9.rank_ref) | copy-start | bytes 73732
  81.3 20.1 %collective-permute-start.1 = (bf16[96,1536]{1,0:T(8,128)(2,1)S(1)}, bf16[96,1536]{1,0:T(8,128)(2,1)S(1)}, u32[]{:S(2)}, u32[]{:S(2)}) collective-permute-start(bf16[96,1536]{1,0:T(8,128)(2,1)S(1)} %broadcast_select_fusion.3), channel_id=1, source_target_pairs={{0,192},{32,224},{64,0},{96,32},{128,64},{160,96},{192,128},{224,1... | collective-permute-start | bytes 884744 | tf_op jit(solution)/shard_map/ppermute | solution.py:460
  83.0 30.7 %collective-permute-start.5 = (bf16[768,512]{1,0:T(8,128)(2,1)S(1)}, bf16[768,512]{1,0:T(8,128)(2,1)S(1)}, u32[]{:S(2)}, u32[]{:S(2)}) collective-permute-start(bf16[768,512]{1,0:T(8,128)(2,1)S(1)} %broadcast_select_fusion.1), channel_id=1, source_target_pairs={{0,64},{32,224},{64,128},{96,32},{128,192},{160,96},{192,0},{224,1... | collective-permute-start | bytes 2359304 | tf_op jit(solution)/shard_map/ppermute | solution.py:436
  85.7 28.6 %collective-permute-start.7 = (bf16[768,512]{1,0:T(8,128)(2,1)}, bf16[768,512]{1,0:T(8,128)(2,1)S(1)}, u32[]{:S(2)}, u32[]{:S(2)}) collective-permute-start(bf16[768,512]{1,0:T(8,128)(2,1)} %collective-permute-done.3.refs_4_), channel_id=1, source_target_pairs={{0,32},{32,0},{64,96},{96,64},{128,160},{160,128},{192,224},{224,1... | collective-permute-start | bytes 2359304 | tf_op jit(solution)/shard_map/ppermute | solution.py:436
  101.5 12.2 %collective-permute-start.2 = (bf16[96,1536]{1,0:T(8,128)(2,1)S(1)}, bf16[96,1536]{1,0:T(8,128)(2,1)S(1)}, u32[]{:S(2)}, u32[]{:S(2)}) collective-permute-start(bf16[96,1536]{1,0:T(8,128)(2,1)S(1)} %broadcast_select_fusion.5), channel_id=1, source_target_pairs={{0,128},{32,160},{64,192},{96,224},{128,0},{160,32},{192,64},{224,... | collective-permute-start | bytes 884744 | tf_op jit(solution)/shard_map/ppermute | solution.py:460
  102.9 13.4 %copy-start.13 = (bf16[768,512]{1,0:T(8,128)(2,1)}, bf16[768,512]{1,0:T(8,128)(2,1)S(1)}, u32[]{:S(2)}) copy-start(bf16[768,512]{1,0:T(8,128)(2,1)S(1)} %collective-permute-done.6.refs_7_) | copy-start | bytes 2359300
  102.9 20.2 %collective-permute-start.13 = (bf16[512,1536]{1,0:T(8,128)(2,1)S(1)}, bf16[512,1536]{1,0:T(8,128)(2,1)S(1)}, u32[]{:S(2)}, u32[]{:S(2)}) collective-permute-start(bf16[512,1536]{1,0:T(8,128)(2,1)S(1)} %bitcast.27), channel_id=1, source_target_pairs={{0,32},{32,0},{64,96},{96,64},{128,160},{160,128},{192,224},{224,1... | collective-permute-start | bytes 4718600 | tf_op jit(solution)/shard_map/ppermute | solution.py:436
  113.7 2.5 collective-permute-start.8
  113.7 6.4 %copy-start.14 = (bf16[768,512]{1,0:T(8,128)(2,1)}, bf16[768,512]{1,0:T(8,128)(2,1)S(1)}, u32[]{:S(2)}) copy-start(bf16[768,512]{1,0:T(8,128)(2,1)S(1)} %collective-permute-done.5.refs_6_) | copy-start | bytes 2359300
  113.7 10.1 %collective-permute-start.14 = (bf16[512,1536]{1,0:T(8,128)(2,1)S(1)}, bf16[512,1536]{1,0:T(8,128)(2,1)S(1)}, u32[]{:S(2)}, u32[]{:S(2)}) collective-permute-start(bf16[512,1536]{1,0:T(8,128)(2,1)S(1)} %collective-permute-done.10.refs_12_), channel_id=1, source_target_pairs={{0,32},{32,0},{64,96},{96,64},{128,160},{160,128},{192,224},{224,1... | collective-permute-start | bytes 4718600 | tf_op jit(solution)/shard_map/ppermute | solution.py:436
  114.3 2.1 copy-start.15
  114.3 10.1 %collective-permute-start.15 = (bf16[512,1536]{1,0:T(8,128)(2,1)}, bf16[512,1536]{1,0:T(8,128)(2,1)S(1)}, u32[]{:S(2)}, u32[]{:S(2)}) collective-permute-start(bf16[512,1536]{1,0:T(8,128)(2,1)} %collective-permute-done.11.refs_13_), channel_id=1, source_target_pairs={{0,32},{32,0},{64,96},{96,64},{128,160},{160,128},{192,224},{224,1... | collective-permute-start | bytes 4718600 | tf_op jit(solution)/shard_map/ppermute | solution.py:436
  114.6 5.5 %copy-start.8 = (bf16[512,1536]{1,0:T(8,128)(2,1)}, bf16[512,1536]{1,0:T(8,128)(2,1)S(1)}, u32[]{:S(2)}) copy-start(bf16[512,1536]{1,0:T(8,128)(2,1)S(1)} %collective-permute-done.12.refs_14_) | copy-start | bytes 4718596
  114.6 12.1 %collective-permute-start.16 = (bf16[512,1536]{1,0:T(8,128)(2,1)S(1)}, bf16[512,1536]{1,0:T(8,128)(2,1)}, u32[]{:S(2)}, u32[]{:S(2)}) collective-permute-start(bf16[512,1536]{1,0:T(8,128)(2,1)S(1)} %collective-permute-done.12.refs_14_), channel_id=1, source_target_pairs={{0,32},{32,0},{64,96},{96,64},{128,160},{160,128},{192,224},{224,1... | collective-permute-start | bytes 4718600 | tf_op jit(solution)/shard_map/ppermute | solution.py:436
  116.2 0.9 copy-start.16
  116.2 7.6 %collective-permute-start.9 = (bf16[768,512]{1,0:T(8,128)(2,1)S(1)}, bf16[768,512]{1,0:T(8,128)(2,1)S(1)}, u32[]{:S(2)}, u32[]{:S(2)}) collective-permute-start(bf16[768,512]{1,0:T(8,128)(2,1)S(1)} %collective-permute-done.5.refs_6_), channel_id=1, source_target_pairs={{0,32},{32,0},{64,96},{96,64},{128,160},{160,128},{192,224},{224,1... | collective-permute-start | bytes 2359304 | tf_op jit(solution)/shard_map/ppermute | solution.py:436
  120.1 0.7 copy-start.1
  120.8 1.2 copy-start.3
  122.0 1.2 copy-start.4
  123.2 1.2 copy-start.9
  123.8 0.9 copy-start.17
  124.3 1.1 copy-start.10
  125.5 1.2 copy-start.11
  145.4 9.4 %copy-start.5 = (bf16[576,1536]{1,0:T(8,128)(2,1)S(1)}, bf16[576,1536]{1,0:T(8,128)(2,1)}, u32[]{:S(2)}) copy-start(bf16[576,1536]{1,0:T(8,128)(2,1)} %get-tuple-element.15.rows_ref) | copy-start | bytes 5308420
  145.4 116.9 %all-to-all-start.1 = ((bf16[32,16,4608]{2,1,0:T(8,128)(2,1)}), bf16[32,16,4608]{2,1,0:T(8,128)(2,1)}, u32[]{:S(2)}, u32[]{:S(2)}) async-start(bf16[32,16,4608]{2,1,0:T(8,128)(2,1)} %bitcast.22), calls=%async_computation.1 | async-start | bytes 9437184 | tf_op jit(solution)/shard_map/all_to_all | solution.py:467
  159.0 3.7 %collective-permute-start.17 = (bf16[96,1536]{1,0:T(8,128)(2,1)S(1)}, bf16[96,1536]{1,0:T(8,128)(2,1)S(1)}, u32[]{:S(2)}, u32[]{:S(2)}) collective-permute-start(bf16[96,1536]{1,0:T(8,128)(2,1)S(1)} %slice.12), channel_id=1, source_target_pairs={{0,32},{32,64},{64,96},{96,128},{128,160},{160,192},{192,224},{224... | collective-permute-start | bytes 884744 | tf_op jit(solution)/shard_map/ppermute | solution.py:460
  163.6 7.5 %collective-permute-start.18 = (bf16[96,1536]{1,0:T(8,128)(2,1)S(1)}, bf16[96,1536]{1,0:T(8,128)(2,1)S(1)}, u32[]{:S(2)}, u32[]{:S(2)}) collective-permute-start(bf16[96,1536]{1,0:T(8,128)(2,1)S(1)} %broadcast_select_fusion.2), channel_id=1, source_target_pairs={{0,64},{32,96},{64,128},{96,160},{128,192},{160,224},{192,0},{224,... | collective-permute-start | bytes 884744 | tf_op jit(solution)/shard_map/ppermute | solution.py:460
  171.2 7.6 %collective-permute-start.19 = (bf16[96,1536]{1,0:T(8,128)(2,1)S(1)}, bf16[96,1536]{1,0:T(8,128)(2,1)S(1)}, u32[]{:S(2)}, u32[]{:S(2)}) collective-permute-start(bf16[96,1536]{1,0:T(8,128)(2,1)S(1)} %broadcast_select_fusion.4), channel_id=1, source_target_pairs={{0,128},{32,160},{64,192},{96,224},{128,0},{160,32},{192,64},{224,... | collective-permute-start | bytes 884744 | tf_op jit(solution)/shard_map/ppermute | solution.py:460

commit v5 on v4

--- a/solution.py
+++ b/solution.py
@@ -55,10 +55,10 @@
 ):
     choices, tokens = ids_hbm.shape
     full, left = experts * MAIN, experts * 2
-    width = grads.shape[2]
+    width = grads.shape[2] // 2
 
     def grad_copy(cut):
-        return pltpu.make_async_copy(grad_ref.at[:, pl.ds(cut * width, width)], grads.at[cut], grad_sem.at[cut])
+        return pltpu.make_async_copy(grad_ref.at[:, pl.ds(cut * 2 * width, 2 * width)], grads.at[cut], grad_sem.at[cut])
 
     def send_copy(cut):
         return pltpu.make_async_copy(stage.at[cut], send_ref.at[:, pl.ds(cut * width, width)], sems.at[cut])
@@ -68,8 +68,8 @@
     rank_copy = pltpu.make_async_copy(rank_ref, rank_hbm, small_sem.at[2])
     ids_copy.start()
     gates_copy.start()
-    for cut in range(CUTS):
-        grad_copy(cut).start()
+    for pair in range(CUTS // 2):
+        grad_copy(pair).start()
     earlier = (iota((tokens, tokens), 0) < iota((tokens, tokens), 1)).astype(F32).astype(BF16)
     ids_copy.wait()
     gates_copy.wait()
@@ -92,12 +92,14 @@
     taken = rows_by(rank, left) == last
     pick[full:] = jnp.where(taken, 1.0, 0.0).astype(BF16)
     scale_of[full:] = jnp.sum(jnp.where(taken, rows_by(gate, left), 0.0), axis=1, keepdims=True)
-    for cut in range(CUTS):
-        grad_copy(cut).wait()
-        scaled = (plain_dot(pick[...], grads[cut]) * scale_of[...]).astype(BF16)
-        stage[cut] = scaled[:full]
-        send_copy(cut).start()
-        pieces[cut] = scaled[full:]
+    for pair in range(CUTS // 2):
+        grad_copy(pair).wait()
+        scaled = (plain_dot(pick[...], grads[pair]) * scale_of[...]).astype(BF16)
+        for cut in (2 * pair, 2 * pair + 1):
+            own = scaled[:, (cut % 2) * width : (cut % 2 + 1) * width]
+            stage[cut] = own[:full]
+            send_copy(cut).start()
+            pieces[cut] = own[full:]
     stage[CUTS] = plain_dot(piece_rows((full, full), 0, left), pieces[...].reshape(full, width)).astype(BF16)
     send_copy(CUTS).start()
     for cut in range(CUTS + 1):
@@ -129,7 +131,7 @@
             pltpu.VMEM((experts, tokens), F32),
             pltpu.VMEM((full + left, tokens), BF16),
             pltpu.VMEM((full + left, 1), F32),
-            pltpu.VMEM((CUTS, tokens, width), BF16),
+            pltpu.VMEM((CUTS // 2, tokens, 2 * width), BF16),
             pltpu.VMEM((CUTS + 1, full, width), BF16),
             pltpu.VMEM((CUTS, left, width), BF16),
             pltpu.SemaphoreType.DMA((CUTS,)),

time: 267 us -> 266 us (level)
  transfers between devices with their start and end apart: 22 -> 22, of which waited for: 11 -> 11; matrix products, arithmetic and copies ran while one was open for 3% -> 2% of each run, Pallas kernels for 2% -> 2%
where the time goes in v5:
time: 266 us
  waiting for transfers between devices  177 us (67%)
  starting transfers between devices  40.4 us (15%)
  Pallas kernels  33.6 us (13%)
  local copies, waits for them, and re-layouts  8.38 us (3%)
  other arithmetic  4.83 us (2%)
    all_to_all x2, waiting for transfers between devices, exchange(): lax.all_to_all(blocks, 'expert', split_axis=0, concat_axis=0, tiled=True)  82.8 us
    ppermute x6, waiting for transfers between devices, moved(): lax.ppermute(rows, 'dp', [(i, (i + by) % replicas) for i in range(replica...  62.3 us
    ppermute x14, waiting for transfers between devices, along_dp(): lax.ppermute(shard, 'dp', [(i, target(i)) for i in range(lax.axis_size('d...  31.9 us
    all_to_all x2, starting transfers between devices, exchange(): lax.all_to_all(blocks, 'expert', split_axis=0, concat_axis=0, tiled=True)  20.4 us
    pallas_call x1, Pallas kernels, expert_pass(): pl.pallas_call(functools.partial(expert_kernel, experts), in_specs=[anywh...  18.7 us
    ppermute x14, starting transfers between devices, along_dp(): lax.ppermute(shard, 'dp', [(i, target(i)) for i in range(lax.axis_size('d...  11.3 us
    ppermute x6, starting transfers between devices, moved(): lax.ppermute(rows, 'dp', [(i, (i + by) % replicas) for i in range(replica...  8.64 us
    unnamed x36, local copies, waits for them, and re-layouts  6.67 us
  transfers between devices with their start and end apart: 22, of which 11 were waited for; matrix products, arithmetic and copies ran while one was open for 2% of the time, Pallas kernels for 2%

profile of v5, /device:TPU:35, one launch (start us, length us, event | category | flops | bytes accessed | tf_op | source)
XLA Modules:
  0.0 265.9 jit_solution(13488994448126929978)
XLA Ops:
  0.6 4.6 %dispatch.1 = (bf16[512,4608]{1,0:T(8,128)(2,1)}, f32[32,192]{1,0:T(8,128)}) custom-call(s32[8,192]{1,0:T(8,128)} %bitcast.32, f32[8,192]{1,0:T(8,128)} %bitcast.33, bf16[192,4096]{1,0:T(8,128)(2,1)} %grad_ref.1), custom_call_target="tpu_custom_call" | custom-call | flops 805306368 | bytes 5767168 | tf_op jit(solution)/shard_map/dispatch/pallas_call | solution.py:120
  5.3 11.0 %all-to-all-start = ((bf16[32,16,4608]{2,1,0:T(8,128)(2,1)}), bf16[32,16,4608]{2,1,0:T(8,128)(2,1)}, u32[]{:S(2)}, u32[]{:S(2)}) async-start(bf16[32,16,4608]{2,1,0:T(8,128)(2,1)} %bitcast.21), calls=%async_computation | async-start | bytes 9437184 | tf_op jit(solution)/shard_map/all_to_all | solution.py:469
  16.3 1.3 collective-permute-start.10
  17.6 0.3 collective-permute-start.11
  17.8 1.2 collective-permute-start.3
  19.0 0.3 collective-permute-start.4
  19.3 0.7 slice_bitcast_fusion
  20.0 2.3 collective-permute-start
  22.4 28.9 %collective-permute-done.10.refs_12_ = bf16[512,1536]{1,0:T(8,128)(2,1)S(1)} collective-permute-done((bf16[512,1536]{1,0:T(8,128)(2,1)}, bf16[512,1536]{1,0:T(8,128)(2,1)S(1)}, u32[]{:S(2)}, u32[]{:S(2)}) %collective-permute-start.10) | collective-permute-done | bytes 1572896 | tf_op jit(solution)/shard_map/ppermute | solution.py:438
  51.3 0.9 collective-permute-done.11.refs_13_
  52.2 1.6 broadcast_select_fusion
  53.8 1.2 collective-permute-start.12
  55.0 3.2 %collective-permute-start.6 = (bf16[768,512]{1,0:T(8,128)(2,1)S(1)}, bf16[768,512]{1,0:T(8,128)(2,1)S(1)}, u32[]{:S(2)}, u32[]{:S(2)}) collective-permute-start(bf16[768,512]{1,0:T(8,128)(2,1)S(1)} %bitcast.31), channel_id=1, source_target_pairs={{0,32},{32,0},{64,96},{96,64},{128,160},{160,128},{192,224},{224,1... | collective-permute-start | bytes 2359304 | tf_op jit(solution)/shard_map/ppermute | solution.py:438
  58.8 20.7 %collective-permute-done = bf16[96,1536]{1,0:T(8,128)(2,1)} collective-permute-done((bf16[96,1536]{1,0:T(8,128)(2,1)}, bf16[96,1536]{1,0:T(8,128)(2,1)}, u32[]{:S(2)}, u32[]{:S(2)}) %collective-permute-start) | collective-permute-done | bytes 294944 | tf_op jit(solution)/shard_map/ppermute | solution.py:462
  79.6 0.3 collective-permute-start.1
  79.9 1.3 broadcast_select_fusion.1
  81.2 2.6 collective-permute-start.5
  83.9 16.8 %collective-permute-done.1 = bf16[96,1536]{1,0:T(8,128)(2,1)S(1)} collective-permute-done((bf16[96,1536]{1,0:T(8,128)(2,1)S(1)}, bf16[96,1536]{1,0:T(8,128)(2,1)S(1)}, u32[]{:S(2)}, u32[]{:S(2)}) %collective-permute-start.1) | collective-permute-done | bytes 294944 | tf_op jit(solution)/shard_map/ppermute | solution.py:462
  100.7 2.1 collective-permute-start.2
  102.9 10.0 %collective-permute-done.2 = bf16[96,1536]{1,0:T(8,128)(2,1)S(1)} collective-permute-done((bf16[96,1536]{1,0:T(8,128)(2,1)S(1)}, bf16[96,1536]{1,0:T(8,128)(2,1)S(1)}, u32[]{:S(2)}, u32[]{:S(2)}) %collective-permute-start.2) | collective-permute-done | bytes 294944 | tf_op jit(solution)/shard_map/ppermute | solution.py:462
  112.9 0.6 collective-permute-start.14
  113.5 0.3 collective-permute-start.15
  113.8 0.2 collective-permute-start.16
  114.0 1.4 collective-permute-done.8.refs_9_
  115.4 0.1 collective-permute-start.9
  115.6 0.7 copy-done.16
  116.3 2.9 %factors.1 = (f32[576,768]{1,0:T(8,128)S(1)}, f32[576,768]{1,0:T(8,128)S(1)}, bf16[192,576]{1,0:T(8,128)(2,1)S(1)}) custom-call(f32[32,192]{1,0:T(8,128)S(1)} %copy-done.2, bf16[576,1536]{1,0:T(8,128)(2,1)S(1)} %bitcast.19, bf16[96,1536]{1,0:T(8,128)(2,1)S(1)} %broadcast_select_fusion.6.refs_1_.refs_3_, bf16[576,1536]{1,0:T(8,128)(2,1)S(1)} %bitcast.20, ...), custom_call_target="tpu_custom_call" | custom-call | flops 1019215872 | bytes 5308416 | tf_op jit(solution)/shard_map/factors/pallas_call | solution.py:199
  119.3 0.7 copy-done.1
  120.0 1.2 copy-done.3
  121.2 1.2 copy-done.4
  122.4 0.6 collective-permute-done.9.refs_10_
  123.0 0.5 copy-done.9
  123.5 0.4 copy-done.17
  123.9 0.8 copy-done.10
  124.7 1.2 copy-done.11
  125.9 18.7 %experts.1 = (bf16[576,1536]{1,0:T(8,128)(2,1)}, bf16[512,4608]{1,0:T(8,128)(2,1)}) custom-call(bf16[512,4608]{1,0:T(8,128)(2,1)} %bitcast.8.refs_0_, f32[576,768]{1,0:T(8,128)} %copy-done.3, f32[576,768]{1,0:T(8,128)} %copy-done.4, bf16[768,512]{1,0:T(8,128)(2,1)} %bitcast.30, bf16[768,512]{1,0:T(8,128)(2,1)} %collective-permute-done.3.refs_4_, ...), custom_call_target="tpu_custom_call" | custom-call | flops 10871635968 | bytes 31850496 | tf_op jit(solution)/shard_map/experts/pallas_call | solution.py:342
  144.6 9.4 %all-to-all-start.1 = ((bf16[32,16,4608]{2,1,0:T(8,128)(2,1)}), bf16[32,16,4608]{2,1,0:T(8,128)(2,1)}, u32[]{:S(2)}, u32[]{:S(2)}) async-start(bf16[32,16,4608]{2,1,0:T(8,128)(2,1)} %bitcast.22), calls=%async_computation.1 | async-start | bytes 9437184 | tf_op jit(solution)/shard_map/all_to_all | solution.py:469
  154.0 3.1 %to_slots.1 = bf16[576,1536]{1,0:T(8,128)(2,1)} custom-call(bf16[576,1536]{1,0:T(8,128)(2,1)S(1)} %copy-done.5), custom_call_target="tpu_custom_call" | custom-call | flops 1019215872 | bytes 3538944 | tf_op jit(solution)/shard_map/to_slots/pallas_call | solution.py:232
  157.2 1.0 slice.12
  158.2 3.7 %collective-permute-done.17 = bf16[96,1536]{1,0:T(8,128)(2,1)S(1)} collective-permute-done((bf16[96,1536]{1,0:T(8,128)(2,1)S(1)}, bf16[96,1536]{1,0:T(8,128)(2,1)S(1)}, u32[]{:S(2)}, u32[]{:S(2)}) %collective-permute-start.17) | collective-permute-done | bytes 294944 | tf_op jit(solution)/shard_map/ppermute | solution.py:462
  161.8 1.0 broadcast_select_fusion.2
  162.8 2.1 collective-permute-start.18
  164.9 5.4 %collective-permute-done.18 = bf16[96,1536]{1,0:T(8,128)(2,1)S(1)} collective-permute-done((bf16[96,1536]{1,0:T(8,128)(2,1)S(1)}, bf16[96,1536]{1,0:T(8,128)(2,1)S(1)}, u32[]{:S(2)}, u32[]{:S(2)}) %collective-permute-start.18) | collective-permute-done | bytes 294944 | tf_op jit(solution)/shard_map/ppermute | solution.py:462
  170.3 1.7 collective-permute-start.19
  172.1 5.9 %collective-permute-done.19 = bf16[96,1536]{1,0:T(8,128)(2,1)S(1)} collective-permute-done((bf16[96,1536]{1,0:T(8,128)(2,1)S(1)}, bf16[96,1536]{1,0:T(8,128)(2,1)S(1)}, u32[]{:S(2)}, u32[]{:S(2)}) %collective-permute-start.19) | collective-permute-done | bytes 294944 | tf_op jit(solution)/shard_map/ppermute | solution.py:462
  177.9 0.8 bitcast_dynamic-update-slice_fusion
  178.7 82.8 %all-to-all-done.1 = bf16[32,16,4608]{2,1,0:T(8,128)(2,1)} async-done(((bf16[32,16,4608]{2,1,0:T(8,128)(2,1)}), bf16[32,16,4608]{2,1,0:T(8,128)(2,1)}, u32[]{:S(2)}, u32[]{:S(2)}) %all-to-all-start.1) | async-done | bytes 4718624 | tf_op jit(solution)/shard_map/all_to_all | solution.py:469
  261.5 4.2 %combine.1 = bf16[192,4096]{1,0:T(8,128)(2,1)} custom-call(bf16[192,576]{1,0:T(8,128)(2,1)} %copy-done.1, bf16[512,4608]{1,0:T(8,128)(2,1)} %bitcast.12.returned), custom_call_target="tpu_custom_call" | custom-call | flops 905969664 | bytes 6291456 | tf_op jit(solution)/shard_map/combine/pallas_call | solution.py:415
  (47 shorter events, 0.3 us)
Async XLA Ops:
  5.3 14.0 %copy-start = (bf16[1,1,576,1536]{3,2,1,0:T(8,128)(2,1)S(1)}, bf16[1,1,576,1536]{3,2,1,0:T(8,128)(2,1)}, u32[]{:S(2)}) copy-start(bf16[1,1,576,1536]{3,2,1,0:T(8,128)(2,1)} %param.11) | copy-start | bytes 5308420
  5.3 120.6 %all-to-all-start = ((bf16[32,16,4608]{2,1,0:T(8,128)(2,1)}), bf16[32,16,4608]{2,1,0:T(8,128)(2,1)}, u32[]{:S(2)}, u32[]{:S(2)}) async-start(bf16[32,16,4608]{2,1,0:T(8,128)(2,1)} %bitcast.21), calls=%async_computation | async-start | bytes 9437184 | tf_op jit(solution)/shard_map/all_to_all | solution.py:469
  16.3 35.0 %collective-permute-start.10 = (bf16[512,1536]{1,0:T(8,128)(2,1)}, bf16[512,1536]{1,0:T(8,128)(2,1)S(1)}, u32[]{:S(2)}, u32[]{:S(2)}) collective-permute-start(bf16[512,1536]{1,0:T(8,128)(2,1)} %bitcast.24), channel_id=1, source_target_pairs={{0,64},{32,96},{64,128},{96,160},{128,192},{160,224},{192,0},{224,... | collective-permute-start | bytes 4718600 | tf_op jit(solution)/shard_map/ppermute | solution.py:438
  17.6 34.7 %collective-permute-start.11 = (bf16[512,1536]{1,0:T(8,128)(2,1)}, bf16[512,1536]{1,0:T(8,128)(2,1)}, u32[]{:S(2)}, u32[]{:S(2)}) collective-permute-start(bf16[512,1536]{1,0:T(8,128)(2,1)} %bitcast.25), channel_id=1, source_target_pairs={{0,192},{32,224},{64,0},{96,32},{128,64},{160,96},{192,128},{224,1... | collective-permute-start | bytes 4718600 | tf_op jit(solution)/shard_map/ppermute | solution.py:438
  17.8 62.1 %collective-permute-start.3 = (bf16[768,512]{1,0:T(8,128)(2,1)}, bf16[768,512]{1,0:T(8,128)(2,1)}, u32[]{:S(2)}, u32[]{:S(2)}) collective-permute-start(bf16[768,512]{1,0:T(8,128)(2,1)} %bitcast.28), channel_id=1, source_target_pairs={{0,64},{32,96},{64,128},{96,160},{128,192},{160,224},{192,0},{224,... | collective-permute-start | bytes 2359304 | tf_op jit(solution)/shard_map/ppermute | solution.py:438
  19.0 60.9 %collective-permute-start.4 = (bf16[768,512]{1,0:T(8,128)(2,1)}, bf16[768,512]{1,0:T(8,128)(2,1)}, u32[]{:S(2)}, u32[]{:S(2)}) collective-permute-start(bf16[768,512]{1,0:T(8,128)(2,1)} %bitcast.29), channel_id=1, source_target_pairs={{0,192},{32,224},{64,0},{96,32},{128,64},{160,96},{192,128},{224,1... | collective-permute-start | bytes 2359304 | tf_op jit(solution)/shard_map/ppermute | solution.py:438
  20.0 59.5 %collective-permute-start = (bf16[96,1536]{1,0:T(8,128)(2,1)}, bf16[96,1536]{1,0:T(8,128)(2,1)}, u32[]{:S(2)}, u32[]{:S(2)}) collective-permute-start(bf16[96,1536]{1,0:T(8,128)(2,1)} %slice_bitcast_fusion), channel_id=1, source_target_pairs={{0,224},{32,0},{64,32},{96,64},{128,96},{160,128},{192,160},{224,1... | collective-permute-start | bytes 884744 | tf_op jit(solution)/shard_map/ppermute | solution.py:462
  22.4 32.6 %copy-start.12 = (bf16[1,768,512]{2,1,0:T(8,128)(2,1)S(1)}, bf16[1,768,512]{2,1,0:T(8,128)(2,1)}, u32[]{:S(2)}) copy-start(bf16[1,768,512]{2,1,0:T(8,128)(2,1)} %param.12) | copy-start | bytes 2359300
  51.3 61.6 %copy-start.6 = (bf16[512,1536]{1,0:T(8,128)(2,1)}, bf16[512,1536]{1,0:T(8,128)(2,1)S(1)}, u32[]{:S(2)}) copy-start(bf16[512,1536]{1,0:T(8,128)(2,1)S(1)} %collective-permute-done.10.refs_12_) | copy-start | bytes 4718596
  53.8 59.9 %collective-permute-start.12 = (bf16[512,1536]{1,0:T(8,128)(2,1)S(1)}, bf16[512,1536]{1,0:T(8,128)(2,1)S(1)}, u32[]{:S(2)}, u32[]{:S(2)}) collective-permute-start(bf16[512,1536]{1,0:T(8,128)(2,1)S(1)} %broadcast_select_fusion), channel_id=1, source_target_pairs={{0,64},{32,224},{64,128},{96,32},{128,192},{160,96},{192,0},{224,1... | collective-permute-start | bytes 4718600 | tf_op jit(solution)/shard_map/ppermute | solution.py:438
  55.0 47.8 %collective-permute-start.6 = (bf16[768,512]{1,0:T(8,128)(2,1)S(1)}, bf16[768,512]{1,0:T(8,128)(2,1)S(1)}, u32[]{:S(2)}, u32[]{:S(2)}) collective-permute-start(bf16[768,512]{1,0:T(8,128)(2,1)S(1)} %bitcast.31), channel_id=1, source_target_pairs={{0,32},{32,0},{64,96},{96,64},{128,160},{160,128},{192,224},{224,1... | collective-permute-start | bytes 2359304 | tf_op jit(solution)/shard_map/ppermute | solution.py:438
  79.5 23.3 %copy-start.7 = (bf16[1,512,1536]{2,1,0:T(8,128)(2,1)S(1)}, bf16[1,512,1536]{2,1,0:T(8,128)(2,1)}, u32[]{:S(2)}) copy-start(bf16[1,512,1536]{2,1,0:T(8,128)(2,1)} %param.13) | copy-start | bytes 4718596
  79.6 36.7 %copy-start.2 = (f32[32,192]{1,0:T(8,128)S(1)}, f32[32,192]{1,0:T(8,128)}, u32[]{:S(2)}) copy-start(f32[32,192]{1,0:T(8,128)} %get-tuple-element.9.rank_ref) | copy-start | bytes 73732
  79.6 21.1 %collective-permute-start.1 = (bf16[96,1536]{1,0:T(8,128)(2,1)S(1)}, bf16[96,1536]{1,0:T(8,128)(2,1)S(1)}, u32[]{:S(2)}, u32[]{:S(2)}) collective-permute-start(bf16[96,1536]{1,0:T(8,128)(2,1)S(1)} %broadcast_select_fusion.3), channel_id=1, source_target_pairs={{0,192},{32,224},{64,0},{96,32},{128,64},{160,96},{192,128},{224,1... | collective-permute-start | bytes 884744 | tf_op jit(solution)/shard_map/ppermute | solution.py:462
  81.2 31.6 %collective-permute-start.5 = (bf16[768,512]{1,0:T(8,128)(2,1)S(1)}, bf16[768,512]{1,0:T(8,128)(2,1)S(1)}, u32[]{:S(2)}, u32[]{:S(2)}) collective-permute-start(bf16[768,512]{1,0:T(8,128)(2,1)S(1)} %broadcast_select_fusion.1), channel_id=1, source_target_pairs={{0,64},{32,224},{64,128},{96,32},{128,192},{160,96},{192,0},{224,1... | collective-permute-start | bytes 2359304 | tf_op jit(solution)/shard_map/ppermute | solution.py:438
  83.9 29.6 %collective-permute-start.7 = (bf16[768,512]{1,0:T(8,128)(2,1)}, bf16[768,512]{1,0:T(8,128)(2,1)S(1)}, u32[]{:S(2)}, u32[]{:S(2)}) collective-permute-start(bf16[768,512]{1,0:T(8,128)(2,1)} %collective-permute-done.3.refs_4_), channel_id=1, source_target_pairs={{0,32},{32,0},{64,96},{96,64},{128,160},{160,128},{192,224},{224,1... | collective-permute-start | bytes 2359304 | tf_op jit(solution)/shard_map/ppermute | solution.py:438
  100.7 12.2 %collective-permute-start.2 = (bf16[96,1536]{1,0:T(8,128)(2,1)S(1)}, bf16[96,1536]{1,0:T(8,128)(2,1)S(1)}, u32[]{:S(2)}, u32[]{:S(2)}) collective-permute-start(bf16[96,1536]{1,0:T(8,128)(2,1)S(1)} %broadcast_select_fusion.5), channel_id=1, source_target_pairs={{0,128},{32,160},{64,192},{96,224},{128,0},{160,32},{192,64},{224,... | collective-permute-start | bytes 884744 | tf_op jit(solution)/shard_map/ppermute | solution.py:462
  102.8 12.8 %copy-start.13 = (bf16[768,512]{1,0:T(8,128)(2,1)}, bf16[768,512]{1,0:T(8,128)(2,1)S(1)}, u32[]{:S(2)}) copy-start(bf16[768,512]{1,0:T(8,128)(2,1)S(1)} %collective-permute-done.6.refs_7_) | copy-start | bytes 2359300
  102.8 19.6 %collective-permute-start.13 = (bf16[512,1536]{1,0:T(8,128)(2,1)S(1)}, bf16[512,1536]{1,0:T(8,128)(2,1)S(1)}, u32[]{:S(2)}, u32[]{:S(2)}) collective-permute-start(bf16[512,1536]{1,0:T(8,128)(2,1)S(1)} %bitcast.27), channel_id=1, source_target_pairs={{0,32},{32,0},{64,96},{96,64},{128,160},{160,128},{192,224},{224,1... | collective-permute-start | bytes 4718600 | tf_op jit(solution)/shard_map/ppermute | solution.py:438
  112.9 2.5 collective-permute-start.8
  112.9 6.4 %copy-start.14 = (bf16[768,512]{1,0:T(8,128)(2,1)}, bf16[768,512]{1,0:T(8,128)(2,1)S(1)}, u32[]{:S(2)}) copy-start(bf16[768,512]{1,0:T(8,128)(2,1)S(1)} %collective-permute-done.5.refs_6_) | copy-start | bytes 2359300
  112.9 10.1 %collective-permute-start.14 = (bf16[512,1536]{1,0:T(8,128)(2,1)S(1)}, bf16[512,1536]{1,0:T(8,128)(2,1)S(1)}, u32[]{:S(2)}, u32[]{:S(2)}) collective-permute-start(bf16[512,1536]{1,0:T(8,128)(2,1)S(1)} %collective-permute-done.10.refs_12_), channel_id=1, source_target_pairs={{0,32},{32,0},{64,96},{96,64},{128,160},{160,128},{192,224},{224,1... | collective-permute-start | bytes 4718600 | tf_op jit(solution)/shard_map/ppermute | solution.py:438
  113.5 2.1 copy-start.15
  113.5 10.1 %collective-permute-start.15 = (bf16[512,1536]{1,0:T(8,128)(2,1)}, bf16[512,1536]{1,0:T(8,128)(2,1)S(1)}, u32[]{:S(2)}, u32[]{:S(2)}) collective-permute-start(bf16[512,1536]{1,0:T(8,128)(2,1)} %collective-permute-done.11.refs_13_), channel_id=1, source_target_pairs={{0,32},{32,0},{64,96},{96,64},{128,160},{160,128},{192,224},{224,1... | collective-permute-start | bytes 4718600 | tf_op jit(solution)/shard_map/ppermute | solution.py:438
  113.8 5.5 %copy-start.8 = (bf16[512,1536]{1,0:T(8,128)(2,1)}, bf16[512,1536]{1,0:T(8,128)(2,1)S(1)}, u32[]{:S(2)}) copy-start(bf16[512,1536]{1,0:T(8,128)(2,1)S(1)} %collective-permute-done.12.refs_14_) | copy-start | bytes 4718596
  113.8 12.1 %collective-permute-start.16 = (bf16[512,1536]{1,0:T(8,128)(2,1)S(1)}, bf16[512,1536]{1,0:T(8,128)(2,1)}, u32[]{:S(2)}, u32[]{:S(2)}) collective-permute-start(bf16[512,1536]{1,0:T(8,128)(2,1)S(1)} %collective-permute-done.12.refs_14_), channel_id=1, source_target_pairs={{0,32},{32,0},{64,96},{96,64},{128,160},{160,128},{192,224},{224,1... | collective-permute-start | bytes 4718600 | tf_op jit(solution)/shard_map/ppermute | solution.py:438
  115.4 0.9 copy-start.16
  115.4 7.6 %collective-permute-start.9 = (bf16[768,512]{1,0:T(8,128)(2,1)S(1)}, bf16[768,512]{1,0:T(8,128)(2,1)S(1)}, u32[]{:S(2)}, u32[]{:S(2)}) collective-permute-start(bf16[768,512]{1,0:T(8,128)(2,1)S(1)} %collective-permute-done.5.refs_6_), channel_id=1, source_target_pairs={{0,32},{32,0},{64,96},{96,64},{128,160},{160,128},{192,224},{224,1... | collective-permute-start | bytes 2359304 | tf_op jit(solution)/shard_map/ppermute | solution.py:438
  119.3 0.7 copy-start.1
  120.0 1.2 copy-start.3
  121.2 1.2 copy-start.4
  122.4 1.2 copy-start.9
  123.0 0.9 copy-start.17
  123.5 1.1 copy-start.10
  124.7 1.2 copy-start.11
  144.6 9.4 %copy-start.5 = (bf16[576,1536]{1,0:T(8,128)(2,1)S(1)}, bf16[576,1536]{1,0:T(8,128)(2,1)}, u32[]{:S(2)}) copy-start(bf16[576,1536]{1,0:T(8,128)(2,1)} %get-tuple-element.15.rows_ref) | copy-start | bytes 5308420
  144.6 116.9 %all-to-all-start.1 = ((bf16[32,16,4608]{2,1,0:T(8,128)(2,1)}), bf16[32,16,4608]{2,1,0:T(8,128)(2,1)}, u32[]{:S(2)}, u32[]{:S(2)}) async-start(bf16[32,16,4608]{2,1,0:T(8,128)(2,1)} %bitcast.22), calls=%async_computation.1 | async-start | bytes 9437184 | tf_op jit(solution)/shard_map/all_to_all | solution.py:469
  158.1 3.7 %collective-permute-start.17 = (bf16[96,1536]{1,0:T(8,128)(2,1)S(1)}, bf16[96,1536]{1,0:T(8,128)(2,1)S(1)}, u32[]{:S(2)}, u32[]{:S(2)}) collective-permute-start(bf16[96,1536]{1,0:T(8,128)(2,1)S(1)} %slice.12), channel_id=1, source_target_pairs={{0,32},{32,64},{64,96},{96,128},{128,160},{160,192},{192,224},{224... | collective-permute-start | bytes 884744 | tf_op jit(solution)/shard_map/ppermute | solution.py:462
  162.8 7.5 %collective-permute-start.18 = (bf16[96,1536]{1,0:T(8,128)(2,1)S(1)}, bf16[96,1536]{1,0:T(8,128)(2,1)S(1)}, u32[]{:S(2)}, u32[]{:S(2)}) collective-permute-start(bf16[96,1536]{1,0:T(8,128)(2,1)S(1)} %broadcast_select_fusion.2), channel_id=1, source_target_pairs={{0,64},{32,96},{64,128},{96,160},{128,192},{160,224},{192,0},{224,... | collective-permute-start | bytes 884744 | tf_op jit(solution)/shard_map/ppermute | solution.py:462
  170.3 7.6 %collective-permute-start.19 = (bf16[96,1536]{1,0:T(8,128)(2,1)S(1)}, bf16[96,1536]{1,0:T(8,128)(2,1)S(1)}, u32[]{:S(2)}, u32[]{:S(2)}) collective-permute-start(bf16[96,1536]{1,0:T(8,128)(2,1)S(1)} %broadcast_select_fusion.4), channel_id=1, source_target_pairs={{0,128},{32,160},{64,192},{96,224},{128,0},{160,32},{192,64},{224,... | collective-permute-start | bytes 884744 | tf_op jit(solution)/shard_map/ppermute | solution.py:462
